TPU v7x, 32 devices: a whole 2x2x4 slice. The times are simulated.
32 devices in a mesh: tok: 8 (over z, x), head: 2 (over core), vid: 2 (over y).
Axes of the slice: x: 2, y: 2, z: 4, core: 2. Of those that a mesh axis runs over, the one named last changes fastest.
Arguments:
- queries: bfloat16 [2, 3, 1024, 2, 256], P('vid', None, 'tok', 'head'), may hold values from -6 to 6
- keys: bfloat16 [2, 3, 1024, 2, 256], P('vid', None, 'tok', 'head'), may hold values from -6 to 6
- values: bfloat16 [2, 3, 1024, 2, 256], P('vid', None, 'tok', 'head'), may hold values from -6 to 6
- out_grad: bfloat16 [2, 3, 1024, 2, 256], P('vid', None, 'tok', 'head'), may hold values from -6 to 6
- fast_init: bfloat16 [2, 3, 256, 256], P('head'), may hold values from -0.375 to 0.375
- updates: bfloat16 [2, 2, 2, 3, 256, 256], P('vid', None, 'head'), may hold values from -4 to 4
Outputs:
- query_grad: bfloat16 [2, 3, 1024, 2, 256], P('vid', None, 'tok', 'head')
- key_grad: bfloat16 [2, 3, 1024, 2, 256], P('vid', None, 'tok', 'head')
- value_grad: bfloat16 [2, 3, 1024, 2, 256], P('vid', None, 'tok', 'head')
- init_grad: float32 [2, 3, 256, 256], P('head')
All inputs are finite; a program needn't handle non-finite values.
Results may differ from a plain program's by a relative error of at most 0.0014.
Values sent between devices are 32-bit elements; how exact they have to be, the bound alone decides.
No kernel may reach another device: no remote copies, remote signals or barrier semaphores. Data moves between devices by JAX's collectives and lax.ppermute only.
A program may use at most 64 MiB of HBM per device.

v0:
```python
import jax
import jax.numpy as jnp
from jax import lax
from jax.sharding import PartitionSpec as P

EPS = 1e-06
HIGH = lax.Precision.HIGHEST


def matmul(left, right):
    return jnp.dot(left, right, precision=HIGH, preferred_element_type=jnp.float32)


def swiglu(rows, weights):
    gate = matmul(rows, weights[0])
    upper = matmul(rows, weights[1])
    return matmul(jax.nn.silu(gate) * upper, weights[2])


def update(weights, key_rows, value_rows, scale):
    gate = matmul(key_rows, weights[0])
    upper = matmul(key_rows, weights[1])
    active = jax.nn.silu(gate)
    sigma = jax.nn.sigmoid(gate)
    down_step = matmul((active * upper).T, value_rows)
    back = matmul(value_rows, weights[2].T)
    gate_step = matmul(key_rows.T, back * upper * sigma * (1.0 + gate * (1.0 - sigma)))
    up_step = matmul(key_rows.T, back * active)
    return jnp.stack([gate_step, up_step, down_step]) * scale


def colnorm(weights, raised):
    old = jnp.sqrt(jnp.sum(weights * weights, axis=-2) + EPS)
    new = jnp.sqrt(jnp.sum(raised * raised, axis=-2) + EPS)
    return raised * (old / new)[..., None, :]


def group_back(weights, query, key_rows, value_rows, cot, upper_adj, scale):

    def group_local(wt, qq, kk, vv, cc, adj):

        def forward(first, second, third, fourth):
            return (swiglu(second, first), update(first, third, fourth, scale))

        _, back = jax.vjp(forward, wt, qq, kk, vv)
        return back((cc, adj))

    inner = jax.vmap(group_local, in_axes=(0, 1, 1, 1, 1, 0), out_axes=(0, 1, 1, 1))
    return jax.vmap(inner)(weights, query, key_rows, value_rows, cot, upper_adj)


def apply_back(weights, query, cot):

    def apply_local(wt, qq, cc):
        _, back = jax.vjp(swiglu, qq, wt)
        return back(cc)

    inner = jax.vmap(apply_local, in_axes=(0, 1, 1), out_axes=(1, 0))
    return jax.vmap(inner)(weights, query, cot)


def local_terms(index, groups, weights, queries, keys, values, out_grad, upper_adj, scale):
    query = queries[:, index].astype(jnp.float32)
    cot = out_grad[:, index].astype(jnp.float32)
    if index + 1 < groups:
        key_rows = keys[:, index].astype(jnp.float32)
        value_rows = values[:, index].astype(jnp.float32)
        wpart, dq, dk, dv = group_back(
            weights[index], query, key_rows, value_rows, cot, upper_adj, scale
        )
    else:
        dq, wpart = apply_back(weights[index], query, cot)
        dk = jnp.zeros(query.shape, jnp.float32)
        dv = jnp.zeros(query.shape, jnp.float32)
    return (wpart, dq, dk, dv)


def on_device(queries, keys, values, out_grad, fast_init, updates):
    tok_count = lax.axis_size("tok")
    scale = float(queries.shape[2] * tok_count) ** (-0.5)
    vids = queries.shape[0]
    groups = queries.shape[1]
    init = fast_init.astype(jnp.float32)
    steps = updates.astype(jnp.float32)
    weights = [init[None]]
    for index in range(groups - 1):
        weights.append(colnorm(weights[index], weights[index] + steps[:, index]))
    zero_adj = jnp.zeros(weights[0].shape, jnp.float32)
    grads_q, grads_k, grads_v = ([], [], [])
    adjoint = zero_adj
    init_grad = None
    for index in reversed(range(groups)):
        current = weights[index]
        if index + 1 < groups:
            _, norm_back = jax.vjp(colnorm, current, current + steps[:, index])
            direct, upper_adj = norm_back(adjoint)
        else:
            direct, upper_adj = (zero_adj, zero_adj)
        wpart, dq, dk, dv = local_terms(
            index, groups, weights, queries, keys, values, out_grad, upper_adj, scale
        )
        if index > 0:
            adjoint = direct + upper_adj + lax.psum(wpart, "tok")
        else:
            carried = jnp.sum(wpart + (direct + upper_adj) / tok_count, axis=0)
            init_grad = lax.psum(carried, ("tok", "vid"))
        grads_q.append(dq)
        grads_k.append(dk)
        grads_v.append(dv)

    def stacked(items):
        return jnp.stack(items[::-1], axis=1).astype(jnp.bfloat16)

    return (stacked(grads_q), stacked(grads_k), stacked(grads_v), init_grad)


def solution(mesh):
    return jax.shard_map(
        on_device,
        mesh=mesh,
        in_specs=(
            P("vid", None, "tok", "head", None),
            P("vid", None, "tok", "head", None),
            P("vid", None, "tok", "head", None),
            P("vid", None, "tok", "head", None),
            P("head", None, None, None),
            P("vid", None, "head", None, None, None),
        ),
        out_specs=(
            P("vid", None, "tok", "head", None),
            P("vid", None, "tok", "head", None),
            P("vid", None, "tok", "head", None),
            P("head", None, None, None),
        ),
        check_vma=False,
    )
```

profile of v0, /device:TPU:1, one launch (start us, length us, event | category | flops | bytes accessed | tf_op | source)
XLA Modules:
  0.0 294.8 jit_solution(4153284058002502673)
XLA Ops:
  7.2 1.3 convert_element_type.44
  12.2 0.9 pad_add_fusion.1
  13.2 1.0 fusion.97
  14.3 1.0 fusion.95
  15.3 1.0 fusion.99
  16.3 1.7 fusion.96
  18.0 1.7 fusion.98
  19.9 1.0 convolution_bitcast_fusion
  21.0 1.0 convolution_bitcast_fusion.2
  22.0 1.0 convolution_bitcast_fusion.1
  24.3 1.0 convolution_bitcast_fusion.6
  25.3 1.0 convolution_bitcast_fusion.8
  26.4 1.0 convolution_bitcast_fusion.7
  27.8 0.9 fusion.94
  31.2 0.9 fusion.36
  32.1 0.9 fusion.37
  33.0 0.9 fusion.35
  33.9 55.2 %all-reduce.19.cloned.1.call-done = f32[1,1,3,256,256]{4,3,2,1,0:T(8,128)} async-done(((f32[1,1,3,256,256]{4,3,2,1,0:T(8,128)}), f32[1,1,3,256,256]{4,3,2,1,0:T(8,128)}) %all-reduce.19.cloned.1.call-update) | async-done | bytes 786448 | tf_op jit(solution)/shard_map/psum | solution.py:103
  89.1 1.3 multiply_reduce_fusion.1
  90.4 1.3 multiply_multiply_fusion.1
  92.7 1.3 convolution_bitcast_fusion.15
  95.4 1.0 pad_add_fusion
  96.7 1.3 convolution_bitcast_fusion.18
  98.0 2.2 fusion.21
  100.2 1.4 fusion.33
  101.7 1.4 fusion
  103.1 1.0 fusion.15
  104.1 66.3 %all-reduce.21.cloned.1.call-done = f32[1,1,3,256,256]{4,3,2,1,0:T(8,128)} async-done(((f32[1,1,3,256,256]{4,3,2,1,0:T(8,128)}), f32[1,1,3,256,256]{4,3,2,1,0:T(8,128)}) %all-reduce.21.cloned.1.call-update) | async-done | bytes 786448 | tf_op jit(solution)/shard_map/psum | solution.py:103
  170.4 1.8 multiply_reduce_fusion
  176.2 1.1 fusion.28
  180.7 105.5 %all-reduce.23.cloned.1.call-done = f32[1,3,256,256]{3,2,1,0:T(8,128)} async-done(((f32[1,3,256,256]{3,2,1,0:T(8,128)}), f32[1,3,256,256]{3,2,1,0:T(8,128)}) %all-reduce.23.cloned.1.call-update) | async-done | bytes 786448 | tf_op jit(solution)/shard_map/psum | solution.py:106
  286.2 2.1 copy.77
  (157 shorter events, 17.4 us)
Async XLA Ops:
  7.2 81.9 %all-reduce.19.cloned.1.call-start = ((), (), s32[]{:S(2)}) async-start(), calls=%async_computation | async-start | bytes 1572864 | tf_op jit(solution)/shard_map/psum | solution.py:103
  9.3 2.1 copy-start.49
  10.2 1.9 copy-start.3
  10.5 1.6 copy-start.40
  13.1 157.3 %all-reduce.21.cloned.1.call-start = ((), (), s32[]{:S(2)}) async-start(), calls=%async_computation.1 | async-start | bytes 1572864 | tf_op jit(solution)/shard_map/psum | solution.py:103
  13.2 6.8 %copy-start.11 = (bf16[1,3,128,1,256]{4,2,3,1,0:T(8,128)(2,1)S(1)}, bf16[1,3,128,1,256]{4,2,3,1,0:T(8,128)(2,1)}, u32[]{:S(2)}) copy-start(bf16[1,3,128,1,256]{4,2,3,1,0:T(8,128)(2,1)} %param.6) | copy-start | bytes 589828
  13.2 7.8 %copy-start.39 = (bf16[1,3,128,1,256]{4,2,3,1,0:T(8,128)(2,1)S(1)}, bf16[1,3,128,1,256]{4,2,3,1,0:T(8,128)(2,1)}, u32[]{:S(2)}) copy-start(bf16[1,3,128,1,256]{4,2,3,1,0:T(8,128)(2,1)} %param.9) | copy-start | bytes 589828
  23.6 3.8 %copy-start.4 = (f32[1,1,3,256,256]{4,3,2,1,0:T(8,128)S(1)}, f32[1,1,3,256,256]{4,3,2,1,0:T(8,128)}, u32[]{:S(2)}) copy-start(f32[1,1,3,256,256]{4,3,2,1,0:T(8,128)} %copy-done.3) | copy-start | bytes 2359300
  23.6 3.8 %copy-start.41 = (f32[128,256]{1,0:T(8,128)S(1)}, f32[128,256]{1,0:T(8,128)}, u32[]{:S(2)}) copy-start(f32[128,256]{1,0:T(8,128)} %copy-done.40) | copy-start | bytes 393220
  23.6 3.8 %copy-start.45 = (f32[128,256]{1,0:T(8,128)S(1)}, f32[128,256]{1,0:T(8,128)}, u32[]{:S(2)}) copy-start(f32[128,256]{1,0:T(8,128)} %copy-done.44) | copy-start | bytes 393220
  23.9 3.9 %copy-start.12 = (bf16[1,3,128,1,256]{4,2,3,1,0:T(8,128)(2,1)S(1)}, bf16[1,3,128,1,256]{4,2,3,1,0:T(8,128)(2,1)}, u32[]{:S(2)}) copy-start(bf16[1,3,128,1,256]{4,2,3,1,0:T(8,128)(2,1)} %param.8) | copy-start | bytes 589828
  26.4 3.0 %copy-start.43 = (f32[128,256]{1,0:T(8,128)S(1)}, f32[128,256]{1,0:T(8,128)}, u32[]{:S(2)}) copy-start(f32[128,256]{1,0:T(8,128)} %copy-done.42) | copy-start | bytes 393220
  28.7 2.5 copy-start.7
  89.1 2.7 copy-start.1
  90.4 1.8 copy-start.8
  91.8 2.2 copy-start.19
  91.9 2.4 copy-start.5
  96.4 189.8 %all-reduce.23.cloned.1.call-start = ((), (), s32[]{:S(2)}) async-start(), calls=%async_computation.2 | async-start | bytes 1572864 | tf_op jit(solution)/shard_map/psum | solution.py:106
  96.6 5.0 %copy-start.16 = (f32[256,128]{0,1:T(8,128)S(1)}, f32[256,128]{0,1:T(8,128)}, u32[]{:S(2)}) copy-start(f32[256,128]{0,1:T(8,128)} %fusion.36) | copy-start | bytes 393220
  96.6 5.0 %copy-start.18 = (f32[256,128]{0,1:T(8,128)S(1)}, f32[256,128]{0,1:T(8,128)}, u32[]{:S(2)}) copy-start(f32[256,128]{0,1:T(8,128)} %fusion.37) | copy-start | bytes 393220
  96.6 5.0 %copy-start.20 = (f32[256,128]{0,1:T(8,128)S(1)}, f32[256,128]{0,1:T(8,128)}, u32[]{:S(2)}) copy-start(f32[256,128]{0,1:T(8,128)} %fusion.35) | copy-start | bytes 393220
  96.7 6.4 %copy-start.27 = (f32[128,256]{1,0:T(8,128)S(1)}, f32[128,256]{1,0:T(8,128)}, u32[]{:S(2)}) copy-start(f32[128,256]{1,0:T(8,128)} %copy-done.26) | copy-start | bytes 393220
  170.4 1.9 copy-start.47
  170.4 1.9 copy-start.2
  170.4 1.9 copy-start.6
  170.4 1.9 copy-start.50
  174.5 1.7 copy-start.35
  174.5 1.7 copy-start.36
  174.5 1.7 copy-start.37
  177.3 1.6 copy-start.33
  177.3 1.6 copy-start.34
  177.3 1.6 copy-start.51
  (23 other events, 26.1 us)
Sparse Core Ops, SparseCore 0:
  13.2 75.8 all-reduce.18
  96.5 73.8 all-reduce.20
  177.5 108.7 all-reduce.22
where the time goes:
time: 298 us; the launch traced here: 295 us
  waiting for transfers between devices  227 us (76%)
  matrix products  35.5 us (12%)
  between operations  14.7 us (5%)
  other arithmetic  10.9 us (4%)
  local copies, waits for them, and re-layouts  6.44 us (2%)
    psum x2, waiting for transfers between devices, on_device(): adjoint = direct + upper_adj + lax.psum(wpart, 'tok')  121 us
    psum x1, waiting for transfers between devices, on_device(): init_grad = lax.psum(carried, ('tok', 'vid'))  106 us
    dot_general x54, matrix products, matmul(): jnp.dot(left, right, precision=HIGH, preferred_element_type=jnp.float32)  35.5 us
  transfers between devices with their start and end apart: 3, of which 3 were waited for; matrix products, arithmetic and copies ran while one was open for 11% of the time, Pallas kernels for 0%

commit v1 on v0

v1 whole, which is shorter than its diff:
```python
import functools

import jax
import jax.numpy as jnp
from jax import lax
from jax.experimental import pallas as pl
from jax.experimental.pallas import tpu as pltpu
from jax.sharding import PartitionSpec as P

EPS = 1e-06
F32 = jnp.float32
BF16 = jnp.bfloat16
NN = (((1,), (0,)), ((), ()))
NT = (((1,), (1,)), ((), ()))
TN = (((0,), (0,)), ((), ()))
PAD = 8


def dot(left, right, dims):
    return lax.dot_general(left, right, dims, preferred_element_type=F32)


def split(array):
    high = array.astype(BF16)
    return high, (array - high.astype(F32)).astype(BF16)


def exact_left(left, right, dims):
    return dot(left, right[0], dims) + dot(left, right[1], dims)


def exact_right(left, right, dims):
    return dot(left[0], right, dims) + dot(left[1], right, dims)


def both_split(left, right, dims):
    return (
        dot(left[0], right[0], dims)
        + (dot(left[0], right[1], dims) + dot(left[1], right[0], dims))
    )


def silu_parts(gate):
    sigma = jax.nn.sigmoid(gate)
    rest = 1.0 - sigma
    silu = gate * sigma
    first = sigma * (1.0 + gate * rest)
    second = sigma * rest * (2.0 + gate * (1.0 - 2.0 * sigma))
    return silu, first, second


def rows_of_half(gate, up, down, which):
    dim = gate.shape[0]
    half = dim // 2
    cut = slice(which * half, (which + 1) * half)
    return [
        (0, gate[:, cut]),
        (dim, up[:, cut]),
        (2 * dim, down[cut, :half]),
        (2 * dim + half, down[cut, half:]),
    ]


def load_half(rows, dim):
    half = dim // 2
    gate_up = jnp.concatenate([rows[:dim], rows[dim : 2 * dim]], axis=1)
    down = jnp.concatenate([rows[2 * dim : 2 * dim + half], rows[2 * dim + half :]], axis=1)
    return gate_up, down


def store_parts(refs, row, value):
    size = refs[-1].shape[0]
    start = 0
    while start < value.shape[0]:
        part, inside = divmod(row + start, size)
        count = min(value.shape[0] - start, size - inside)
        refs[part][inside : inside + count, :] = value[start : start + count, :]
        start += count


def prep_kernel(init_ref, upd_ref, full_ref, mine_ref, send_ref):
    groups = upd_ref.shape[0] + 1
    dim = init_ref.shape[-1]
    half = dim // 2
    core = lax.axis_index("head") % 2
    weights = [init_ref[index].astype(F32) for index in range(3)]
    vectors = []
    levels = []
    for level in range(groups):
        levels.append(weights)
        if level + 1 == groups:
            break
        raised, ratio, cross, inverse = [], [], [], []
        for index in range(3):
            up = weights[index] + upd_ref[level, index].astype(F32)
            old2 = jnp.sum(weights[index] * weights[index], axis=0, keepdims=True) + EPS
            new2 = jnp.sum(up * up, axis=0, keepdims=True) + EPS
            old, new = jnp.sqrt(old2), jnp.sqrt(new2)
            ratio.append(old / new)
            cross.append(1.0 / (old * new))
            inverse.append(1.0 / old2)
            raised.append(up * ratio[index])
        vectors.append((ratio, cross, inverse))
        weights = raised
        for index in range(3):
            full_ref[level, index] = weights[index]

    def write(ref, which):
        cut = slice(which * half, (which + 1) * half)
        for level in range(groups):
            for row, value in rows_of_half(*levels[level], which):
                base = level * 3 * dim + row
                ref[base : base + value.shape[0], :] = value
        base = groups * 3 * dim
        for kinds in vectors:
            for gate, up, down in kinds:
                for value in (gate[:, cut], up[:, cut], down[:, :half], down[:, half:]):
                    ref[base : base + 1, :] = value
                    base += 1

    @pl.when(core == 0)
    def _():
        write(mine_ref, 0)
        write(send_ref, 1)

    @pl.when(core != 0)
    def _():
        write(mine_ref, 1)
        write(send_ref, 0)


def query_kernel(q_ref, c_ref, init_ref, full_ref, out_ref):
    groups = q_ref.shape[0]
    for index in range(groups):
        query, cot = q_ref[index], c_ref[index]
        if index == 0:
            pieces = [(init_ref[part], None) for part in range(3)]
        else:
            pieces = [split(full_ref[index - 1, part]) for part in range(3)]

        def apply(left, right, dims):
            return dot(left, right[0], dims) if right[1] is None else exact_left(left, right, dims)

        gate = apply(query, pieces[0], NN)
        up = apply(query, pieces[1], NN)
        back = apply(cot, pieces[2], NT)
        silu, first, _ = silu_parts(gate)
        total = None
        for value, piece in ((back * up * first, pieces[0]), (back * silu, pieces[1])):
            value = split(value)
            term = exact_right(value, piece[0], NT) if piece[1] is None else both_split(value, piece, NT)
            total = term if total is None else total + term
        out_ref[index] = total.astype(out_ref.dtype)


def stack_tokens(mine_ref, sib_ref, index):
    return jnp.concatenate([mine_ref[index], sib_ref[index]], axis=0).astype(BF16)


def apply_terms(query, cot, rows, dim):
    half = dim // 2
    gate_up, down = load_half(rows, dim)
    raw = exact_left(query, split(gate_up), NN)
    back = exact_left(cot, split(down), NT)
    gate, up = raw[:, :half], raw[:, half:]
    silu, first, _ = silu_parts(gate)
    grads = jnp.concatenate([back * up * first, back * silu], axis=1)
    d_gate_up = exact_left(query, split(grads), TN)
    d_down = exact_right(split(silu * up), cot, TN)
    return d_gate_up, d_down


def last_kernel(mine_ref, sib_ref, w_ref, *out_refs):
    parts, sums_ref = out_refs[:-1], out_refs[-1]
    dim = mine_ref.shape[-1]
    half = dim // 2
    query, cot = (stack_tokens(mine_ref, sib_ref, index) for index in range(2))
    d_gate_up, d_down = apply_terms(query, cot, w_ref[...], dim)
    store_parts(parts, 0, d_gate_up[:, :half])
    store_parts(parts, dim, d_gate_up[:, half:])
    sums_ref[...] = jnp.zeros_like(sums_ref)
    for block in range(2):
        value = d_down[:, block * half : (block + 1) * half]
        row = 2 * dim + block * half
        store_parts(parts, row, value)
        sums_ref[block : block + 1, :] = jnp.sum(
            value * w_ref[row : row + half, :], axis=0, keepdims=True
        )


def pre_kernel(mine_ref, sib_ref, w_ref, grad_ref, coef_ref):
    dim = mine_ref.shape[-1]
    half = dim // 2
    query, cot, key, value = (stack_tokens(mine_ref, sib_ref, index) for index in range(4))
    rows = w_ref[...]
    d_gate_up, d_down = apply_terms(query, cot, rows, dim)
    grad_ref[:dim, :] = d_gate_up[:, :half]
    grad_ref[dim : 2 * dim, :] = d_gate_up[:, half:]
    grad_ref[2 * dim : 2 * dim + half, :] = d_down[:, :half]
    grad_ref[2 * dim + half :, :] = d_down[:, half:]
    gate_up, down = load_half(rows, dim)
    raw = exact_left(key, split(gate_up), NN)
    back = exact_left(value, split(down), NT)
    gate, up = raw[:, :half], raw[:, half:]
    silu, first, second = silu_parts(gate)
    coef_ref[0] = first * up
    coef_ref[1] = silu
    coef_ref[2] = back * second * up
    coef_ref[3] = back * first
    coef_ref[4] = back * first * up
    coef_ref[5] = back * silu
    coef_ref[6] = silu * up


def key_kernel(scale, share, count, *refs):
    mine, recv = refs[:count], refs[count : 2 * count]
    tok_ref, sib_ref, new_ref, old_ref, vec_ref, grad_ref, coef_ref = refs[2 * count : 2 * count + 7]
    outs = refs[2 * count + 7 :]
    parts, (sums_ref, up_ref, mid_ref) = outs[:count], outs[count:]
    dim = tok_ref.shape[-1]
    half = dim // 2
    size = mine[-1].shape[0]
    total = jnp.concatenate([mine[j][:size] + recv[j][:size] for j in range(count)], axis=0)
    down_sums = mine[0][size:] + recv[0][size:]
    pieces = ((0, dim, 0), (dim, dim, 1), (2 * dim, half, 2), (2 * dim + half, half, 3))
    upper, carried = [], []
    for row, rows, slot in pieces:
        adj = total[row : row + rows]
        new = new_ref[row : row + rows, :]
        if slot < 2:
            sums = jnp.sum(new * adj, axis=0, keepdims=True)
        else:
            sums = down_sums[slot - 2 : slot - 1]
        ratio = vec_ref[slot : slot + 1, :]
        cross = vec_ref[4 + slot : 5 + slot, :]
        inverse = vec_ref[8 + slot : 9 + slot, :]
        up_adj = adj * ratio - new * (sums * cross)
        direct = old_ref[row : row + rows, :] * (sums * inverse)
        upper.append(up_adj * scale)
        carried.append((up_adj + direct) * share)
        up_ref[row : row + rows, :] = upper[-1]
    key, value = (stack_tokens(tok_ref, sib_ref, index) for index in (2, 3))
    raw = exact_left(key, split(jnp.concatenate(upper[:2], axis=1)), NN)
    back = exact_left(value, split(jnp.concatenate(upper[2:], axis=1)), NT)
    gate, up = raw[:, :half], raw[:, half:]
    hidden = coef_ref[0] * gate + coef_ref[1] * up
    d_gate = coef_ref[2] * gate + coef_ref[3] * up + coef_ref[0] * back
    d_up = coef_ref[3] * gate + coef_ref[1] * back
    d_gate_up = exact_left(key, split(jnp.concatenate([d_gate, d_up], axis=1)), TN)
    d_down = exact_right(split(hidden), value, TN)
    mid_ref[0] = d_gate
    mid_ref[1] = d_up
    mid_ref[2] = hidden
    store_parts(parts, 0, d_gate_up[:, :half] + grad_ref[:dim, :] + carried[0])
    store_parts(parts, dim, d_gate_up[:, half:] + grad_ref[dim : 2 * dim, :] + carried[1])
    sums_ref[...] = jnp.zeros_like(sums_ref)
    for block in range(2):
        row = 2 * dim + block * half
        out = d_down[:, block * half : (block + 1) * half]
        out = out + grad_ref[row : row + half, :] + carried[2 + block]
        store_parts(parts, row, out)
        sums_ref[block : block + 1, :] = jnp.sum(
            out * old_ref[row : row + half, :], axis=0, keepdims=True
        )


def token_kernel(mid_ref, coef_ref, w_ref, up_ref, mine_ref, sib_ref):
    dim = mine_ref.shape[-1]
    count = mine_ref.shape[1]
    w_gate_up, w_down = load_half(w_ref[...], dim)
    u_gate_up, u_down = load_half(up_ref[...], dim)
    left = jnp.concatenate([mid_ref[0], mid_ref[1]], axis=1)
    d_key = both_split(split(left), split(w_gate_up), NT)
    left = jnp.concatenate([coef_ref[4], coef_ref[5]], axis=1)
    d_key = d_key + both_split(split(left), split(u_gate_up), NT)
    left = jnp.concatenate([mid_ref[2], coef_ref[6]], axis=1)
    right = jnp.concatenate([w_down, u_down], axis=0)
    d_value = both_split(split(left), split(right), NN)
    mine_ref[0] = d_key[:count]
    mine_ref[1] = d_value[:count]
    sib_ref[0] = d_key[count:]
    sib_ref[1] = d_value[count:]


def working(tok_index, tok_count):
    return tok_index // (tok_count // 2) == lax.axis_index("head") % 2


def tokens_out_kernel(tok_count, *refs):
    key_ref, value_ref = refs[-2:]
    stays = working(lax.axis_index("tok"), tok_count)
    ins = refs[:-2]
    groups = len(ins) // 2
    for index in range(groups):

        def put(source):
            key_ref[index] = source[0].astype(key_ref.dtype)
            value_ref[index] = source[1].astype(value_ref.dtype)

        pl.when(stays)(functools.partial(put, ins[2 * index]))
        pl.when(jnp.logical_not(stays))(functools.partial(put, ins[2 * index + 1]))
    key_ref[groups] = jnp.zeros_like(key_ref[groups])
    value_ref[groups] = jnp.zeros_like(value_ref[groups])


def init_out_kernel(dims, *refs):
    out_ref = refs[-1]
    dim = out_ref.shape[-1]
    half = dim // 2
    for index in range(3):
        mine, recv = refs[2 * index], refs[2 * index + 1]
        size = mine.shape[1]
        axis, mask = dims[index]
        bit = (lax.axis_index(axis) // mask) % 2

        def put(first, second):
            for which in range(2):
                cut = slice(which * half, (which + 1) * half)
                for at, source in enumerate((first, second)):
                    if index < 2:
                        out_ref[index, at * size : (at + 1) * size, cut] = source[which]
                    else:
                        out_ref[index, cut, at * size : (at + 1) * size] = source[which]

        pl.when(bit == 0)(functools.partial(put, mine, recv))
        pl.when(bit != 0)(functools.partial(put, recv, mine))


def call(kernel, outs, *args, specs=None, flops=0):
    size = sum(a.size * a.dtype.itemsize for a in args)
    size += sum(o.size * o.dtype.itemsize for o in outs)
    kwargs = {} if specs is None else {"in_specs": specs}
    return pl.pallas_call(
        kernel,
        out_shape=outs,
        cost_estimate=pl.CostEstimate(flops=flops, bytes_accessed=size, transcendentals=0),
        compiler_params=pltpu.CompilerParams(vmem_limit_bytes=32 * 1024 * 1024),
        **kwargs,
    )(*args)


def shape(*dims, dtype=F32):
    return jax.ShapeDtypeStruct(dims, dtype)


def flip(array, axis, mask):
    count = lax.axis_size(axis)
    return lax.ppermute(array, axis, [(i, i ^ mask) for i in range(count)])


def swap_heads(array, tok_count, head_count):
    pairs = []
    for tok in range(tok_count):
        for head in range(head_count):
            if tok // (tok_count // 2) != head % 2:
                there = (tok ^ (tok_count // 2)) * head_count + (head ^ 1)
                pairs.append((tok * head_count + head, there))
    return lax.ppermute(array, ("tok", "head"), pairs)


def share_heads(array, tok_count, head_count):
    pairs = []
    for tok in range(tok_count):
        for head in range(head_count):
            if tok // (tok_count // 2) == head % 2:
                there = (tok ^ (tok_count // 2)) * head_count + head
                pairs.append((tok * head_count + head, there))
    return lax.ppermute(array, ("tok", "head"), pairs)


def bit_of(axis, mask):
    return (lax.axis_index(axis) // mask) % 2 == 1


def on_device(queries, keys, values, out_grad, fast_init, updates):
    tok_count = lax.axis_size("tok")
    head_count = lax.axis_size("head")
    vid_count = lax.axis_size("vid")
    _, groups, count, _, dim = queries.shape
    half = dim // 2
    rows = 3 * dim
    scale = float(count * tok_count) ** (-0.5)
    share = 2.0 / tok_count
    tok_masks = [1 << i for i in range((tok_count // 2).bit_length() - 1)]
    vid_masks = [1 << i for i in range(vid_count.bit_length() - 1)]
    assert len(tok_masks) >= 1 and 2 << len(tok_masks) == tok_count
    assert 1 << len(vid_masks) == vid_count and head_count % 2 == 0
    assert queries.shape[0] == 1 and queries.shape[3] == 1

    stays = working(lax.axis_index("tok"), tok_count)
    core = lax.axis_index("head") % 2
    flat = lambda array: array.reshape(groups, count, dim)
    q_all, k_all, v_all, c_all = (flat(a) for a in (queries, keys, values, out_grad))

    def gathered(arrays, after=None):
        own = jnp.stack(arrays).astype(F32)
        if after is not None:
            own, _ = lax.optimization_barrier((own, after))
        moved = swap_heads(own, tok_count, head_count)
        mine = jnp.where(stays, own, moved)
        return mine, flip(mine, "head", 1), moved

    top = groups - 1
    tokens = {}
    tokens[top] = gathered([q_all[top], c_all[top]])
    last = tokens[top][2]
    for index in reversed(range(top)):
        arrays = [q_all[index], c_all[index], k_all[index], v_all[index]]
        tokens[index] = gathered(arrays, last)
        last = tokens[index][2]

    init = fast_init.reshape(3, dim, dim)
    steps = updates.reshape(groups - 1, 3, dim, dim)
    vec_rows = 12
    pay_rows = groups * rows + (groups - 1) * vec_rows
    pad_rows = -pay_rows % 8
    full, mine, send = call(
        prep_kernel,
        [shape(groups - 1, 3, dim, dim)] + [shape(pay_rows + pad_rows, half)] * 2,
        init,
        steps,
    )
    weights = jnp.where(stays, mine, flip(send, "head", 1))
    level = lambda index: weights[index * rows : (index + 1) * rows]
    vectors = lambda index: weights[groups * rows + index * vec_rows :][:vec_rows]

    (query_grad,) = call(
        query_kernel,
        [shape(groups, count, dim, dtype=BF16)],
        q_all,
        c_all,
        init,
        full,
        flops=2 * groups * 10 * count * dim * dim,
    )

    n_parts = 2
    size = rows // n_parts
    part_shapes = [shape(size, half)] * n_parts
    sums_shape = shape(PAD, half)

    def reduced(outs):
        parts, sums = list(outs[:n_parts]), outs[n_parts]
        sums = sums + flip(sums, "head", 1)
        parts[0] = jnp.concatenate([parts[0], sums], axis=0)
        count_steps = len(tok_masks)
        for at in range(count_steps):
            moved = [
                flip(part, "tok", tok_masks[(at + j) % count_steps]) for j, part in enumerate(parts)
            ]
            if at + 1 < count_steps:
                parts = [part + other for part, other in zip(parts, moved)]
        return parts, moved

    product = 2 * 2 * count * dim * half
    outs = call(
        last_kernel,
        part_shapes + [sums_shape],
        tokens[top][0],
        tokens[top][1],
        level(top),
        flops=2 * 6 * product,
    )
    token_grads = {}
    for index in reversed(range(top)):
        own, other, _ = tokens[index]
        grad, coef = call(
            pre_kernel,
            [shape(rows, half), shape(7, 2 * count, half)],
            own,
            other,
            level(index),
            flops=2 * 9 * product,
        )
        parts, moved = reduced(outs)
        *outs, upper, mid = call(
            functools.partial(key_kernel, scale, share, n_parts),
            part_shapes + [sums_shape, shape(rows, half), shape(3, 2 * count, half)],
            *parts,
            *moved,
            own,
            other,
            level(index + 1),
            level(index),
            vectors(index),
            grad,
            coef,
            flops=2 * 6 * product,
        )
        d_mine, d_sib = call(
            token_kernel,
            [shape(2, count, dim)] * 2,
            mid,
            coef,
            level(index),
            upper,
            flops=3 * 6 * product,
        )
        d_mine = d_mine + flip(d_sib, "head", 1)
        token_grads[index] = (d_mine, swap_heads(d_mine, tok_count, head_count))

    dims = [("tok", mask) for mask in tok_masks] + [("vid", mask) for mask in vid_masks]
    orders = [dims[j % len(dims) :] + dims[: j % len(dims)] for j in range(3)]
    whole = jnp.concatenate(outs[:n_parts], axis=0)
    pieces = [whole[j * dim : (j + 1) * dim] for j in range(3)]
    for at in range(len(dims)):
        kept, sent = [], []
        for j in range(3):
            bit = bit_of(*orders[j][at])
            low, high = jnp.split(pieces[j], 2, axis=0)
            kept.append(jnp.where(bit, high, low))
            sent.append(jnp.where(bit, low, high))
        pieces = [kept[j] + flip(sent[j], *orders[j][at]) for j in range(3)]
    mine = jnp.stack(pieces)
    other = flip(mine, "head", 1)
    pair = jnp.stack([jnp.where(core == 0, mine, other), jnp.where(core == 0, other, mine)], axis=1)
    pair = jnp.where(stays, pair, share_heads(pair, tok_count, head_count))
    pieces = [pair[j] for j in range(3)]
    for at in reversed(range(len(dims))):
        moved = [flip(pieces[j], *orders[j][at]) for j in range(3)]
        if at == 0:
            break
        for j in range(3):
            bit = bit_of(*orders[j][at])
            low = jnp.where(bit, moved[j], pieces[j])
            high = jnp.where(bit, pieces[j], moved[j])
            pieces[j] = jnp.concatenate([low, high], axis=1)
    (init_grad,) = call(
        functools.partial(init_out_kernel, [orders[j][0] for j in range(3)]),
        [shape(3, dim, dim)],
        *[array for j in range(3) for array in (pieces[j], moved[j])],
    )

    key_grad, value_grad = call(
        functools.partial(tokens_out_kernel, tok_count),
        [shape(groups, count, dim, dtype=BF16)] * 2,
        *[array for index in range(top) for array in token_grads[index]],
    )
    back = lambda array: array.reshape(queries.shape)
    return back(query_grad), back(key_grad), back(value_grad), init_grad.reshape(fast_init.shape)


def solution(mesh):
    tokens = P("vid", None, "tok", "head", None)
    return jax.shard_map(
        on_device,
        mesh=mesh,
        in_specs=(
            tokens,
            tokens,
            tokens,
            tokens,
            P("head", None, None, None),
            P("vid", None, "head", None, None, None),
        ),
        out_specs=(tokens, tokens, tokens, P("head", None, None, None)),
        check_vma=False,
    )
```

time: 298 us -> 128 us (0.43)
  waiting for transfers between devices: 227 us -> 41.5 us
  starting transfers between devices: 0.3 us -> 58.5 us
  matrix products: 35.5 us -> 0 us
  between operations: 14.7 us -> 1.19 us
  Pallas kernels: 0 us -> 10.6 us
  other arithmetic: 10.9 us -> 5.68 us
    psum x3 -> x0, waiting for transfers between devices: 227 us -> none  [the longest x2 121 us: on_device(): adjoint = direct + upper_adj + lax.psum(wpart, 'tok')]
    ppermute x0 -> x41, starting transfers between devices: none -> 58.5 us  [the longest x35 39.7 us: flip(): return lax.ppermute(array, axis, [(i, i ^ mask) for i in range(count)])]
    ppermute x0 -> x41, waiting for transfers between devices: none -> 41.5 us  [the longest x35 25.9 us: flip(): return lax.ppermute(array, axis, [(i, i ^ mask) for i in range(count)])]
    dot_general x54 -> x0, matrix products: 35.5 us -> none  [matmul(): jnp.dot(left, right, precision=HIGH, preferred_element_type=jnp.float32)]
    pallas_call x0 -> x11, Pallas kernels: none -> 10.6 us  [call(): pl.pallas_call(kernel, out_shape=outs, cost_estimate=pl.CostEstimate(flop...]
    reduce_sum x6 -> x0, other arithmetic: 4.8 us -> none  [the longest x2 3.16 us: colnorm(): return raised * (old / new)[..., None, :]]
    unnamed x107 -> x40, local copies, waits for them, and re-layouts: 5.77 us -> 8.3 us
  transfers between devices with their start and end apart: 3 -> 41, of which waited for: 3 -> 16; matrix products, arithmetic and copies ran while one was open for 11% -> 4% of each run, Pallas kernels for 0% -> 5%
where the time goes in v1:
time: 128 us; the launch traced here: 127 us
  starting transfers between devices  58.5 us (46%)
  waiting for transfers between devices  41.5 us (32%)
  Pallas kernels  10.6 us (8%)
  local copies, waits for them, and re-layouts  9.38 us (7%)
  other arithmetic  5.68 us (4%)
    ppermute x35, starting transfers between devices, flip(): return lax.ppermute(array, axis, [(i, i ^ mask) for i in range(count)])  39.7 us
    ppermute x35, waiting for transfers between devices, flip(): return lax.ppermute(array, axis, [(i, i ^ mask) for i in range(count)])  25.9 us
    ppermute x5, starting transfers between devices, swap_heads(): return lax.ppermute(array, ('tok', 'head'), pairs)  17.4 us
    ppermute x5, waiting for transfers between devices, swap_heads(): return lax.ppermute(array, ('tok', 'head'), pairs)  13.7 us
    pallas_call x11, Pallas kernels, call(): pl.pallas_call(kernel, out_shape=outs, cost_estimate=pl.CostEstimate(flop...  10.6 us
    unnamed x40, local copies, waits for them, and re-layouts  8.3 us
  transfers between devices with their start and end apart: 41, of which 16 were waited for; matrix products, arithmetic and copies ran while one was open for 4% of the time, Pallas kernels for 5%

profile of v1, /device:TPU:1, one launch (start us, length us, event | category | flops | bytes accessed | tf_op | source)
XLA Modules:
  0.0 126.9 jit_solution(15448235541969683118)
XLA Ops:
  4.8 5.6 %collective-permute-start = (f32[2,128,256]{2,1,0:T(8,128)S(1)}, f32[2,128,256]{2,1,0:T(8,128)}, u32[]{:S(2)}, u32[]{:S(2)}) collective-permute-start(f32[2,128,256]{2,1,0:T(8,128)S(1)} %maximum_convert_fusion.2), channel_id=1, source_target_pairs={{2,16},{6,20},{10,24},{14,28},{16,2},{20,6},{24,10},{28,14},{3,17}... | collective-permute-start | bytes 786440 | tf_op jit(solution)/shard_map/ppermute | solution.py:358
  11.4 5.9 %collective-permute-done = f32[2,128,256]{2,1,0:T(8,128)} collective-permute-done((f32[2,128,256]{2,1,0:T(8,128)S(1)}, f32[2,128,256]{2,1,0:T(8,128)}, u32[]{:S(2)}, u32[]{:S(2)}) %collective-permute-start) | collective-permute-done | bytes 262176 | tf_op jit(solution)/shard_map/ppermute | solution.py:358
  18.4 1.9 %collective-permute-start.8 = (f32[4,128,256]{2,1,0:T(8,128)S(1)}, f32[4,128,256]{2,1,0:T(8,128)S(1)}, u32[]{:S(2)}, u32[]{:S(2)}) collective-permute-start(f32[4,128,256]{2,1,0:T(8,128)S(1)} %maximum_convert_fusion), channel_id=1, source_target_pairs={{2,16},{6,20},{10,24},{14,28},{16,2},{20,6},{24,10},{28,14},{3,17}... | collective-permute-start | bytes 1572872 | tf_op jit(solution)/shard_map/ppermute | solution.py:358
  20.3 1.4 %broadcast_select_fusion = f32[2328,128]{1,0:T(8,128)S(1)} fusion(f32[2328,128]{1,0:T(8,128)S(1)} %get-tuple-element.32, f32[2328,128]{1,0:T(8,128)} %collective-permute-done.2, pred[]{:T(512)S(6)} %eq.46), kind=kLoop, calls=%fused_computation | loop fusion | flops 297984 | bytes 3575809 | tf_op jit(solution)/shard_map/jit(_where)/select_n | solution.py:423
  22.5 3.9 %collective-permute-start.5 = (f32[384,128]{1,0:T(8,128)S(1)}, f32[384,128]{1,0:T(8,128)S(1)}, u32[]{:S(2)}, u32[]{:S(2)}) collective-permute-start(f32[384,128]{1,0:T(8,128)S(1)} %get-tuple-element.36), channel_id=1, source_target_pairs={{0,8},{4,12},{8,0},{12,4},{16,24},{20,28},{24,16},{28,20},{1,9},{5... | collective-permute-start | bytes 589832 | tf_op jit(solution)/shard_map/ppermute | solution.py:348
  27.7 7.8 %collective-permute-done.8 = f32[4,128,256]{2,1,0:T(8,128)S(1)} collective-permute-done((f32[4,128,256]{2,1,0:T(8,128)S(1)}, f32[4,128,256]{2,1,0:T(8,128)S(1)}, u32[]{:S(2)}, u32[]{:S(2)}) %collective-permute-start.8) | collective-permute-done | bytes 524320 | tf_op jit(solution)/shard_map/ppermute | solution.py:358
  35.7 1.9 %collective-permute-start.15 = (f32[4,128,256]{2,1,0:T(8,128)S(1)}, f32[4,128,256]{2,1,0:T(8,128)S(1)}, u32[]{:S(2)}, u32[]{:S(2)}) collective-permute-start(f32[4,128,256]{2,1,0:T(8,128)S(1)} %maximum_convert_fusion.1), channel_id=1, source_target_pairs={{2,16},{6,20},{10,24},{14,28},{16,2},{20,6},{24,10},{28,14},{3,17}... | collective-permute-start | bytes 1572872 | tf_op jit(solution)/shard_map/ppermute | solution.py:358
  37.7 1.7 %collective-permute-start.7 = (f32[384,128]{1,0:T(8,128)S(1)}, f32[384,128]{1,0:T(8,128)S(1)}, u32[]{:S(2)}, u32[]{:S(2)}) collective-permute-start(f32[384,128]{1,0:T(8,128)S(1)} %add.84.refs_1_), channel_id=1, source_target_pairs={{0,4},{4,0},{8,12},{12,8},{16,20},{20,16},{24,28},{28,24},{1,5},{5... | collective-permute-start | bytes 589832 | tf_op jit(solution)/shard_map/ppermute | solution.py:348
  41.4 3.0 %collective-permute-done.7.refs_3_ = f32[384,128]{1,0:T(8,128)S(1)} collective-permute-done((f32[384,128]{1,0:T(8,128)S(1)}, f32[384,128]{1,0:T(8,128)S(1)}, u32[]{:S(2)}, u32[]{:S(2)}) %collective-permute-start.7) | collective-permute-done | bytes 196640 | tf_op jit(solution)/shard_map/ppermute | solution.py:348
  44.4 3.7 %collective-permute-done.6.refs_2_ = f32[392,128]{1,0:T(8,128)S(1)} collective-permute-done((f32[392,128]{1,0:T(8,128)S(1)}, f32[392,128]{1,0:T(8,128)S(1)}, u32[]{:S(2)}, u32[]{:S(2)}) %collective-permute-start.6) | collective-permute-done | bytes 200736 | tf_op jit(solution)/shard_map/ppermute | solution.py:348
  50.1 1.5 %collective-permute-start.11 = (f32[392,128]{1,0:T(8,128)S(1)}, f32[392,128]{1,0:T(8,128)S(1)}, u32[]{:S(2)}, u32[]{:S(2)}) collective-permute-start(f32[392,128]{1,0:T(8,128)S(1)} %pad_maximum_fusion.1), channel_id=1, source_target_pairs={{0,4},{4,0},{8,12},{12,8},{16,20},{20,16},{24,28},{28,24},{1,5},{5... | collective-permute-start | bytes 602120 | tf_op jit(solution)/shard_map/ppermute | solution.py:348
  52.2 1.9 %collective-permute-start.12 = (f32[384,128]{1,0:T(8,128)S(1)}, f32[384,128]{1,0:T(8,128)S(1)}, u32[]{:S(2)}, u32[]{:S(2)}) collective-permute-start(f32[384,128]{1,0:T(8,128)S(1)} %get-tuple-element.42), channel_id=1, source_target_pairs={{0,8},{4,12},{8,0},{12,4},{16,24},{20,28},{24,16},{28,20},{1,9},{5... | collective-permute-start | bytes 589832 | tf_op jit(solution)/shard_map/ppermute | solution.py:348
  54.1 2.3 %collective-permute-done.11 = f32[392,128]{1,0:T(8,128)S(1)} collective-permute-done((f32[392,128]{1,0:T(8,128)S(1)}, f32[392,128]{1,0:T(8,128)S(1)}, u32[]{:S(2)}, u32[]{:S(2)}) %collective-permute-start.11) | collective-permute-done | bytes 200736 | tf_op jit(solution)/shard_map/ppermute | solution.py:348
  56.5 2.2 %collective-permute-start.13 = (f32[392,128]{1,0:T(8,128)S(1)}, f32[392,128]{1,0:T(8,128)}, u32[]{:S(2)}, u32[]{:S(2)}) collective-permute-start(f32[392,128]{1,0:T(8,128)S(1)} %fusion.refs_0_), channel_id=1, source_target_pairs={{0,8},{4,12},{8,0},{12,4},{16,24},{20,28},{24,16},{28,20},{1,9},{5... | collective-permute-start | bytes 602120 | tf_op jit(solution)/shard_map/ppermute | solution.py:348
  63.4 2.7 %collective-permute-done.14.refs_3_ = f32[384,128]{1,0:T(8,128)} collective-permute-done((f32[384,128]{1,0:T(8,128)}, f32[384,128]{1,0:T(8,128)}, u32[]{:S(2)}, u32[]{:S(2)}) %collective-permute-start.14) | collective-permute-done | bytes 196640 | tf_op jit(solution)/shard_map/ppermute | solution.py:348
  66.1 2.3 %shard_map.99 = (f32[384,128]{1,0:T(8,128)S(1)}, f32[384,128]{1,0:T(8,128)S(1)}, f32[8,128]{1,0:T(8,128)}, f32[768,128]{1,0:T(8,128)S(1)}, f32[3,256,128]{2,1,0:T(8,128)S(1)}) custom-call(f32[392,128]{1,0:T(8,128)S(1)} %fusion.refs_0_, f32[384,128]{1,0:T(8,128)} %add.87.refs_1_, f32[392,128]{1,0:T(8,128)} %collective-permute-done.13.refs_2_, ...), custom_call_target="tpu_custom_call" | custom-call | flops 201326592 | bytes 5130240 | tf_op jit(solution)/shard_map/pallas_call | solution.py:333
  70.8 1.5 %collective-permute-start.27 = (f32[128,128]{1,0:T(8,128)S(1)}, f32[128,128]{1,0:T(8,128)S(1)}, u32[]{:S(2)}, u32[]{:S(2)}) collective-permute-start(f32[128,128]{1,0:T(8,128)S(1)} %slice_select_fusion), channel_id=1, source_target_pairs={{0,1},{1,0},{2,3},{3,2},{4,5},{5,4},{6,7},{7,6},{8,9},{9,8},{10,11... | collective-permute-start | bytes 196616 | tf_op jit(solution)/shard_map/ppermute | solution.py:348
  72.3 1.5 %collective-permute-done.21 = f32[128,128]{1,0:T(8,128)S(1)} collective-permute-done((f32[128,128]{1,0:T(8,128)S(1)}, f32[128,128]{1,0:T(8,128)S(1)}, u32[]{:S(2)}, u32[]{:S(2)}) %collective-permute-start.21) | collective-permute-done | bytes 65568 | tf_op jit(solution)/shard_map/ppermute | solution.py:348
  80.3 1.5 %collective-permute-start.23 = (f32[32,128]{1,0:T(8,128)S(1)}, f32[32,128]{1,0:T(8,128)S(1)}, u32[]{:S(2)}, u32[]{:S(2)}) collective-permute-start(f32[32,128]{1,0:T(8,128)S(1)} %slice_select_fusion.8), channel_id=1, source_target_pairs={{0,1},{1,0},{2,3},{3,2},{4,5},{5,4},{6,7},{7,6},{8,9},{9,8},{10,11... | collective-permute-start | bytes 49160 | tf_op jit(solution)/shard_map/ppermute | solution.py:348
  82.8 2.7 %collective-permute-done.25 = f32[64,128]{1,0:T(8,128)S(1)} collective-permute-done((f32[64,128]{1,0:T(8,128)S(1)}, f32[64,128]{1,0:T(8,128)S(1)}, u32[]{:S(2)}, u32[]{:S(2)}) %collective-permute-start.25) | collective-permute-done | bytes 32800 | tf_op jit(solution)/shard_map/ppermute | solution.py:348
  85.8 2.6 %collective-permute-done.26 = f32[32,128]{1,0:T(8,128)S(1)} collective-permute-done((f32[32,128]{1,0:T(8,128)S(1)}, f32[32,128]{1,0:T(8,128)S(1)}, u32[]{:S(2)}, u32[]{:S(2)}) %collective-permute-start.26) | collective-permute-done | bytes 16416 | tf_op jit(solution)/shard_map/ppermute | solution.py:348
  88.5 7.2 %collective-permute-start.30 = (f32[3,32,128]{2,1,0:T(8,128)S(1)}, f32[3,32,128]{2,1,0:T(8,128)S(1)}, u32[]{:S(2)}, u32[]{:S(2)}) collective-permute-start(f32[3,32,128]{2,1,0:T(8,128)S(1)} %pad_maximum_fusion.9), channel_id=1, source_target_pairs={{0,2},{2,0},{1,3},{3,1},{4,6},{6,4},{5,7},{7,5},{8,10},{10,8},{9,1... | collective-permute-start | bytes 147464 | tf_op jit(solution)/shard_map/ppermute | solution.py:348
  96.6 1.4 %collective-permute-start.31 = (f32[3,2,32,128]{3,2,1,0:T(8,128)S(1)}, f32[3,2,32,128]{3,2,1,0:T(8,128)S(1)}, u32[]{:S(2)}, u32[]{:S(2)}) collective-permute-start(f32[3,2,32,128]{3,2,1,0:T(8,128)S(1)} %pad_maximum_fusion.5), channel_id=1, source_target_pairs={{0,16},{4,20},{8,24},{12,28},{18,2},{22,6},{26,10},{30,14},{1,17},... | collective-permute-start | bytes 294920 | tf_op jit(solution)/shard_map/ppermute | solution.py:368
  99.6 1.7 %collective-permute-start.19 = (f32[2,128,256]{2,1,0:T(8,128)S(1)}, f32[2,128,256]{2,1,0:T(8,128)S(1)}, u32[]{:S(2)}, u32[]{:S(2)}) collective-permute-start(f32[2,128,256]{2,1,0:T(8,128)S(1)} %get-tuple-element.53), channel_id=1, source_target_pairs={{0,2},{2,0},{1,3},{3,1},{4,6},{6,4},{5,7},{7,5},{8,10},{10,8},{9,1... | collective-permute-start | bytes 786440 | tf_op jit(solution)/shard_map/ppermute | solution.py:348
  102.3 1.8 %collective-permute-done.31 = f32[3,2,32,128]{3,2,1,0:T(8,128)S(1)} collective-permute-done((f32[3,2,32,128]{3,2,1,0:T(8,128)S(1)}, f32[3,2,32,128]{3,2,1,0:T(8,128)S(1)}, u32[]{:S(2)}, u32[]{:S(2)}) %collective-permute-start.31) | collective-permute-done | bytes 98336 | tf_op jit(solution)/shard_map/ppermute | solution.py:368
  104.6 6.0 %collective-permute-start.20 = (f32[2,128,256]{2,1,0:T(8,128)S(1)}, f32[2,128,256]{2,1,0:T(8,128)S(1)}, u32[]{:S(2)}, u32[]{:S(2)}) collective-permute-start(f32[2,128,256]{2,1,0:T(8,128)S(1)} %add.89.refs_2_), channel_id=1, source_target_pairs={{2,16},{6,20},{10,24},{14,28},{16,2},{20,6},{24,10},{28,14},{3,17}... | collective-permute-start | bytes 786440 | tf_op jit(solution)/shard_map/ppermute | solution.py:358
  110.6 2.1 %collective-permute-start.18 = (f32[2,128,256]{2,1,0:T(8,128)S(1)}, f32[2,128,256]{2,1,0:T(8,128)S(1)}, u32[]{:S(2)}, u32[]{:S(2)}) collective-permute-start(f32[2,128,256]{2,1,0:T(8,128)S(1)} %add.88.refs_0_), channel_id=1, source_target_pairs={{2,16},{6,20},{10,24},{14,28},{16,2},{20,6},{24,10},{28,14},{3,17}... | collective-permute-start | bytes 786440 | tf_op jit(solution)/shard_map/ppermute | solution.py:358
  112.9 1.6 %collective-permute-start.36 = (f32[2,64,128]{2,1,0:T(8,128)S(1)}, f32[2,64,128]{2,1,0:T(8,128)S(1)}, u32[]{:S(2)}, u32[]{:S(2)}) collective-permute-start(f32[2,64,128]{2,1,0:T(8,128)S(1)} %pad_maximum_fusion.7), channel_id=1, source_target_pairs={{0,1},{1,0},{2,3},{3,2},{4,5},{5,4},{6,7},{7,6},{8,9},{9,8},{10,11... | collective-permute-start | bytes 196616 | tf_op jit(solution)/shard_map/ppermute | solution.py:348
  115.5 3.6 %collective-permute-done.33 = f32[2,64,128]{2,1,0:T(8,128)S(1)} collective-permute-done((f32[2,64,128]{2,1,0:T(8,128)S(1)}, f32[2,64,128]{2,1,0:T(8,128)S(1)}, u32[]{:S(2)}, u32[]{:S(2)}) %collective-permute-start.33) | collective-permute-done | bytes 65568 | tf_op jit(solution)/shard_map/ppermute | solution.py:348
  119.3 2.3 %collective-permute-start.37 = (f32[2,128,128]{2,1,0:T(8,128)S(1)}, f32[2,128,128]{2,1,0:T(8,128)S(1)}, u32[]{:S(2)}, u32[]{:S(2)}) collective-permute-start(f32[2,128,128]{2,1,0:T(8,128)S(1)} %pad_maximum_fusion.3.refs_2_), channel_id=1, source_target_pairs={{0,8},{4,12},{8,0},{12,4},{16,24},{20,28},{24,16},{28,20},{1,9},{5... | collective-permute-start | bytes 393224 | tf_op jit(solution)/shard_map/ppermute | solution.py:348
  121.6 1.6 %collective-permute-start.40 = (f32[2,128,128]{2,1,0:T(8,128)S(1)}, f32[2,128,128]{2,1,0:T(8,128)S(1)}, u32[]{:S(2)}, u32[]{:S(2)}) collective-permute-start(f32[2,128,128]{2,1,0:T(8,128)S(1)} %pad_maximum_fusion.4.refs_4_), channel_id=1, source_target_pairs={{0,1},{1,0},{2,3},{3,2},{4,5},{5,4},{6,7},{7,6},{8,9},{9,8},{10,11... | collective-permute-start | bytes 393224 | tf_op jit(solution)/shard_map/ppermute | solution.py:348
  123.2 1.9 %shard_map.94 = bf16[3,128,256]{2,1,0:T(8,128)(2,1)} custom-call(bf16[3,128,256]{2,1,0:T(8,128)(2,1)S(1)} %bitcast.67, bf16[3,128,256]{2,1,0:T(8,128)(2,1)S(1)} %bitcast.68, bf16[3,256,256]{2,1,0:T(8,128)(2,1)S(1)} %bitcast.65, f32[2,3,256,256]{3,2,1,0:T(8,128)S(1)} %copy-done.3), custom_call_target="tpu_custom_call" | custom-call | flops 503316480 | bytes 2555904 | tf_op jit(solution)/shard_map/pallas_call | solution.py:333
  (153 shorter events, 35.1 us)
Async XLA Ops:
  4.7 15.6 %collective-permute-start.2 = (f32[2328,128]{1,0:T(8,128)S(1)}, f32[2328,128]{1,0:T(8,128)}, u32[]{:S(2)}, u32[]{:S(2)}) collective-permute-start(f32[2328,128]{1,0:T(8,128)S(1)} %get-tuple-element.33), channel_id=1, source_target_pairs={{0,2},{2,0},{1,3},{3,1},{4,6},{6,4},{5,7},{7,5},{8,10},{10,8},{9,1... | collective-permute-start | bytes 3575816 | tf_op jit(solution)/shard_map/ppermute | solution.py:348
  4.8 12.5 %collective-permute-start = (f32[2,128,256]{2,1,0:T(8,128)S(1)}, f32[2,128,256]{2,1,0:T(8,128)}, u32[]{:S(2)}, u32[]{:S(2)}) collective-permute-start(f32[2,128,256]{2,1,0:T(8,128)S(1)} %maximum_convert_fusion.2), channel_id=1, source_target_pairs={{2,16},{6,20},{10,24},{14,28},{16,2},{20,6},{24,10},{28,14},{3,17}... | collective-permute-start | bytes 786440 | tf_op jit(solution)/shard_map/ppermute | solution.py:358
  18.4 17.1 %collective-permute-start.8 = (f32[4,128,256]{2,1,0:T(8,128)S(1)}, f32[4,128,256]{2,1,0:T(8,128)S(1)}, u32[]{:S(2)}, u32[]{:S(2)}) collective-permute-start(f32[4,128,256]{2,1,0:T(8,128)S(1)} %maximum_convert_fusion), channel_id=1, source_target_pairs={{2,16},{6,20},{10,24},{14,28},{16,2},{20,6},{24,10},{28,14},{3,17}... | collective-permute-start | bytes 1572872 | tf_op jit(solution)/shard_map/ppermute | solution.py:358
  22.5 15.1 %collective-permute-start.5 = (f32[384,128]{1,0:T(8,128)S(1)}, f32[384,128]{1,0:T(8,128)S(1)}, u32[]{:S(2)}, u32[]{:S(2)}) collective-permute-start(f32[384,128]{1,0:T(8,128)S(1)} %get-tuple-element.36), channel_id=1, source_target_pairs={{0,8},{4,12},{8,0},{12,4},{16,24},{20,28},{24,16},{28,20},{1,9},{5... | collective-permute-start | bytes 589832 | tf_op jit(solution)/shard_map/ppermute | solution.py:348
  26.4 13.0 %collective-permute-start.4 = (f32[392,128]{1,0:T(8,128)S(1)}, f32[392,128]{1,0:T(8,128)S(1)}, u32[]{:S(2)}, u32[]{:S(2)}) collective-permute-start(f32[392,128]{1,0:T(8,128)S(1)} %pad_maximum_fusion), channel_id=1, source_target_pairs={{0,4},{4,0},{8,12},{12,8},{16,20},{20,16},{24,28},{28,24},{1,5},{5... | collective-permute-start | bytes 602120 | tf_op jit(solution)/shard_map/ppermute | solution.py:348
  35.6 5.1 %collective-permute-start.9 = (f32[4,128,256]{2,1,0:T(8,128)S(1)}, f32[4,128,256]{2,1,0:T(8,128)S(1)}, u32[]{:S(2)}, u32[]{:S(2)}) collective-permute-start(f32[4,128,256]{2,1,0:T(8,128)S(1)} %broadcast_select_fusion.2.mine_ref.refs_4_), channel_id=1, source_target_pairs={{0,2},{2,0},{1,3},{3,1},{4,6},{6,4},{5,7},{7,5},{8,10},{10,8},{9,1... | collective-permute-start | bytes 1572872 | tf_op jit(solution)/shard_map/ppermute | solution.py:348
  35.7 15.9 %collective-permute-start.15 = (f32[4,128,256]{2,1,0:T(8,128)S(1)}, f32[4,128,256]{2,1,0:T(8,128)S(1)}, u32[]{:S(2)}, u32[]{:S(2)}) collective-permute-start(f32[4,128,256]{2,1,0:T(8,128)S(1)} %maximum_convert_fusion.1), channel_id=1, source_target_pairs={{2,16},{6,20},{10,24},{14,28},{16,2},{20,6},{24,10},{28,14},{3,17}... | collective-permute-start | bytes 1572872 | tf_op jit(solution)/shard_map/ppermute | solution.py:358
  37.7 6.7 %collective-permute-start.7 = (f32[384,128]{1,0:T(8,128)S(1)}, f32[384,128]{1,0:T(8,128)S(1)}, u32[]{:S(2)}, u32[]{:S(2)}) collective-permute-start(f32[384,128]{1,0:T(8,128)S(1)} %add.84.refs_1_), channel_id=1, source_target_pairs={{0,4},{4,0},{8,12},{12,8},{16,20},{20,16},{24,28},{28,24},{1,5},{5... | collective-permute-start | bytes 589832 | tf_op jit(solution)/shard_map/ppermute | solution.py:348
  39.4 8.7 %collective-permute-start.6 = (f32[392,128]{1,0:T(8,128)S(1)}, f32[392,128]{1,0:T(8,128)S(1)}, u32[]{:S(2)}, u32[]{:S(2)}) collective-permute-start(f32[392,128]{1,0:T(8,128)S(1)} %fusion.1.refs_0_), channel_id=1, source_target_pairs={{0,8},{4,12},{8,0},{12,4},{16,24},{20,28},{24,16},{28,20},{1,9},{5... | collective-permute-start | bytes 602120 | tf_op jit(solution)/shard_map/ppermute | solution.py:348
  50.1 6.3 %collective-permute-start.11 = (f32[392,128]{1,0:T(8,128)S(1)}, f32[392,128]{1,0:T(8,128)S(1)}, u32[]{:S(2)}, u32[]{:S(2)}) collective-permute-start(f32[392,128]{1,0:T(8,128)S(1)} %pad_maximum_fusion.1), channel_id=1, source_target_pairs={{0,4},{4,0},{8,12},{12,8},{16,20},{20,16},{24,28},{28,24},{1,5},{5... | collective-permute-start | bytes 602120 | tf_op jit(solution)/shard_map/ppermute | solution.py:348
  51.7 9.1 %collective-permute-start.16 = (f32[4,128,256]{2,1,0:T(8,128)S(1)}, f32[4,128,256]{2,1,0:T(8,128)S(1)}, u32[]{:S(2)}, u32[]{:S(2)}) collective-permute-start(f32[4,128,256]{2,1,0:T(8,128)S(1)} %broadcast_select_fusion.1.mine_ref.refs_4_), channel_id=1, source_target_pairs={{0,2},{2,0},{1,3},{3,1},{4,6},{6,4},{5,7},{7,5},{8,10},{10,8},{9,1... | collective-permute-start | bytes 1572872 | tf_op jit(solution)/shard_map/ppermute | solution.py:348
  52.2 7.1 %collective-permute-start.12 = (f32[384,128]{1,0:T(8,128)S(1)}, f32[384,128]{1,0:T(8,128)S(1)}, u32[]{:S(2)}, u32[]{:S(2)}) collective-permute-start(f32[384,128]{1,0:T(8,128)S(1)} %get-tuple-element.42), channel_id=1, source_target_pairs={{0,8},{4,12},{8,0},{12,4},{16,24},{20,28},{24,16},{28,20},{1,9},{5... | collective-permute-start | bytes 589832 | tf_op jit(solution)/shard_map/ppermute | solution.py:348
  56.5 9.6 %collective-permute-start.13 = (f32[392,128]{1,0:T(8,128)S(1)}, f32[392,128]{1,0:T(8,128)}, u32[]{:S(2)}, u32[]{:S(2)}) collective-permute-start(f32[392,128]{1,0:T(8,128)S(1)} %fusion.refs_0_), channel_id=1, source_target_pairs={{0,8},{4,12},{8,0},{12,4},{16,24},{20,28},{24,16},{28,20},{1,9},{5... | collective-permute-start | bytes 602120 | tf_op jit(solution)/shard_map/ppermute | solution.py:348
  60.0 6.1 %collective-permute-start.14 = (f32[384,128]{1,0:T(8,128)}, f32[384,128]{1,0:T(8,128)}, u32[]{:S(2)}, u32[]{:S(2)}) collective-permute-start(f32[384,128]{1,0:T(8,128)} %add.87.refs_1_), channel_id=1, source_target_pairs={{0,4},{4,0},{8,12},{12,8},{16,20},{20,16},{24,28},{28,24},{1,5},{5... | collective-permute-start | bytes 589832 | tf_op jit(solution)/shard_map/ppermute | solution.py:348
  76.4 5.3 %collective-permute-start.24 = (f32[128,128]{1,0:T(8,128)S(1)}, f32[128,128]{1,0:T(8,128)S(1)}, u32[]{:S(2)}, u32[]{:S(2)}) collective-permute-start(f32[128,128]{1,0:T(8,128)S(1)} %get-tuple-element.68), channel_id=1, source_target_pairs={{0,8},{4,12},{8,0},{12,4},{16,24},{20,28},{24,16},{28,20},{1,9},{5... | collective-permute-start | bytes 196616 | tf_op jit(solution)/shard_map/ppermute | solution.py:348
  77.9 4.9 %collective-permute-start.29 = (f32[32,128]{1,0:T(8,128)S(1)}, f32[32,128]{1,0:T(8,128)S(1)}, u32[]{:S(2)}, u32[]{:S(2)}) collective-permute-start(f32[32,128]{1,0:T(8,128)S(1)} %slice_select_fusion.6), channel_id=1, source_target_pairs={{0,8},{4,12},{8,0},{12,4},{16,24},{20,28},{24,16},{28,20},{1,9},{5... | collective-permute-start | bytes 49160 | tf_op jit(solution)/shard_map/ppermute | solution.py:348
  80.3 5.5 %collective-permute-start.23 = (f32[32,128]{1,0:T(8,128)S(1)}, f32[32,128]{1,0:T(8,128)S(1)}, u32[]{:S(2)}, u32[]{:S(2)}) collective-permute-start(f32[32,128]{1,0:T(8,128)S(1)} %slice_select_fusion.8), channel_id=1, source_target_pairs={{0,1},{1,0},{2,3},{3,2},{4,5},{5,4},{6,7},{7,6},{8,9},{9,8},{10,11... | collective-permute-start | bytes 49160 | tf_op jit(solution)/shard_map/ppermute | solution.py:348
  88.5 8.1 %collective-permute-start.30 = (f32[3,32,128]{2,1,0:T(8,128)S(1)}, f32[3,32,128]{2,1,0:T(8,128)S(1)}, u32[]{:S(2)}, u32[]{:S(2)}) collective-permute-start(f32[3,32,128]{2,1,0:T(8,128)S(1)} %pad_maximum_fusion.9), channel_id=1, source_target_pairs={{0,2},{2,0},{1,3},{3,1},{4,6},{6,4},{5,7},{7,5},{8,10},{10,8},{9,1... | collective-permute-start | bytes 147464 | tf_op jit(solution)/shard_map/ppermute | solution.py:348
  96.6 7.4 %collective-permute-start.31 = (f32[3,2,32,128]{3,2,1,0:T(8,128)S(1)}, f32[3,2,32,128]{3,2,1,0:T(8,128)S(1)}, u32[]{:S(2)}, u32[]{:S(2)}) collective-permute-start(f32[3,2,32,128]{3,2,1,0:T(8,128)S(1)} %pad_maximum_fusion.5), channel_id=1, source_target_pairs={{0,16},{4,20},{8,24},{12,28},{18,2},{22,6},{26,10},{30,14},{1,17},... | collective-permute-start | bytes 294920 | tf_op jit(solution)/shard_map/ppermute | solution.py:368
  99.6 4.9 %collective-permute-start.19 = (f32[2,128,256]{2,1,0:T(8,128)S(1)}, f32[2,128,256]{2,1,0:T(8,128)S(1)}, u32[]{:S(2)}, u32[]{:S(2)}) collective-permute-start(f32[2,128,256]{2,1,0:T(8,128)S(1)} %get-tuple-element.53), channel_id=1, source_target_pairs={{0,2},{2,0},{1,3},{3,1},{4,6},{6,4},{5,7},{7,5},{8,10},{10,8},{9,1... | collective-permute-start | bytes 786440 | tf_op jit(solution)/shard_map/ppermute | solution.py:348
  101.8 8.8 %collective-permute-start.17 = (f32[2,128,256]{2,1,0:T(8,128)S(1)}, f32[2,128,256]{2,1,0:T(8,128)S(1)}, u32[]{:S(2)}, u32[]{:S(2)}) collective-permute-start(f32[2,128,256]{2,1,0:T(8,128)S(1)} %get-tuple-element.49), channel_id=1, source_target_pairs={{0,2},{2,0},{1,3},{3,1},{4,6},{6,4},{5,7},{7,5},{8,10},{10,8},{9,1... | collective-permute-start | bytes 786440 | tf_op jit(solution)/shard_map/ppermute | solution.py:348
  104.1 8.6 %collective-permute-start.38 = (f32[2,32,128]{2,1,0:T(8,128)S(1)}, f32[2,32,128]{2,1,0:T(8,128)S(1)}, u32[]{:S(2)}, u32[]{:S(2)}) collective-permute-start(f32[2,32,128]{2,1,0:T(8,128)S(1)} %get-tuple-element.96), channel_id=1, source_target_pairs={{0,8},{4,12},{8,0},{12,4},{16,24},{20,28},{24,16},{28,20},{1,9},{5... | collective-permute-start | bytes 98312 | tf_op jit(solution)/shard_map/ppermute | solution.py:348
  104.2 8.5 %collective-permute-start.35 = (f32[2,32,128]{2,1,0:T(8,128)S(1)}, f32[2,32,128]{2,1,0:T(8,128)S(1)}, u32[]{:S(2)}, u32[]{:S(2)}) collective-permute-start(f32[2,32,128]{2,1,0:T(8,128)S(1)} %get-tuple-element.97), channel_id=1, source_target_pairs={{0,4},{4,0},{8,12},{12,8},{16,20},{20,16},{24,28},{28,24},{1,5},{5... | collective-permute-start | bytes 98312 | tf_op jit(solution)/shard_map/ppermute | solution.py:348
  104.5 8.2 %collective-permute-start.32 = (f32[2,32,128]{2,1,0:T(8,128)S(1)}, f32[2,32,128]{2,1,0:T(8,128)S(1)}, u32[]{:S(2)}, u32[]{:S(2)}) collective-permute-start(f32[2,32,128]{2,1,0:T(8,128)S(1)} %get-tuple-element.98), channel_id=1, source_target_pairs={{0,1},{1,0},{2,3},{3,2},{4,5},{5,4},{6,7},{7,6},{8,9},{9,8},{10,11... | collective-permute-start | bytes 98312 | tf_op jit(solution)/shard_map/ppermute | solution.py:348
  104.6 20.5 %collective-permute-start.20 = (f32[2,128,256]{2,1,0:T(8,128)S(1)}, f32[2,128,256]{2,1,0:T(8,128)S(1)}, u32[]{:S(2)}, u32[]{:S(2)}) collective-permute-start(f32[2,128,256]{2,1,0:T(8,128)S(1)} %add.89.refs_2_), channel_id=1, source_target_pairs={{2,16},{6,20},{10,24},{14,28},{16,2},{20,6},{24,10},{28,14},{3,17}... | collective-permute-start | bytes 786440 | tf_op jit(solution)/shard_map/ppermute | solution.py:358
  110.6 14.5 %collective-permute-start.18 = (f32[2,128,256]{2,1,0:T(8,128)S(1)}, f32[2,128,256]{2,1,0:T(8,128)S(1)}, u32[]{:S(2)}, u32[]{:S(2)}) collective-permute-start(f32[2,128,256]{2,1,0:T(8,128)S(1)} %add.88.refs_0_), channel_id=1, source_target_pairs={{2,16},{6,20},{10,24},{14,28},{16,2},{20,6},{24,10},{28,14},{3,17}... | collective-permute-start | bytes 786440 | tf_op jit(solution)/shard_map/ppermute | solution.py:358
  112.8 6.3 %collective-permute-start.33 = (f32[2,64,128]{2,1,0:T(8,128)S(1)}, f32[2,64,128]{2,1,0:T(8,128)S(1)}, u32[]{:S(2)}, u32[]{:S(2)}) collective-permute-start(f32[2,64,128]{2,1,0:T(8,128)S(1)} %pad_maximum_fusion.6), channel_id=1, source_target_pairs={{0,8},{4,12},{8,0},{12,4},{16,24},{20,28},{24,16},{28,20},{1,9},{5... | collective-permute-start | bytes 196616 | tf_op jit(solution)/shard_map/ppermute | solution.py:348
  112.9 6.3 %collective-permute-start.36 = (f32[2,64,128]{2,1,0:T(8,128)S(1)}, f32[2,64,128]{2,1,0:T(8,128)S(1)}, u32[]{:S(2)}, u32[]{:S(2)}) collective-permute-start(f32[2,64,128]{2,1,0:T(8,128)S(1)} %pad_maximum_fusion.7), channel_id=1, source_target_pairs={{0,1},{1,0},{2,3},{3,2},{4,5},{5,4},{6,7},{7,6},{8,9},{9,8},{10,11... | collective-permute-start | bytes 196616 | tf_op jit(solution)/shard_map/ppermute | solution.py:348
  114.5 7.0 %collective-permute-start.39 = (f32[2,64,128]{2,1,0:T(8,128)S(1)}, f32[2,64,128]{2,1,0:T(8,128)S(1)}, u32[]{:S(2)}, u32[]{:S(2)}) collective-permute-start(f32[2,64,128]{2,1,0:T(8,128)S(1)} %pad_maximum_fusion.8), channel_id=1, source_target_pairs={{0,4},{4,0},{8,12},{12,8},{16,20},{20,16},{24,28},{28,24},{1,5},{5... | collective-permute-start | bytes 196616 | tf_op jit(solution)/shard_map/ppermute | solution.py:348
  119.1 6.8 %collective-permute-start.34 = (f32[2,128,128]{2,1,0:T(8,128)S(1)}, f32[2,128,128]{2,1,0:T(8,128)S(1)}, u32[]{:S(2)}, u32[]{:S(2)}) collective-permute-start(f32[2,128,128]{2,1,0:T(8,128)S(1)} %pad_maximum_fusion.2.refs_0_), channel_id=1, source_target_pairs={{0,4},{4,0},{8,12},{12,8},{16,20},{20,16},{24,28},{28,24},{1,5},{5... | collective-permute-start | bytes 393224 | tf_op jit(solution)/shard_map/ppermute | solution.py:348
  119.3 6.6 %collective-permute-start.37 = (f32[2,128,128]{2,1,0:T(8,128)S(1)}, f32[2,128,128]{2,1,0:T(8,128)S(1)}, u32[]{:S(2)}, u32[]{:S(2)}) collective-permute-start(f32[2,128,128]{2,1,0:T(8,128)S(1)} %pad_maximum_fusion.3.refs_2_), channel_id=1, source_target_pairs={{0,8},{4,12},{8,0},{12,4},{16,24},{20,28},{24,16},{28,20},{1,9},{5... | collective-permute-start | bytes 393224 | tf_op jit(solution)/shard_map/ppermute | solution.py:348
  121.6 4.3 %collective-permute-start.40 = (f32[2,128,128]{2,1,0:T(8,128)S(1)}, f32[2,128,128]{2,1,0:T(8,128)S(1)}, u32[]{:S(2)}, u32[]{:S(2)}) collective-permute-start(f32[2,128,128]{2,1,0:T(8,128)S(1)} %pad_maximum_fusion.4.refs_4_), channel_id=1, source_target_pairs={{0,1},{1,0},{2,3},{3,2},{4,5},{5,4},{6,7},{7,6},{8,9},{9,8},{10,11... | collective-permute-start | bytes 393224 | tf_op jit(solution)/shard_map/ppermute | solution.py:348
  (29 other events, 125.1 us)

commit v2 on v1

v2 whole, which is shorter than its diff:
```python
import functools

import jax
import jax.numpy as jnp
from jax import lax
from jax.experimental import pallas as pl
from jax.experimental.pallas import tpu as pltpu
from jax.sharding import PartitionSpec as P

EPS = 1e-06
F32 = jnp.float32
BF16 = jnp.bfloat16
NN = (((1,), (0,)), ((), ()))
NT = (((1,), (1,)), ((), ()))
TN = (((0,), (0,)), ((), ()))
PAD = 8
VEC = 12


def dot(left, right, dims):
    return lax.dot_general(left, right, dims, preferred_element_type=F32)


def split(array):
    high = array.astype(BF16)
    return high, (array - high.astype(F32)).astype(BF16)


def exact_left(left, right, dims):
    return dot(left, right[0], dims) + dot(left, right[1], dims)


def exact_right(left, right, dims):
    return dot(left[0], right, dims) + dot(left[1], right, dims)


def both_split(left, right, dims):
    return (
        dot(left[0], right[0], dims)
        + (dot(left[0], right[1], dims) + dot(left[1], right[0], dims))
    )


def silu_parts(gate):
    sigma = jax.nn.sigmoid(gate)
    rest = 1.0 - sigma
    silu = gate * sigma
    first = sigma * (1.0 + gate * rest)
    second = sigma * rest * (2.0 + gate * (1.0 - 2.0 * sigma))
    return silu, first, second


def rows_of_half(gate, up, down, which):
    dim = gate.shape[0]
    half = dim // 2
    cut = slice(which * half, (which + 1) * half)
    return [
        (0, gate[:, cut]),
        (dim, up[:, cut]),
        (2 * dim, down[cut, :half]),
        (2 * dim + half, down[cut, half:]),
    ]


def load_half(rows, dim):
    half = dim // 2
    gate_up = jnp.concatenate([rows[:dim], rows[dim : 2 * dim]], axis=1)
    down = jnp.concatenate([rows[2 * dim : 2 * dim + half], rows[2 * dim + half :]], axis=1)
    return gate_up, down


def prep_kernel(init_hbm, upd_hbm, full_ref, *refs):
    *halves, init_ref, upd_ref, sems = refs
    levels = range(upd_ref.shape[0])
    pairs = [(init_hbm, init_ref)] + [(upd_hbm.at[at], upd_ref.at[at]) for at in levels]
    fetch(pairs, sems)
    groups = upd_ref.shape[0] + 1
    dim = init_ref.shape[-1]
    half = dim // 2
    core = lax.axis_index("head") % 2
    weights = [init_ref[index].astype(F32) for index in range(3)]
    vectors = []
    levels = []
    for level in range(groups):
        levels.append(weights)
        if level + 1 == groups:
            break
        raised, ratio, cross, inverse = [], [], [], []
        for index in range(3):
            up = weights[index] + upd_ref[level, index].astype(F32)
            old2 = jnp.sum(weights[index] * weights[index], axis=0, keepdims=True) + EPS
            new2 = jnp.sum(up * up, axis=0, keepdims=True) + EPS
            old, new = jnp.sqrt(old2), jnp.sqrt(new2)
            ratio.append(old / new)
            cross.append(1.0 / (old * new))
            inverse.append(1.0 / old2)
            raised.append(up * ratio[index])
        vectors.append((ratio, cross, inverse))
        weights = raised
        for index in range(3):
            full_ref[level, index] = weights[index]

    def write(top_ref, ref, which):
        cut = slice(which * half, (which + 1) * half)
        for level in range(groups):
            target, base = (ref, level * 3 * dim) if level + 1 < groups else (top_ref, 0)
            for row, value in rows_of_half(*levels[level], which):
                target[base + row : base + row + value.shape[0], :] = value
        base = (groups - 1) * 3 * dim
        for kinds in vectors:
            for gate, up, down in kinds:
                for value in (gate[:, cut], up[:, cut], down[:, :half], down[:, half:]):
                    ref[base : base + 1, :] = value
                    base += 1

    @pl.when(core == 0)
    def _():
        write(*halves[:2], 0)
        write(*halves[2:], 1)

    @pl.when(core != 0)
    def _():
        write(*halves[:2], 1)
        write(*halves[2:], 0)


def query_kernel(q_ref, c_ref, init_ref, full_ref, out_ref):
    groups = q_ref.shape[0]
    for index in range(groups):
        query, cot = q_ref[index], c_ref[index]
        if index == 0:
            pieces = [(init_ref[part], None) for part in range(3)]
        else:
            pieces = [split(full_ref[index - 1, part]) for part in range(3)]

        def apply(left, right, dims):
            return dot(left, right[0], dims) if right[1] is None else exact_left(left, right, dims)

        gate = apply(query, pieces[0], NN)
        up = apply(query, pieces[1], NN)
        back = apply(cot, pieces[2], NT)
        silu, first, _ = silu_parts(gate)
        total = None
        for value, piece in ((back * up * first, pieces[0]), (back * silu, pieces[1])):
            value = split(value)
            term = exact_right(value, piece[0], NT) if piece[1] is None else both_split(value, piece, NT)
            total = term if total is None else total + term
        out_ref[index] = total.astype(out_ref.dtype)


def apply_terms(query, cot, rows, dim):
    half = dim // 2
    gate_up, down = load_half(rows, dim)
    raw = exact_left(query, split(gate_up), NN)
    back = exact_left(cot, split(down), NT)
    gate, up = raw[:, :half], raw[:, half:]
    silu, first, _ = silu_parts(gate)
    grads = jnp.concatenate([back * up * first, back * silu], axis=1)
    d_gate_up = exact_left(query, split(grads), TN)
    d_down = exact_right(split(silu * up), cot, TN)
    return d_gate_up, d_down


def fetch(pairs, sems):
    copies = [
        pltpu.make_async_copy(source, target, sems.at[at])
        for at, (source, target) in enumerate(pairs)
    ]
    for copy in copies:
        copy.start()
    for copy in copies:
        copy.wait()


def send_kernel(group, count, *refs):
    ins, outs, (scratch, sems) = refs[:count], refs[count:-2], refs[-2:]
    fetch([(ref.at[group], scratch.at[at]) for at, ref in enumerate(ins)], sems)
    for index in range(count):
        outs[index // 2][index % 2] = scratch[index].astype(F32)


def weights_kernel(tok_count, *refs):
    mine_ref, recv_ref = refs[:2]
    outs = refs[2:]
    stays = working(tok_count)

    def put(source):
        base = 0
        for ref in outs:
            ref[...] = source[base : base + ref.shape[0], :]
            base += ref.shape[0]

    pl.when(stays)(functools.partial(put, mine_ref))
    pl.when(jnp.logical_not(stays))(functools.partial(put, recv_ref))


def pick_tokens(tok_count, token_refs, scratch):
    count = token_refs[0].shape[1]
    stays = working(tok_count)

    def put(base, first, second):
        for index in range(2):
            scratch[base + index, :count, :] = first[index].astype(BF16)
            scratch[base + index, count:, :] = second[index].astype(BF16)

    for base in range(0, scratch.shape[0], 2):
        own_ref, first_ref, late_ref = token_refs[3 * base // 2 :][:3]
        pl.when(stays)(functools.partial(put, base, own_ref, first_ref))
        pl.when(jnp.logical_not(stays))(functools.partial(put, base, first_ref, late_ref))


def last_kernel(tok_count, *refs):
    token_refs, w_ref, out_ref, scratch = refs[:3], *refs[3:]
    dim = scratch.shape[-1]
    half = dim // 2
    pick_tokens(tok_count, token_refs, scratch)
    d_gate_up, d_down = apply_terms(scratch[0], scratch[1], w_ref[...], dim)
    out_ref[:dim, :] = d_gate_up[:, :half]
    out_ref[dim : 2 * dim, :] = d_gate_up[:, half:]
    out_ref[3 * dim :, :] = jnp.zeros((PAD, half), F32)
    for block in range(2):
        value = d_down[:, block * half : (block + 1) * half]
        row = 2 * dim + block * half
        out_ref[row : row + half, :] = value
        out_ref[3 * dim + block : 3 * dim + block + 1, :] = jnp.sum(
            value * w_ref[row : row + half, :], axis=0, keepdims=True
        )


def pre_kernel(tok_count, *refs):
    token_refs, w_ref, grad_ref, coef_ref, tok_ref, scratch = refs[:6], *refs[6:]
    dim = scratch.shape[-1]
    half = dim // 2
    pick_tokens(tok_count, token_refs, scratch)
    query, cot, key, value = (scratch[index] for index in range(4))
    tok_ref[0] = key
    tok_ref[1] = value
    rows = w_ref[...]
    d_gate_up, d_down = apply_terms(query, cot, rows, dim)
    grad_ref[:dim, :] = d_gate_up[:, :half]
    grad_ref[dim : 2 * dim, :] = d_gate_up[:, half:]
    grad_ref[2 * dim : 2 * dim + half, :] = d_down[:, :half]
    grad_ref[2 * dim + half :, :] = d_down[:, half:]
    gate_up, down = load_half(rows, dim)
    raw = exact_left(key, split(gate_up), NN)
    back = exact_left(value, split(down), NT)
    gate, up = raw[:, :half], raw[:, half:]
    silu, first, second = silu_parts(gate)
    coef_ref[0] = first * up
    coef_ref[1] = silu
    coef_ref[2] = back * second * up
    coef_ref[3] = back * first
    coef_ref[4] = back * first * up
    coef_ref[5] = back * silu
    coef_ref[6] = silu * up


def add_kernel(mine_ref, recv_ref, out_ref, *tail_refs):
    total = mine_ref[...] + recv_ref[...]
    out_ref[...] = total
    for ref in tail_refs:
        ref[...] = total[total.shape[0] - ref.shape[0] :]


def key_kernel(scale, share, order, *refs):
    total_ref, sums_ref, sib_ref, tok_ref, new_ref, old_ref, vec_ref, grad_ref, coef_ref = refs[:9]
    *outs, up_ref, mid_ref = refs[9:]
    dim = tok_ref.shape[-1]
    half = dim // 2
    down_sums = sums_ref[...] + sib_ref[...]
    pieces = ((0, dim, 0), (dim, dim, 1), (2 * dim, half, 2), (2 * dim + half, half, 3))
    upper, carried = [], []
    for row, rows, slot in pieces:
        adj = total_ref[row : row + rows, :]
        new = new_ref[row : row + rows, :]
        if slot < 2:
            sums = jnp.sum(new * adj, axis=0, keepdims=True)
        else:
            sums = down_sums[slot - 2 : slot - 1]
        ratio = vec_ref[slot : slot + 1, :]
        cross = vec_ref[4 + slot : 5 + slot, :]
        inverse = vec_ref[8 + slot : 9 + slot, :]
        up_adj = adj * ratio - new * (sums * cross)
        direct = old_ref[row : row + rows, :] * (sums * inverse)
        upper.append(up_adj * scale)
        carried.append((up_adj + direct) * share + grad_ref[row : row + rows, :])
        up_ref[row : row + rows, :] = upper[-1]
    key, value = tok_ref[0], tok_ref[1]
    raw = exact_left(key, split(jnp.concatenate(upper[:2], axis=1)), NN)
    back = exact_left(value, split(jnp.concatenate(upper[2:], axis=1)), NT)
    gate, up = raw[:, :half], raw[:, half:]
    hidden = coef_ref[0] * gate + coef_ref[1] * up
    d_gate = coef_ref[2] * gate + coef_ref[3] * up + coef_ref[0] * back
    d_up = coef_ref[3] * gate + coef_ref[1] * back
    d_gate_up = exact_left(key, split(jnp.concatenate([d_gate, d_up], axis=1)), TN)
    d_down = exact_right(split(hidden), value, TN)
    mid_ref[0] = d_gate
    mid_ref[1] = d_up
    mid_ref[2] = hidden
    results = [
        d_gate_up[:, :half] + carried[0],
        d_gate_up[:, half:] + carried[1],
        d_down[:, :half] + carried[2],
        d_down[:, half:] + carried[3],
    ]
    if order is None:
        (out_ref,) = outs
        out_ref[3 * dim :, :] = jnp.zeros((PAD, half), F32)
        for (row, rows, slot), value in zip(pieces, results):
            out_ref[row : row + rows, :] = value
            if slot >= 2:
                out_ref[3 * dim + slot - 2 : 3 * dim + slot - 1, :] = jnp.sum(
                    value * old_ref[row : row + rows, :], axis=0, keepdims=True
                )
    else:
        halves = [[results[0][:half], results[1][:half], results[2]]]
        halves.append([results[0][half:], results[1][half:], results[3]])
        store_halves(halves, order, *outs)


def store_halves(halves, order, keep_ref, send_ref):
    bit = bit_of(order)

    def put(kept, sent):
        for index in range(3):
            keep_ref[index] = kept[index]
            send_ref[index] = sent[index]

    pl.when(bit)(functools.partial(put, halves[1], halves[0]))
    pl.when(jnp.logical_not(bit))(functools.partial(put, halves[0], halves[1]))


def halve_kernel(order, mine_ref, recv_ref, *outs):
    total = mine_ref[...] + recv_ref[...]
    if order is None:
        outs[0][...] = total
        return
    size = total.shape[1] // 2
    halves = [[total[m, at * size : (at + 1) * size] for m in range(3)] for at in range(2)]
    store_halves(halves, order, *outs)


def pair_kernel(mine_ref, other_ref, out_ref):
    out_ref[0] = mine_ref[...]
    out_ref[1] = other_ref[...]


def choose_kernel(tok_count, own_ref, moved_ref, out_ref):
    stays = working(tok_count)

    def put(source):
        out_ref[...] = source[...]

    pl.when(stays)(functools.partial(put, own_ref))
    pl.when(jnp.logical_not(stays))(functools.partial(put, moved_ref))


def init_out_kernel(tok_count, rs_orders, ag_orders, mine_ref, recv_ref, out_ref):
    dim = out_ref.shape[-1]
    half = dim // 2
    blocks = mine_ref.shape[0]
    size = mine_ref.shape[3]
    steps = len(ag_orders[0])
    stays = working(tok_count)
    for core in range(2):

        @pl.when(lax.axis_index("head") % 2 == core)
        def _():
            for flipped in range(2 * blocks):
                source = mine_ref if flipped < blocks else recv_ref
                where = flipped % blocks
                for slot in range(2):
                    which = core if slot == 0 else 1 - core
                    offset, first = 0, None
                    for at, (axis, mask) in enumerate(rs_orders[which]):
                        bit = (lax.axis_index(axis) // mask) % 2
                        step = ag_orders[core].index((axis, mask))
                        if (flipped >> step) & 1:
                            bit = 1 - bit
                        if at == 0:
                            first = bit
                        else:
                            offset = offset + bit * (dim >> (at + 1))
                    offset = pl.multiple_of(offset, size)
                    low = first * half + offset
                    for index in range(2):
                        out_ref[index, pl.ds(pl.multiple_of(low, size), size), which * half : (which + 1) * half] = (
                            source[where, slot, index]
                        )
                    rows = pl.ds(pl.multiple_of(which * half + offset, size), size)
                    pl.when(first == 0)(functools.partial(put_block, out_ref, rows, slice(0, half), source, where, slot))
                    pl.when(first == 1)(functools.partial(put_block, out_ref, rows, slice(half, dim), source, where, slot))


def put_block(out_ref, rows, lanes, source, where, slot):
    out_ref[2, rows, lanes] = source[where, slot, 2]


def token_kernel(tok_count, mid_ref, coef_ref, w_ref, up_ref, keep_ref, give_ref):
    dim = keep_ref.shape[-1]
    count = keep_ref.shape[1]
    w_gate_up, w_down = load_half(w_ref[...], dim)
    u_gate_up, u_down = load_half(up_ref[...], dim)
    left = jnp.concatenate([mid_ref[0], mid_ref[1]], axis=1)
    d_key = both_split(split(left), split(w_gate_up), NT)
    left = jnp.concatenate([coef_ref[4], coef_ref[5]], axis=1)
    d_key = d_key + both_split(split(left), split(u_gate_up), NT)
    left = jnp.concatenate([mid_ref[2], coef_ref[6]], axis=1)
    right = jnp.concatenate([w_down, u_down], axis=0)
    d_value = both_split(split(left), split(right), NN)

    def put(first, second):
        for index, value in enumerate((d_key, d_value)):
            first[index] = value[:count]
            second[index] = value[count:]

    stays = working(tok_count)
    pl.when(stays)(functools.partial(put, keep_ref, give_ref))
    pl.when(jnp.logical_not(stays))(functools.partial(put, give_ref, keep_ref))


def tokens_out_kernel(tok_count, *refs):
    key_ref, value_ref = refs[-2:]
    stays = working(tok_count)
    ins = refs[:-2]
    groups = len(ins) // 2
    for index in range(groups):

        def put(source):
            key_ref[index] = source[0].astype(key_ref.dtype)
            value_ref[index] = source[1].astype(value_ref.dtype)

        pl.when(stays)(functools.partial(put, ins[2 * index]))
        pl.when(jnp.logical_not(stays))(functools.partial(put, ins[2 * index + 1]))
    key_ref[groups] = jnp.zeros_like(key_ref[groups])
    value_ref[groups] = jnp.zeros_like(value_ref[groups])


def call(kernel, outs, *args, scratch=(), limit=16, **kwargs):
    return pl.pallas_call(
        kernel,
        out_shape=outs,
        **kwargs,
        scratch_shapes=scratch,
        cost_estimate=pl.CostEstimate(flops=1, bytes_accessed=1, transcendentals=0),
        compiler_params=pltpu.CompilerParams(vmem_limit_bytes=limit * 1024 * 1024),
    )(*args)


def shape(*dims, dtype=F32):
    return jax.ShapeDtypeStruct(dims, dtype)


def tie(array, after):
    return lax.optimization_barrier((array, after))[0]


def working(tok_count):
    return lax.axis_index("tok") // (tok_count // 2) == lax.axis_index("head") % 2


def bit_of(order):
    bits = [(lax.axis_index(axis) // mask) % 2 for axis, mask in order]
    return jnp.where(lax.axis_index("head") % 2 == 0, bits[0], bits[1]) == 1


def on_device(queries, keys, values, out_grad, fast_init, updates):
    tok_count = lax.axis_size("tok")
    head_count = lax.axis_size("head")
    vid_count = lax.axis_size("vid")
    _, groups, count, _, dim = queries.shape
    half = dim // 2
    rows = 3 * dim
    scale = float(count * tok_count) ** (-0.5)
    share = 2.0 / tok_count
    tok_dims = [("tok", 1 << i) for i in range((tok_count // 2).bit_length() - 1)]
    vid_dims = [("vid", 1 << i) for i in range(vid_count.bit_length() - 1)]
    assert len(tok_dims) >= 1 and 2 << len(tok_dims) == tok_count
    assert 1 << len(vid_dims) == vid_count and head_count % 2 == 0
    assert queries.shape[0] == 1 and queries.shape[3] == 1

    def stays_at(tok, head):
        return tok // (tok_count // 2) == head % 2

    def permute(array, goes):
        pairs = []
        for tok in range(tok_count):
            for head in range(head_count):
                for vid in range(vid_count):
                    there = goes(tok, head, vid)
                    if there is not None:
                        number = lambda t, h, v: (t * head_count + h) * vid_count + v
                        pairs.append((number(tok, head, vid), number(*there)))
        return lax.ppermute(array, ("tok", "head", "vid"), pairs)

    def meet(array, order):
        def goes(tok, head, vid):
            axis, mask = order[head % 2]
            return (tok ^ mask, head, vid) if axis == "tok" else (tok, head, vid ^ mask)

        return permute(array, goes)

    def sibling(array, from_staying=None):
        def goes(tok, head, vid):
            if from_staying is None or stays_at(tok, head) == from_staying:
                return (tok, head ^ 1, vid)

        return permute(array, goes)

    def spread(array):
        def goes(tok, head, vid):
            if stays_at(tok, head):
                return (tok, head ^ 1, vid)
            return (tok ^ (tok_count // 2), head, vid)

        return permute(array, goes)

    def swap(array):
        def goes(tok, head, vid):
            if not stays_at(tok, head):
                return (tok ^ (tok_count // 2), head ^ 1, vid)

        return permute(array, goes)

    def lend(array):
        def goes(tok, head, vid):
            if stays_at(tok, head):
                return (tok ^ (tok_count // 2), head, vid)

        return permute(array, goes)

    flat = lambda array: array.reshape(groups, count, dim)
    q_all, k_all, v_all, c_all = (flat(a) for a in (queries, keys, values, out_grad))
    top = groups - 1
    init = fast_init.reshape(3, dim, dim)
    steps = updates.reshape(groups - 1, 3, dim, dim)

    def send(arrays, index, limit=16):
        return call(
            functools.partial(send_kernel, index, len(arrays)),
            [shape(2, count, dim)] * (len(arrays) // 2),
            *arrays,
            limit=limit,
            in_specs=[pl.BlockSpec(memory_space=pltpu.HBM)] * len(arrays),
            scratch=[
                pltpu.VMEM((len(arrays), count, dim), BF16),
                pltpu.SemaphoreType.DMA((len(arrays),)),
            ],
        )

    own = {top: send([q_all, c_all], top, 60)}
    first = {top: [spread(own[top][0])]}
    init = tie(init, own[top][0])

    low_rows = top * rows + top * VEC
    low_rows += -low_rows % 8
    full, *halves = call(
        prep_kernel,
        [shape(top, 3, dim, dim)] + [shape(rows, half), shape(low_rows, half)] * 2,
        init,
        steps,
        in_specs=[pl.BlockSpec(memory_space=pltpu.HBM)] * 2,
        scratch=[
            pltpu.VMEM(init.shape, BF16),
            pltpu.VMEM(steps.shape, BF16),
            pltpu.SemaphoreType.DMA((groups,)),
        ],
    )

    def chosen(outs, mine, sent):
        return call(functools.partial(weights_kernel, tok_count), outs, mine, sibling(sent))

    (top_weights,) = chosen([shape(rows, half)], halves[0], halves[2])
    (query_grad,) = call(query_kernel, [shape(groups, count, dim, dtype=BF16)], q_all, c_all, init, full)

    def tokens(index, after):
        arrays = []
        for mine, arrived in zip(own[index], first[index]):
            arrays += [mine, arrived, sibling(tie(arrived, after), True)]
        return arrays

    def scratch(index):
        return [pltpu.VMEM((2 * len(own[index]), 2 * count, dim), BF16)]

    both = 2 * count
    (payload,) = call(
        functools.partial(last_kernel, tok_count),
        [shape(rows + PAD, half)],
        *tokens(top, query_grad),
        top_weights,
        scratch=scratch(top),
    )
    weights = chosen(
        [shape(rows, half)] * top + [shape(VEC, half)] * top, halves[1], tie(halves[3], first[top][0])
    )
    factors = list(weights[top:])
    weights = [*weights[:top], top_weights]
    token_grads = {}
    for index in reversed(range(top)):
        own[index] = send([q_all, c_all, k_all, v_all], index)
        first[index] = [spread(tie(array, first[index + 1])) for array in own[index]]
        for at in range(len(tok_dims)):
            arrived = meet(payload, (tok_dims[at], tok_dims[at - 1]))
            if at + 1 < len(tok_dims):
                (payload,) = call(add_kernel, [shape(rows + PAD, half)], payload, arrived)
        grad, coef, keyed = call(
            functools.partial(pre_kernel, tok_count),
            [shape(rows, half), shape(7, both, half), shape(2, both, dim, dtype=BF16)],
            *tokens(index, payload),
            weights[index],
            scratch=scratch(index),
        )
        total, sums = call(add_kernel, [shape(rows + PAD, half), shape(PAD, half)], payload, arrived)
        if index > 0:
            out_shapes, order = [shape(rows + PAD, half)], None
        else:
            dims = tok_dims[:1] + vid_dims + tok_dims[1:]
            rs_orders = [dims, dims[-1:] + dims[:-1]]
            order = [rs_orders[0][0], rs_orders[1][0]]
            out_shapes = [shape(3, half, half)] * 2
        *outs, upper, mid = call(
            functools.partial(key_kernel, scale, share, order),
            out_shapes + [shape(rows, half), shape(3, both, half)],
            total,
            sums,
            sibling(sums),
            keyed,
            weights[index + 1],
            weights[index],
            factors[index],
            grad,
            coef,
        )
        payload = outs[0]
        keep, give = call(
            functools.partial(token_kernel, tok_count),
            [shape(2, count, dim)] * 2,
            mid,
            coef,
            weights[index],
            upper,
        )
        (d_tokens,) = call(add_kernel, [shape(2, count, dim)], keep, sibling(give))
        token_grads[index] = d_tokens

    kept, sends = outs
    for at in range(len(dims)):
        arrived = meet(sends, [order[at] for order in rs_orders])
        if at + 1 < len(dims):
            out_shapes = [shape(3, kept.shape[1] // 2, half)] * 2
            order = [order[at + 1] for order in rs_orders]
            kept, sends = call(functools.partial(halve_kernel, order), out_shapes, kept, arrived)
        else:
            (kept,) = call(functools.partial(halve_kernel, None), [shape(*kept.shape)], kept, arrived)
    (pair,) = call(pair_kernel, [shape(2, *kept.shape)], kept, sibling(kept))
    (block,) = call(
        functools.partial(choose_kernel, tok_count), [shape(*pair.shape)], pair, lend(pair)
    )
    block = block[None]
    ag_orders = [order[::-1] for order in rs_orders]
    for at in range(len(dims)):
        arrived = meet(block, [order[at] for order in ag_orders])
        if at + 1 < len(dims):
            (pair,) = call(pair_kernel, [shape(2, *block.shape)], block, arrived)
            block = pair.reshape(2 * block.shape[0], *block.shape[1:])
    (init_grad,) = call(
        functools.partial(init_out_kernel, tok_count, rs_orders, ag_orders),
        [shape(3, dim, dim)],
        block,
        arrived,
    )
    arrays = []
    for index in range(top):
        arrays += [token_grads[index], swap(token_grads[index])]
    key_grad, value_grad = call(
        functools.partial(tokens_out_kernel, tok_count),
        [shape(groups, count, dim, dtype=BF16)] * 2,
        *arrays,
    )
    back = lambda array: array.reshape(queries.shape)
    return back(query_grad), back(key_grad), back(value_grad), init_grad.reshape(fast_init.shape)


def solution(mesh):
    tokens = P("vid", None, "tok", "head", None)
    return jax.shard_map(
        on_device,
        mesh=mesh,
        in_specs=(
            tokens,
            tokens,
            tokens,
            tokens,
            P("head", None, None, None),
            P("vid", None, "head", None, None, None),
        ),
        out_specs=(tokens, tokens, tokens, P("head", None, None, None)),
        check_vma=False,
    )
```

time: 128 us -> 112 us (0.88)
  starting transfers between devices: 58.5 us -> 46.5 us
  waiting for transfers between devices: 41.5 us -> 49.4 us
  local copies, waits for them, and re-layouts: 9.38 us -> 2.15 us
  other arithmetic: 5.68 us -> 0 us
  Pallas kernels: 10.6 us -> 12.8 us
    ppermute x41 -> x30, starting transfers between devices: 58.5 us -> 46.5 us  [permute(): return lax.ppermute(array, ('tok', 'head', 'vid'), pairs)]
    ppermute x41 -> x30, waiting for transfers between devices: 41.5 us -> 49.4 us  [permute(): return lax.ppermute(array, ('tok', 'head', 'vid'), pairs)]
    unnamed x40 -> x14, local copies, waits for them, and re-layouts: 8.3 us -> 2.15 us
    add x13 -> x0, other arithmetic: 2.79 us -> none  [the longest x5 1.93 us: on_device(): pieces = [kept[j] + flip(sent[j], *orders[j][at]) for j in range(3)]]
    select_n x17 -> x0, other arithmetic: 2.65 us -> none  [the longest x1 1.41 us: on_device(): weights = jnp.where(stays, mine, flip(send, 'head', 1))]
    pallas_call x11 -> x29, Pallas kernels: 10.6 us -> 12.8 us  [call(): pl.pallas_call(kernel, out_shape=outs, **kwargs, scratch_shapes=scratch,...]
  transfers between devices with their start and end apart: 41 -> 30, of which waited for: 16 -> 15; matrix products, arithmetic and copies ran while one was open for 4% -> 0% of each run, Pallas kernels for 5% -> 8%
where the time goes in v2:
time: 112 us
  waiting for transfers between devices  49.4 us (44%)
  starting transfers between devices  46.5 us (42%)
  Pallas kernels  12.8 us (11%)
  local copies, waits for them, and re-layouts  2.15 us (2%)
    ppermute x30, waiting for transfers between devices, permute(): return lax.ppermute(array, ('tok', 'head', 'vid'), pairs)  49.4 us
    ppermute x30, starting transfers between devices, permute(): return lax.ppermute(array, ('tok', 'head', 'vid'), pairs)  46.5 us
    pallas_call x29, Pallas kernels, call(): pl.pallas_call(kernel, out_shape=outs, **kwargs, scratch_shapes=scratch,...  12.8 us
  transfers between devices with their start and end apart: 30, of which 15 were waited for; matrix products, arithmetic and copies ran while one was open for 0% of the time, Pallas kernels for 8%

profile of v2, /device:TPU:1, one launch (start us, length us, event | category | flops | bytes accessed | tf_op | source)
XLA Modules:
  0.0 111.9 jit_solution(6112983608987460211)
XLA Ops:
  0.7 1.7 %shard_map.93.refs_0_ = f32[2,128,256]{2,1,0:T(8,128)} custom-call(bf16[3,128,256]{2,1,0:T(8,128)(2,1)} %bitcast.19, bf16[3,128,256]{2,1,0:T(8,128)(2,1)} %bitcast.23), custom_call_target="tpu_custom_call" | custom-call | flops 1 | bytes 1 | tf_op jit(solution)/shard_map/pallas_call | solution.py:440
  2.3 3.2 %collective-permute-start = (f32[2,128,256]{2,1,0:T(8,128)}, f32[2,128,256]{2,1,0:T(8,128)S(1)}, u32[]{:S(2)}, u32[]{:S(2)}) collective-permute-start(f32[2,128,256]{2,1,0:T(8,128)} %shard_map.93.refs_0_), channel_id=1, source_target_pairs={{0,2},{1,3},{2,18},{3,19},{4,6},{5,7},{6,22},{7,23},{8,10},{9,11},... | collective-permute-start | bytes 786440 | tf_op jit(solution)/shard_map/ppermute | solution.py:494
  7.6 1.3 %shard_map.94 = (f32[2,3,256,256]{3,2,1,0:T(8,128)S(1)}, f32[768,128]{1,0:T(8,128)S(1)}, f32[1560,128]{1,0:T(8,128)S(1)}, f32[768,128]{1,0:T(8,128)S(1)}, f32[1560,128]{1,0:T(8,128)S(1)}) custom-call(bf16[3,256,256]{2,1,0:T(8,128)(2,1)S(1)} %bitcast.27, bf16[2,3,256,256]{3,2,1,0:T(8,128)(2,1)S(1)} %bitcast.31), custom_call_target="tpu_custom_call" | custom-call | flops 1 | bytes 1 | tf_op jit(solution)/shard_map/pallas_call | solution.py:440
  9.1 1.9 %shard_map.95 = bf16[3,128,256]{2,1,0:T(8,128)(2,1)} custom-call(bf16[3,128,256]{2,1,0:T(8,128)(2,1)S(1)} %bitcast.20, bf16[3,128,256]{2,1,0:T(8,128)(2,1)S(1)} %bitcast.24, bf16[3,256,256]{2,1,0:T(8,128)(2,1)S(1)} %bitcast.28, f32[2,3,256,256]{3,2,1,0:T(8,128)S(1)} %get-tuple-element.56.full_ref), custom_call_target="tpu_custom_call" | custom-call | flops 1 | bytes 1 | tf_op jit(solution)/shard_map/pallas_call | solution.py:440
  11.0 1.4 %collective-permute-start.1 = (f32[2,128,256]{2,1,0:T(8,128)S(1)}, f32[2,128,256]{2,1,0:T(8,128)S(1)}, u32[]{:S(2)}, u32[]{:S(2)}) collective-permute-start(f32[2,128,256]{2,1,0:T(8,128)S(1)} %collective-permute-done.refs_1_), channel_id=1, source_target_pairs={{0,2},{1,3},{4,6},{5,7},{8,10},{9,11},{12,14},{13,15},{18,16},{19,... | collective-permute-start | bytes 786440 | tf_op jit(solution)/shard_map/ppermute | solution.py:494
  12.5 2.8 %collective-permute-start.10 = (f32[1560,128]{1,0:T(8,128)S(1)}, f32[1560,128]{1,0:T(8,128)S(1)}, u32[]{:S(2)}, u32[]{:S(2)}) collective-permute-start(f32[1560,128]{1,0:T(8,128)S(1)} %get-tuple-element.70), channel_id=1, source_target_pairs={{0,2},{1,3},{2,0},{3,1},{4,6},{5,7},{6,4},{7,5},{8,10},{9,11},{10,... | collective-permute-start | bytes 2396168 | tf_op jit(solution)/shard_map/ppermute | solution.py:494
  17.7 1.8 %collective-permute-start.6 = (f32[2,128,256]{2,1,0:T(8,128)S(1)}, f32[2,128,256]{2,1,0:T(8,128)S(1)}, u32[]{:S(2)}, u32[]{:S(2)}) collective-permute-start(f32[2,128,256]{2,1,0:T(8,128)S(1)} %get-tuple-element.63.refs_0_), channel_id=1, source_target_pairs={{0,2},{1,3},{2,18},{3,19},{4,6},{5,7},{6,22},{7,23},{8,10},{9,11},... | collective-permute-start | bytes 786440 | tf_op jit(solution)/shard_map/ppermute | solution.py:494
  19.6 4.6 %collective-permute-done.3.recv_ref = f32[776,128]{1,0:T(8,128)S(1)} collective-permute-done((f32[776,128]{1,0:T(8,128)S(1)}, f32[776,128]{1,0:T(8,128)S(1)}, u32[]{:S(2)}, u32[]{:S(2)}) %collective-permute-start.3) | collective-permute-done | bytes 397344 | tf_op jit(solution)/shard_map/ppermute | solution.py:494
  24.3 3.4 %collective-permute-start.4 = (f32[776,128]{1,0:T(8,128)S(1)}, f32[776,128]{1,0:T(8,128)S(1)}, u32[]{:S(2)}, u32[]{:S(2)}) collective-permute-start(f32[776,128]{1,0:T(8,128)S(1)} %shard_map.98.mine_ref), channel_id=1, source_target_pairs={{0,8},{1,9},{2,6},{3,7},{4,12},{5,13},{6,2},{7,3},{8,0},{9,1},{10,... | collective-permute-start | bytes 1191944 | tf_op jit(solution)/shard_map/ppermute | solution.py:494
  27.7 1.3 %collective-permute-start.7 = (f32[2,128,256]{2,1,0:T(8,128)S(1)}, f32[2,128,256]{2,1,0:T(8,128)S(1)}, u32[]{:S(2)}, u32[]{:S(2)}) collective-permute-start(f32[2,128,256]{2,1,0:T(8,128)S(1)} %collective-permute-done.6.refs_1_), channel_id=1, source_target_pairs={{0,2},{1,3},{4,6},{5,7},{8,10},{9,11},{12,14},{13,15},{18,16},{19,... | collective-permute-start | bytes 786440 | tf_op jit(solution)/shard_map/ppermute | solution.py:494
  29.0 1.3 %collective-permute-start.9 = (f32[2,128,256]{2,1,0:T(8,128)S(1)}, f32[2,128,256]{2,1,0:T(8,128)S(1)}, u32[]{:S(2)}, u32[]{:S(2)}) collective-permute-start(f32[2,128,256]{2,1,0:T(8,128)S(1)} %collective-permute-done.8.refs_4_), channel_id=1, source_target_pairs={{0,2},{1,3},{4,6},{5,7},{8,10},{9,11},{12,14},{13,15},{18,16},{19,... | collective-permute-start | bytes 786440 | tf_op jit(solution)/shard_map/ppermute | solution.py:494
  30.3 2.9 %collective-permute-done.4.recv_ref = f32[776,128]{1,0:T(8,128)S(1)} collective-permute-done((f32[776,128]{1,0:T(8,128)S(1)}, f32[776,128]{1,0:T(8,128)S(1)}, u32[]{:S(2)}, u32[]{:S(2)}) %collective-permute-start.4) | collective-permute-done | bytes 397344 | tf_op jit(solution)/shard_map/ppermute | solution.py:494
  33.3 4.2 %collective-permute-start.5 = (f32[8,128]{1,0:T(8,128)S(1)}, f32[8,128]{1,0:T(8,128)S(1)}, u32[]{:S(2)}, u32[]{:S(2)}) collective-permute-start(f32[8,128]{1,0:T(8,128)S(1)} %get-tuple-element.61.refs_1_), channel_id=1, source_target_pairs={{0,2},{1,3},{2,0},{3,1},{4,6},{5,7},{6,4},{7,5},{8,10},{9,11},{10,... | collective-permute-start | bytes 12296 | tf_op jit(solution)/shard_map/ppermute | solution.py:494
  39.9 7.7 %collective-permute-done.11.recv_ref = f32[776,128]{1,0:T(8,128)S(1)} collective-permute-done((f32[776,128]{1,0:T(8,128)S(1)}, f32[776,128]{1,0:T(8,128)S(1)}, u32[]{:S(2)}, u32[]{:S(2)}) %collective-permute-start.11) | collective-permute-done | bytes 397344 | tf_op jit(solution)/shard_map/ppermute | solution.py:494
  47.8 1.3 %collective-permute-start.17 = (f32[2,128,256]{2,1,0:T(8,128)S(1)}, f32[2,128,256]{2,1,0:T(8,128)S(1)}, u32[]{:S(2)}, u32[]{:S(2)}) collective-permute-start(f32[2,128,256]{2,1,0:T(8,128)S(1)} %collective-permute-done.16.refs_4_), channel_id=1, source_target_pairs={{0,2},{1,3},{4,6},{5,7},{8,10},{9,11},{12,14},{13,15},{18,16},{19,... | collective-permute-start | bytes 786440 | tf_op jit(solution)/shard_map/ppermute | solution.py:494
  49.1 2.0 %collective-permute-done.14.refs_1_ = f32[2,128,256]{2,1,0:T(8,128)S(1)} collective-permute-done((f32[2,128,256]{2,1,0:T(8,128)S(1)}, f32[2,128,256]{2,1,0:T(8,128)S(1)}, u32[]{:S(2)}, u32[]{:S(2)}) %collective-permute-start.14) | collective-permute-done | bytes 262176 | tf_op jit(solution)/shard_map/ppermute | solution.py:494
  52.4 2.4 %collective-permute-done.12.recv_ref = f32[776,128]{1,0:T(8,128)S(1)} collective-permute-done((f32[776,128]{1,0:T(8,128)S(1)}, f32[776,128]{1,0:T(8,128)S(1)}, u32[]{:S(2)}, u32[]{:S(2)}) %collective-permute-start.12) | collective-permute-done | bytes 397344 | tf_op jit(solution)/shard_map/ppermute | solution.py:494
  54.8 4.5 %collective-permute-start.13 = (f32[8,128]{1,0:T(8,128)S(1)}, f32[8,128]{1,0:T(8,128)S(1)}, u32[]{:S(2)}, u32[]{:S(2)}) collective-permute-start(f32[8,128]{1,0:T(8,128)S(1)} %get-tuple-element.78.refs_1_), channel_id=1, source_target_pairs={{0,2},{1,3},{2,0},{3,1},{4,6},{5,7},{6,4},{7,5},{8,10},{9,11},{10,... | collective-permute-start | bytes 12296 | tf_op jit(solution)/shard_map/ppermute | solution.py:494
  60.9 4.8 %collective-permute-done.22.recv_ref = f32[3,128,128]{2,1,0:T(8,128)S(1)} collective-permute-done((f32[3,128,128]{2,1,0:T(8,128)S(1)}, f32[3,128,128]{2,1,0:T(8,128)S(1)}, u32[]{:S(2)}, u32[]{:S(2)}) %collective-permute-start.22) | collective-permute-done | bytes 196640 | tf_op jit(solution)/shard_map/ppermute | solution.py:494
  65.8 1.3 %collective-permute-start.23 = (f32[3,64,128]{2,1,0:T(8,128)S(1)}, f32[3,64,128]{2,1,0:T(8,128)S(1)}, u32[]{:S(2)}, u32[]{:S(2)}) collective-permute-start(f32[3,64,128]{2,1,0:T(8,128)S(1)} %get-tuple-element.103), channel_id=1, source_target_pairs={{0,1},{1,0},{2,6},{3,7},{4,5},{5,4},{6,2},{7,3},{8,9},{9,8},{10,14... | collective-permute-start | bytes 294920 | tf_op jit(solution)/shard_map/ppermute | solution.py:494
  67.1 2.2 %collective-permute-done.23.recv_ref = f32[3,64,128]{2,1,0:T(8,128)S(1)} collective-permute-done((f32[3,64,128]{2,1,0:T(8,128)S(1)}, f32[3,64,128]{2,1,0:T(8,128)S(1)}, u32[]{:S(2)}, u32[]{:S(2)}) %collective-permute-start.23) | collective-permute-done | bytes 98336 | tf_op jit(solution)/shard_map/ppermute | solution.py:494
  69.3 1.9 %collective-permute-start.24 = (f32[3,32,128]{2,1,0:T(8,128)S(1)}, f32[3,32,128]{2,1,0:T(8,128)S(1)}, u32[]{:S(2)}, u32[]{:S(2)}) collective-permute-start(f32[3,32,128]{2,1,0:T(8,128)S(1)} %get-tuple-element.105), channel_id=1, source_target_pairs={{0,8},{1,9},{2,3},{3,2},{4,12},{5,13},{6,7},{7,6},{8,0},{9,1},{10,... | collective-permute-start | bytes 147464 | tf_op jit(solution)/shard_map/ppermute | solution.py:494
  71.2 1.5 %collective-permute-done.24.recv_ref = f32[3,32,128]{2,1,0:T(8,128)S(1)} collective-permute-done((f32[3,32,128]{2,1,0:T(8,128)S(1)}, f32[3,32,128]{2,1,0:T(8,128)S(1)}, u32[]{:S(2)}, u32[]{:S(2)}) %collective-permute-start.24) | collective-permute-done | bytes 49184 | tf_op jit(solution)/shard_map/ppermute | solution.py:494
  72.7 3.3 %collective-permute-start.25 = (f32[3,32,128]{2,1,0:T(8,128)S(1)}, f32[3,32,128]{2,1,0:T(8,128)S(1)}, u32[]{:S(2)}, u32[]{:S(2)}) collective-permute-start(f32[3,32,128]{2,1,0:T(8,128)S(1)} %shard_map.116.mine_ref), channel_id=1, source_target_pairs={{0,2},{1,3},{2,0},{3,1},{4,6},{5,7},{6,4},{7,5},{8,10},{9,11},{10,... | collective-permute-start | bytes 147464 | tf_op jit(solution)/shard_map/ppermute | solution.py:494
  78.2 5.5 %collective-permute-done.26.moved_ref = f32[2,3,32,128]{3,2,1,0:T(8,128)S(1)} collective-permute-done((f32[2,3,32,128]{3,2,1,0:T(8,128)S(1)}, f32[2,3,32,128]{3,2,1,0:T(8,128)S(1)}, u32[]{:S(2)}, u32[]{:S(2)}) %collective-permute-start.26) | collective-permute-done | bytes 98336 | tf_op jit(solution)/shard_map/ppermute | solution.py:494
  83.6 1.8 %collective-permute-start.27 = (f32[1,2,3,32,128]{4,3,2,1,0:T(8,128)S(1)}, f32[1,2,3,32,128]{4,3,2,1,0:T(8,128)S(1)}, u32[]{:S(2)}, u32[]{:S(2)}) collective-permute-start(f32[1,2,3,32,128]{4,3,2,1,0:T(8,128)S(1)} %bitcast.38), channel_id=1, source_target_pairs={{0,8},{1,9},{2,3},{3,2},{4,12},{5,13},{6,7},{7,6},{8,0},{9,1},{10,... | collective-permute-start | bytes 294920 | tf_op jit(solution)/shard_map/ppermute | solution.py:494
  85.4 2.0 %collective-permute-done.27.other_ref = f32[1,2,3,32,128]{4,3,2,1,0:T(8,128)S(1)} collective-permute-done((f32[1,2,3,32,128]{4,3,2,1,0:T(8,128)S(1)}, f32[1,2,3,32,128]{4,3,2,1,0:T(8,128)S(1)}, u32[]{:S(2)}, u32[]{:S(2)}) %collective-permute-start.27) | collective-permute-done | bytes 98336 | tf_op jit(solution)/shard_map/ppermute | solution.py:494
  90.5 1.6 %collective-permute-done.28.other_ref = f32[2,2,3,32,128]{4,3,2,1,0:T(8,128)S(1)} collective-permute-done((f32[2,2,3,32,128]{4,3,2,1,0:T(8,128)S(1)}, f32[2,2,3,32,128]{4,3,2,1,0:T(8,128)S(1)}, u32[]{:S(2)}, u32[]{:S(2)}) %collective-permute-start.28) | collective-permute-done | bytes 196640 | tf_op jit(solution)/shard_map/ppermute | solution.py:494
  92.2 5.4 %collective-permute-start.21 = (f32[2,128,256]{2,1,0:T(8,128)S(1)}, f32[2,128,256]{2,1,0:T(8,128)S(1)}, u32[]{:S(2)}, u32[]{:S(2)}) collective-permute-start(f32[2,128,256]{2,1,0:T(8,128)S(1)} %shard_map.112.refs_2_), channel_id=1, source_target_pairs={{2,16},{3,17},{6,20},{7,21},{10,24},{11,25},{14,28},{15,29},{16,2}... | collective-permute-start | bytes 786440 | tf_op jit(solution)/shard_map/ppermute | solution.py:494
  97.7 1.9 %collective-permute-start.19 = (f32[2,128,256]{2,1,0:T(8,128)S(1)}, f32[2,128,256]{2,1,0:T(8,128)S(1)}, u32[]{:S(2)}, u32[]{:S(2)}) collective-permute-start(f32[2,128,256]{2,1,0:T(8,128)S(1)} %shard_map.110.refs_0_), channel_id=1, source_target_pairs={{2,16},{3,17},{6,20},{7,21},{10,24},{11,25},{14,28},{15,29},{16,2}... | collective-permute-start | bytes 786440 | tf_op jit(solution)/shard_map/ppermute | solution.py:494
  99.6 7.7 %collective-permute-done.21.refs_3_ = f32[2,128,256]{2,1,0:T(8,128)S(1)} collective-permute-done((f32[2,128,256]{2,1,0:T(8,128)S(1)}, f32[2,128,256]{2,1,0:T(8,128)S(1)}, u32[]{:S(2)}, u32[]{:S(2)}) %collective-permute-start.21) | collective-permute-done | bytes 262176 | tf_op jit(solution)/shard_map/ppermute | solution.py:494
  107.3 2.8 %collective-permute-done.19.refs_1_ = f32[2,128,256]{2,1,0:T(8,128)S(1)} collective-permute-done((f32[2,128,256]{2,1,0:T(8,128)S(1)}, f32[2,128,256]{2,1,0:T(8,128)S(1)}, u32[]{:S(2)}, u32[]{:S(2)}) %collective-permute-start.19) | collective-permute-done | bytes 262176 | tf_op jit(solution)/shard_map/ppermute | solution.py:494
  (71 shorter events, 17.7 us)
Async XLA Ops:
  0.6 8.4 %copy-start = (bf16[1,3,128,1,256]{4,2,3,1,0:T(8,128)(2,1)S(1)}, bf16[1,3,128,1,256]{4,2,3,1,0:T(8,128)(2,1)}, u32[]{:S(2)}) copy-start(bf16[1,3,128,1,256]{4,2,3,1,0:T(8,128)(2,1)} %param.6) | copy-start | bytes 589828
  0.6 8.4 %copy-start.1 = (bf16[1,3,128,1,256]{4,2,3,1,0:T(8,128)(2,1)S(1)}, bf16[1,3,128,1,256]{4,2,3,1,0:T(8,128)(2,1)}, u32[]{:S(2)}) copy-start(bf16[1,3,128,1,256]{4,2,3,1,0:T(8,128)(2,1)} %param.9) | copy-start | bytes 589828
  2.3 8.7 %collective-permute-start = (f32[2,128,256]{2,1,0:T(8,128)}, f32[2,128,256]{2,1,0:T(8,128)S(1)}, u32[]{:S(2)}, u32[]{:S(2)}) collective-permute-start(f32[2,128,256]{2,1,0:T(8,128)} %shard_map.93.refs_0_), channel_id=1, source_target_pairs={{0,2},{1,3},{2,18},{3,19},{4,6},{5,7},{6,22},{7,23},{8,10},{9,11},... | collective-permute-start | bytes 786440 | tf_op jit(solution)/shard_map/ppermute | solution.py:494
  9.0 6.2 %collective-permute-start.2 = (f32[768,128]{1,0:T(8,128)S(1)}, f32[768,128]{1,0:T(8,128)S(1)}, u32[]{:S(2)}, u32[]{:S(2)}) collective-permute-start(f32[768,128]{1,0:T(8,128)S(1)} %get-tuple-element.59), channel_id=1, source_target_pairs={{0,2},{1,3},{2,0},{3,1},{4,6},{5,7},{6,4},{7,5},{8,10},{9,11},{10,... | collective-permute-start | bytes 1179656 | tf_op jit(solution)/shard_map/ppermute | solution.py:494
  11.0 5.1 %collective-permute-start.1 = (f32[2,128,256]{2,1,0:T(8,128)S(1)}, f32[2,128,256]{2,1,0:T(8,128)S(1)}, u32[]{:S(2)}, u32[]{:S(2)}) collective-permute-start(f32[2,128,256]{2,1,0:T(8,128)S(1)} %collective-permute-done.refs_1_), channel_id=1, source_target_pairs={{0,2},{1,3},{4,6},{5,7},{8,10},{9,11},{12,14},{13,15},{18,16},{19,... | collective-permute-start | bytes 786440 | tf_op jit(solution)/shard_map/ppermute | solution.py:494
  12.5 25.0 %collective-permute-start.10 = (f32[1560,128]{1,0:T(8,128)S(1)}, f32[1560,128]{1,0:T(8,128)S(1)}, u32[]{:S(2)}, u32[]{:S(2)}) collective-permute-start(f32[1560,128]{1,0:T(8,128)S(1)} %get-tuple-element.70), channel_id=1, source_target_pairs={{0,2},{1,3},{2,0},{3,1},{4,6},{5,7},{6,4},{7,5},{8,10},{9,11},{10,... | collective-permute-start | bytes 2396168 | tf_op jit(solution)/shard_map/ppermute | solution.py:494
  16.8 7.5 %collective-permute-start.3 = (f32[776,128]{1,0:T(8,128)S(1)}, f32[776,128]{1,0:T(8,128)S(1)}, u32[]{:S(2)}, u32[]{:S(2)}) collective-permute-start(f32[776,128]{1,0:T(8,128)S(1)} %shard_map.97.mine_ref), channel_id=1, source_target_pairs={{0,4},{1,5},{2,10},{3,11},{4,0},{5,1},{6,14},{7,15},{8,12},{9,13},... | collective-permute-start | bytes 1191944 | tf_op jit(solution)/shard_map/ppermute | solution.py:494
  17.7 10.0 %collective-permute-start.6 = (f32[2,128,256]{2,1,0:T(8,128)S(1)}, f32[2,128,256]{2,1,0:T(8,128)S(1)}, u32[]{:S(2)}, u32[]{:S(2)}) collective-permute-start(f32[2,128,256]{2,1,0:T(8,128)S(1)} %get-tuple-element.63.refs_0_), channel_id=1, source_target_pairs={{0,2},{1,3},{2,18},{3,19},{4,6},{5,7},{6,22},{7,23},{8,10},{9,11},... | collective-permute-start | bytes 786440 | tf_op jit(solution)/shard_map/ppermute | solution.py:494
  19.5 9.6 %collective-permute-start.8 = (f32[2,128,256]{2,1,0:T(8,128)S(1)}, f32[2,128,256]{2,1,0:T(8,128)S(1)}, u32[]{:S(2)}, u32[]{:S(2)}) collective-permute-start(f32[2,128,256]{2,1,0:T(8,128)S(1)} %get-tuple-element.66.refs_3_), channel_id=1, source_target_pairs={{0,2},{1,3},{2,18},{3,19},{4,6},{5,7},{6,22},{7,23},{8,10},{9,11},... | collective-permute-start | bytes 786440 | tf_op jit(solution)/shard_map/ppermute | solution.py:494
  24.3 8.9 %collective-permute-start.4 = (f32[776,128]{1,0:T(8,128)S(1)}, f32[776,128]{1,0:T(8,128)S(1)}, u32[]{:S(2)}, u32[]{:S(2)}) collective-permute-start(f32[776,128]{1,0:T(8,128)S(1)} %shard_map.98.mine_ref), channel_id=1, source_target_pairs={{0,8},{1,9},{2,6},{3,7},{4,12},{5,13},{6,2},{7,3},{8,0},{9,1},{10,... | collective-permute-start | bytes 1191944 | tf_op jit(solution)/shard_map/ppermute | solution.py:494
  27.7 9.8 %collective-permute-start.7 = (f32[2,128,256]{2,1,0:T(8,128)S(1)}, f32[2,128,256]{2,1,0:T(8,128)S(1)}, u32[]{:S(2)}, u32[]{:S(2)}) collective-permute-start(f32[2,128,256]{2,1,0:T(8,128)S(1)} %collective-permute-done.6.refs_1_), channel_id=1, source_target_pairs={{0,2},{1,3},{4,6},{5,7},{8,10},{9,11},{12,14},{13,15},{18,16},{19,... | collective-permute-start | bytes 786440 | tf_op jit(solution)/shard_map/ppermute | solution.py:494
  29.0 8.5 %collective-permute-start.9 = (f32[2,128,256]{2,1,0:T(8,128)S(1)}, f32[2,128,256]{2,1,0:T(8,128)S(1)}, u32[]{:S(2)}, u32[]{:S(2)}) collective-permute-start(f32[2,128,256]{2,1,0:T(8,128)S(1)} %collective-permute-done.8.refs_4_), channel_id=1, source_target_pairs={{0,2},{1,3},{4,6},{5,7},{8,10},{9,11},{12,14},{13,15},{18,16},{19,... | collective-permute-start | bytes 786440 | tf_op jit(solution)/shard_map/ppermute | solution.py:494
  33.3 5.1 %collective-permute-start.5 = (f32[8,128]{1,0:T(8,128)S(1)}, f32[8,128]{1,0:T(8,128)S(1)}, u32[]{:S(2)}, u32[]{:S(2)}) collective-permute-start(f32[8,128]{1,0:T(8,128)S(1)} %get-tuple-element.61.refs_1_), channel_id=1, source_target_pairs={{0,2},{1,3},{2,0},{3,1},{4,6},{5,7},{6,4},{7,5},{8,10},{9,11},{10,... | collective-permute-start | bytes 12296 | tf_op jit(solution)/shard_map/ppermute | solution.py:494
  39.1 8.6 %collective-permute-start.11 = (f32[776,128]{1,0:T(8,128)S(1)}, f32[776,128]{1,0:T(8,128)S(1)}, u32[]{:S(2)}, u32[]{:S(2)}) collective-permute-start(f32[776,128]{1,0:T(8,128)S(1)} %get-tuple-element.76.mine_ref), channel_id=1, source_target_pairs={{0,4},{1,5},{2,10},{3,11},{4,0},{5,1},{6,14},{7,15},{8,12},{9,13},... | collective-permute-start | bytes 1191944 | tf_op jit(solution)/shard_map/ppermute | solution.py:494
  39.6 8.2 %collective-permute-start.16 = (f32[2,128,256]{2,1,0:T(8,128)S(1)}, f32[2,128,256]{2,1,0:T(8,128)S(1)}, u32[]{:S(2)}, u32[]{:S(2)}) collective-permute-start(f32[2,128,256]{2,1,0:T(8,128)S(1)} %get-tuple-element.83.refs_3_), channel_id=1, source_target_pairs={{0,2},{1,3},{2,18},{3,19},{4,6},{5,7},{6,22},{7,23},{8,10},{9,11},... | collective-permute-start | bytes 786440 | tf_op jit(solution)/shard_map/ppermute | solution.py:494
  39.7 11.3 %collective-permute-start.14 = (f32[2,128,256]{2,1,0:T(8,128)S(1)}, f32[2,128,256]{2,1,0:T(8,128)S(1)}, u32[]{:S(2)}, u32[]{:S(2)}) collective-permute-start(f32[2,128,256]{2,1,0:T(8,128)S(1)} %get-tuple-element.80.refs_0_), channel_id=1, source_target_pairs={{0,2},{1,3},{2,18},{3,19},{4,6},{5,7},{6,22},{7,23},{8,10},{9,11},... | collective-permute-start | bytes 786440 | tf_op jit(solution)/shard_map/ppermute | solution.py:494
  47.7 7.0 %collective-permute-start.12 = (f32[776,128]{1,0:T(8,128)S(1)}, f32[776,128]{1,0:T(8,128)S(1)}, u32[]{:S(2)}, u32[]{:S(2)}) collective-permute-start(f32[776,128]{1,0:T(8,128)S(1)} %shard_map.104.mine_ref), channel_id=1, source_target_pairs={{0,8},{1,9},{2,6},{3,7},{4,12},{5,13},{6,2},{7,3},{8,0},{9,1},{10,... | collective-permute-start | bytes 1191944 | tf_op jit(solution)/shard_map/ppermute | solution.py:494
  47.8 11.5 %collective-permute-start.17 = (f32[2,128,256]{2,1,0:T(8,128)S(1)}, f32[2,128,256]{2,1,0:T(8,128)S(1)}, u32[]{:S(2)}, u32[]{:S(2)}) collective-permute-start(f32[2,128,256]{2,1,0:T(8,128)S(1)} %collective-permute-done.16.refs_4_), channel_id=1, source_target_pairs={{0,2},{1,3},{4,6},{5,7},{8,10},{9,11},{12,14},{13,15},{18,16},{19,... | collective-permute-start | bytes 786440 | tf_op jit(solution)/shard_map/ppermute | solution.py:494
  51.1 8.2 %collective-permute-start.15 = (f32[2,128,256]{2,1,0:T(8,128)S(1)}, f32[2,128,256]{2,1,0:T(8,128)S(1)}, u32[]{:S(2)}, u32[]{:S(2)}) collective-permute-start(f32[2,128,256]{2,1,0:T(8,128)S(1)} %collective-permute-done.14.refs_1_), channel_id=1, source_target_pairs={{0,2},{1,3},{4,6},{5,7},{8,10},{9,11},{12,14},{13,15},{18,16},{19,... | collective-permute-start | bytes 786440 | tf_op jit(solution)/shard_map/ppermute | solution.py:494
  54.8 5.3 %collective-permute-start.13 = (f32[8,128]{1,0:T(8,128)S(1)}, f32[8,128]{1,0:T(8,128)S(1)}, u32[]{:S(2)}, u32[]{:S(2)}) collective-permute-start(f32[8,128]{1,0:T(8,128)S(1)} %get-tuple-element.78.refs_1_), channel_id=1, source_target_pairs={{0,2},{1,3},{2,0},{3,1},{4,6},{5,7},{6,4},{7,5},{8,10},{9,11},{10,... | collective-permute-start | bytes 12296 | tf_op jit(solution)/shard_map/ppermute | solution.py:494
  60.8 4.9 %collective-permute-start.22 = (f32[3,128,128]{2,1,0:T(8,128)S(1)}, f32[3,128,128]{2,1,0:T(8,128)S(1)}, u32[]{:S(2)}, u32[]{:S(2)}) collective-permute-start(f32[3,128,128]{2,1,0:T(8,128)S(1)} %get-tuple-element.101), channel_id=1, source_target_pairs={{0,4},{1,5},{2,10},{3,11},{4,0},{5,1},{6,14},{7,15},{8,12},{9,13},... | collective-permute-start | bytes 589832 | tf_op jit(solution)/shard_map/ppermute | solution.py:494
  65.8 3.5 %collective-permute-start.23 = (f32[3,64,128]{2,1,0:T(8,128)S(1)}, f32[3,64,128]{2,1,0:T(8,128)S(1)}, u32[]{:S(2)}, u32[]{:S(2)}) collective-permute-start(f32[3,64,128]{2,1,0:T(8,128)S(1)} %get-tuple-element.103), channel_id=1, source_target_pairs={{0,1},{1,0},{2,6},{3,7},{4,5},{5,4},{6,2},{7,3},{8,9},{9,8},{10,14... | collective-permute-start | bytes 294920 | tf_op jit(solution)/shard_map/ppermute | solution.py:494
  69.3 3.4 %collective-permute-start.24 = (f32[3,32,128]{2,1,0:T(8,128)S(1)}, f32[3,32,128]{2,1,0:T(8,128)S(1)}, u32[]{:S(2)}, u32[]{:S(2)}) collective-permute-start(f32[3,32,128]{2,1,0:T(8,128)S(1)} %get-tuple-element.105), channel_id=1, source_target_pairs={{0,8},{1,9},{2,3},{3,2},{4,12},{5,13},{6,7},{7,6},{8,0},{9,1},{10,... | collective-permute-start | bytes 147464 | tf_op jit(solution)/shard_map/ppermute | solution.py:494
  72.7 4.2 %collective-permute-start.25 = (f32[3,32,128]{2,1,0:T(8,128)S(1)}, f32[3,32,128]{2,1,0:T(8,128)S(1)}, u32[]{:S(2)}, u32[]{:S(2)}) collective-permute-start(f32[3,32,128]{2,1,0:T(8,128)S(1)} %shard_map.116.mine_ref), channel_id=1, source_target_pairs={{0,2},{1,3},{2,0},{3,1},{4,6},{5,7},{6,4},{7,5},{8,10},{9,11},{10,... | collective-permute-start | bytes 147464 | tf_op jit(solution)/shard_map/ppermute | solution.py:494
  76.9 6.7 %collective-permute-start.26 = (f32[2,3,32,128]{3,2,1,0:T(8,128)S(1)}, f32[2,3,32,128]{3,2,1,0:T(8,128)S(1)}, u32[]{:S(2)}, u32[]{:S(2)}) collective-permute-start(f32[2,3,32,128]{3,2,1,0:T(8,128)S(1)} %shard_map.117.own_ref), channel_id=1, source_target_pairs={{0,16},{1,17},{4,20},{5,21},{8,24},{9,25},{12,28},{13,29},{18,2},{... | collective-permute-start | bytes 294920 | tf_op jit(solution)/shard_map/ppermute | solution.py:494
  83.6 3.8 %collective-permute-start.27 = (f32[1,2,3,32,128]{4,3,2,1,0:T(8,128)S(1)}, f32[1,2,3,32,128]{4,3,2,1,0:T(8,128)S(1)}, u32[]{:S(2)}, u32[]{:S(2)}) collective-permute-start(f32[1,2,3,32,128]{4,3,2,1,0:T(8,128)S(1)} %bitcast.38), channel_id=1, source_target_pairs={{0,8},{1,9},{2,3},{3,2},{4,12},{5,13},{6,7},{7,6},{8,0},{9,1},{10,... | collective-permute-start | bytes 294920 | tf_op jit(solution)/shard_map/ppermute | solution.py:494
  87.5 4.6 %collective-permute-start.28 = (f32[2,2,3,32,128]{4,3,2,1,0:T(8,128)S(1)}, f32[2,2,3,32,128]{4,3,2,1,0:T(8,128)S(1)}, u32[]{:S(2)}, u32[]{:S(2)}) collective-permute-start(f32[2,2,3,32,128]{4,3,2,1,0:T(8,128)S(1)} %bitcast.32), channel_id=1, source_target_pairs={{0,1},{1,0},{2,6},{3,7},{4,5},{5,4},{6,2},{7,3},{8,9},{9,8},{10,14... | collective-permute-start | bytes 589832 | tf_op jit(solution)/shard_map/ppermute | solution.py:494
  89.3 2.9 %collective-permute-start.20 = (f32[2,128,256]{2,1,0:T(8,128)S(1)}, f32[2,128,256]{2,1,0:T(8,128)S(1)}, u32[]{:S(2)}, u32[]{:S(2)}) collective-permute-start(f32[2,128,256]{2,1,0:T(8,128)S(1)} %get-tuple-element.97), channel_id=1, source_target_pairs={{0,2},{1,3},{2,0},{3,1},{4,6},{5,7},{6,4},{7,5},{8,10},{9,11},{10,... | collective-permute-start | bytes 786440 | tf_op jit(solution)/shard_map/ppermute | solution.py:494
  89.9 7.7 %collective-permute-start.18 = (f32[2,128,256]{2,1,0:T(8,128)S(1)}, f32[2,128,256]{2,1,0:T(8,128)S(1)}, u32[]{:S(2)}, u32[]{:S(2)}) collective-permute-start(f32[2,128,256]{2,1,0:T(8,128)S(1)} %get-tuple-element.93), channel_id=1, source_target_pairs={{0,2},{1,3},{2,0},{3,1},{4,6},{5,7},{6,4},{7,5},{8,10},{9,11},{10,... | collective-permute-start | bytes 786440 | tf_op jit(solution)/shard_map/ppermute | solution.py:494
  92.1 18.8 %collective-permute-start.29 = (f32[4,2,3,32,128]{4,3,2,1,0:T(8,128)S(1)}, f32[4,2,3,32,128]{4,3,2,1,0:T(8,128)S(1)}, u32[]{:S(2)}, u32[]{:S(2)}) collective-permute-start(f32[4,2,3,32,128]{4,3,2,1,0:T(8,128)S(1)} %bitcast.29), channel_id=1, source_target_pairs={{0,4},{1,5},{2,10},{3,11},{4,0},{5,1},{6,14},{7,15},{8,12},{9,13},... | collective-permute-start | bytes 1179656 | tf_op jit(solution)/shard_map/ppermute | solution.py:494
  92.2 15.1 %collective-permute-start.21 = (f32[2,128,256]{2,1,0:T(8,128)S(1)}, f32[2,128,256]{2,1,0:T(8,128)S(1)}, u32[]{:S(2)}, u32[]{:S(2)}) collective-permute-start(f32[2,128,256]{2,1,0:T(8,128)S(1)} %shard_map.112.refs_2_), channel_id=1, source_target_pairs={{2,16},{3,17},{6,20},{7,21},{10,24},{11,25},{14,28},{15,29},{16,2}... | collective-permute-start | bytes 786440 | tf_op jit(solution)/shard_map/ppermute | solution.py:494
  97.7 12.4 %collective-permute-start.19 = (f32[2,128,256]{2,1,0:T(8,128)S(1)}, f32[2,128,256]{2,1,0:T(8,128)S(1)}, u32[]{:S(2)}, u32[]{:S(2)}) collective-permute-start(f32[2,128,256]{2,1,0:T(8,128)S(1)} %shard_map.110.refs_0_), channel_id=1, source_target_pairs={{2,16},{3,17},{6,20},{7,21},{10,24},{11,25},{14,28},{15,29},{16,2}... | collective-permute-start | bytes 786440 | tf_op jit(solution)/shard_map/ppermute | solution.py:494
  (5 other events, 21.7 us)

commit v3 on v2

--- a/solution.py
+++ b/solution.py
@@ -602,6 +602,8 @@
         for at in range(len(tok_dims)):
             arrived = meet(payload, (tok_dims[at], tok_dims[at - 1]))
             if at + 1 < len(tok_dims):
+                if at == 0 and index + 1 in token_grads:
+                    arrived = tie(arrived, token_grads[index + 1])
                 (payload,) = call(add_kernel, [shape(rows + PAD, half)], payload, arrived)
         grad, coef, keyed = call(
             functools.partial(pre_kernel, tok_count),
@@ -644,22 +646,31 @@
         token_grads[index] = d_tokens
 
     kept, sends = outs
+    returned = {index: swap(token_grads[index]) for index in range(top)}
+
+    def wait(array, point):
+        for index in range(top):
+            if point == (4,0)[min(index, 1)]:
+                array = tie(array, returned[index])
+        return array
+
     for at in range(len(dims)):
         arrived = meet(sends, [order[at] for order in rs_orders])
+        arrived = wait(arrived, at)
         if at + 1 < len(dims):
             out_shapes = [shape(3, kept.shape[1] // 2, half)] * 2
             order = [order[at + 1] for order in rs_orders]
             kept, sends = call(functools.partial(halve_kernel, order), out_shapes, kept, arrived)
         else:
             (kept,) = call(functools.partial(halve_kernel, None), [shape(*kept.shape)], kept, arrived)
-    (pair,) = call(pair_kernel, [shape(2, *kept.shape)], kept, sibling(kept))
+    (pair,) = call(pair_kernel, [shape(2, *kept.shape)], kept, sibling(wait(kept, 2)))
     (block,) = call(
         functools.partial(choose_kernel, tok_count), [shape(*pair.shape)], pair, lend(pair)
     )
-    block = block[None]
+    block = wait(block[None], 3)
     ag_orders = [order[::-1] for order in rs_orders]
     for at in range(len(dims)):
-        arrived = meet(block, [order[at] for order in ag_orders])
+        arrived = wait(meet(block, [order[at] for order in ag_orders]), 4 + at)
         if at + 1 < len(dims):
             (pair,) = call(pair_kernel, [shape(2, *block.shape)], block, arrived)
             block = pair.reshape(2 * block.shape[0], *block.shape[1:])
@@ -671,7 +682,7 @@
     )
     arrays = []
     for index in range(top):
-        arrays += [token_grads[index], swap(token_grads[index])]
+        arrays += [token_grads[index], returned[index]]
     key_grad, value_grad = call(
         functools.partial(tokens_out_kernel, tok_count),
         [shape(groups, count, dim, dtype=BF16)] * 2,

time: 112 us -> 104 us (0.929); the launches traced: 112 us -> 102 us
  waiting for transfers between devices: 49.4 us -> 44.3 us
  starting transfers between devices: 46.5 us -> 41.6 us
    ppermute x30, waiting for transfers between devices: 49.4 us -> 44.3 us  [permute(): return lax.ppermute(array, ('tok', 'head', 'vid'), pairs)]
    ppermute x30, starting transfers between devices: 46.5 us -> 41.6 us  [permute(): return lax.ppermute(array, ('tok', 'head', 'vid'), pairs)]
  transfers between devices with their start and end apart: 30 -> 30, of which waited for: 15 -> 14; matrix products, arithmetic and copies ran while one was open for 0% -> 0% of each run, Pallas kernels for 8% -> 9%
where the time goes in v3:
time: 104 us; the launch traced here: 102 us
  waiting for transfers between devices  44.3 us (43%)
  starting transfers between devices  41.6 us (40%)
  Pallas kernels  12.8 us (12%)
  local copies, waits for them, and re-layouts  2.15 us (2%)
    ppermute x30, waiting for transfers between devices, permute(): return lax.ppermute(array, ('tok', 'head', 'vid'), pairs)  44.3 us
    ppermute x30, starting transfers between devices, permute(): return lax.ppermute(array, ('tok', 'head', 'vid'), pairs)  41.6 us
    pallas_call x29, Pallas kernels, call(): pl.pallas_call(kernel, out_shape=outs, **kwargs, scratch_shapes=scratch,...  12.8 us
    unnamed x14, local copies, waits for them, and re-layouts  2.15 us
  transfers between devices with their start and end apart: 30, of which 14 were waited for; matrix products, arithmetic and copies ran while one was open for 0% of the time, Pallas kernels for 9%

profile of v3, /device:TPU:1, one launch (start us, length us, event | category | flops | bytes accessed | tf_op | source)
XLA Modules:
  0.0 101.9 jit_solution(7094171897866642074)
XLA Ops:
  0.7 1.7 %shard_map.93.refs_0_ = f32[2,128,256]{2,1,0:T(8,128)} custom-call(bf16[3,128,256]{2,1,0:T(8,128)(2,1)} %bitcast.19, bf16[3,128,256]{2,1,0:T(8,128)(2,1)} %bitcast.23), custom_call_target="tpu_custom_call" | custom-call | flops 1 | bytes 1 | tf_op jit(solution)/shard_map/pallas_call | solution.py:440
  2.3 3.2 %collective-permute-start = (f32[2,128,256]{2,1,0:T(8,128)}, f32[2,128,256]{2,1,0:T(8,128)S(1)}, u32[]{:S(2)}, u32[]{:S(2)}) collective-permute-start(f32[2,128,256]{2,1,0:T(8,128)} %shard_map.93.refs_0_), channel_id=1, source_target_pairs={{0,2},{1,3},{2,18},{3,19},{4,6},{5,7},{6,22},{7,23},{8,10},{9,11},... | collective-permute-start | bytes 786440 | tf_op jit(solution)/shard_map/ppermute | solution.py:494
  6.5 1.1 %copy-done.4 = bf16[1,2,1,3,256,256]{5,4,3,2,1,0:T(8,128)(2,1)S(1)} copy-done((bf16[1,2,1,3,256,256]{5,4,3,2,1,0:T(8,128)(2,1)S(1)}, bf16[1,2,1,3,256,256]{5,4,3,2,1,0:T(8,128)(2,1)}, u32[]{:S(2)}) %copy-start.4) | copy-done | bytes 786456
  7.6 1.3 %shard_map.94 = (f32[2,3,256,256]{3,2,1,0:T(8,128)S(1)}, f32[768,128]{1,0:T(8,128)S(1)}, f32[1560,128]{1,0:T(8,128)S(1)}, f32[768,128]{1,0:T(8,128)S(1)}, f32[1560,128]{1,0:T(8,128)S(1)}) custom-call(bf16[3,256,256]{2,1,0:T(8,128)(2,1)S(1)} %bitcast.27, bf16[2,3,256,256]{3,2,1,0:T(8,128)(2,1)S(1)} %bitcast.31), custom_call_target="tpu_custom_call" | custom-call | flops 1 | bytes 1 | tf_op jit(solution)/shard_map/pallas_call | solution.py:440
  9.1 1.9 %shard_map.95 = bf16[3,128,256]{2,1,0:T(8,128)(2,1)} custom-call(bf16[3,128,256]{2,1,0:T(8,128)(2,1)S(1)} %bitcast.20, bf16[3,128,256]{2,1,0:T(8,128)(2,1)S(1)} %bitcast.24, bf16[3,256,256]{2,1,0:T(8,128)(2,1)S(1)} %bitcast.28, f32[2,3,256,256]{3,2,1,0:T(8,128)S(1)} %get-tuple-element.59.full_ref), custom_call_target="tpu_custom_call" | custom-call | flops 1 | bytes 1 | tf_op jit(solution)/shard_map/pallas_call | solution.py:440
  11.0 1.4 %collective-permute-start.1 = (f32[2,128,256]{2,1,0:T(8,128)S(1)}, f32[2,128,256]{2,1,0:T(8,128)S(1)}, u32[]{:S(2)}, u32[]{:S(2)}) collective-permute-start(f32[2,128,256]{2,1,0:T(8,128)S(1)} %collective-permute-done.refs_1_), channel_id=1, source_target_pairs={{0,2},{1,3},{4,6},{5,7},{8,10},{9,11},{12,14},{13,15},{18,16},{19,... | collective-permute-start | bytes 786440 | tf_op jit(solution)/shard_map/ppermute | solution.py:494
  12.5 2.8 %collective-permute-start.10 = (f32[1560,128]{1,0:T(8,128)S(1)}, f32[1560,128]{1,0:T(8,128)S(1)}, u32[]{:S(2)}, u32[]{:S(2)}) collective-permute-start(f32[1560,128]{1,0:T(8,128)S(1)} %get-tuple-element.73), channel_id=1, source_target_pairs={{0,2},{1,3},{2,0},{3,1},{4,6},{5,7},{6,4},{7,5},{8,10},{9,11},{10,... | collective-permute-start | bytes 2396168 | tf_op jit(solution)/shard_map/ppermute | solution.py:494
  17.7 1.8 %collective-permute-start.6 = (f32[2,128,256]{2,1,0:T(8,128)S(1)}, f32[2,128,256]{2,1,0:T(8,128)S(1)}, u32[]{:S(2)}, u32[]{:S(2)}) collective-permute-start(f32[2,128,256]{2,1,0:T(8,128)S(1)} %get-tuple-element.66.refs_0_), channel_id=1, source_target_pairs={{0,2},{1,3},{2,18},{3,19},{4,6},{5,7},{6,22},{7,23},{8,10},{9,11},... | collective-permute-start | bytes 786440 | tf_op jit(solution)/shard_map/ppermute | solution.py:494
  19.6 4.6 %collective-permute-done.3.recv_ref = f32[776,128]{1,0:T(8,128)S(1)} collective-permute-done((f32[776,128]{1,0:T(8,128)S(1)}, f32[776,128]{1,0:T(8,128)S(1)}, u32[]{:S(2)}, u32[]{:S(2)}) %collective-permute-start.3) | collective-permute-done | bytes 397344 | tf_op jit(solution)/shard_map/ppermute | solution.py:494
  24.3 3.4 %collective-permute-start.4 = (f32[776,128]{1,0:T(8,128)S(1)}, f32[776,128]{1,0:T(8,128)S(1)}, u32[]{:S(2)}, u32[]{:S(2)}) collective-permute-start(f32[776,128]{1,0:T(8,128)S(1)} %shard_map.98.mine_ref), channel_id=1, source_target_pairs={{0,8},{1,9},{2,6},{3,7},{4,12},{5,13},{6,2},{7,3},{8,0},{9,1},{10,... | collective-permute-start | bytes 1191944 | tf_op jit(solution)/shard_map/ppermute | solution.py:494
  27.7 1.3 %collective-permute-start.7 = (f32[2,128,256]{2,1,0:T(8,128)S(1)}, f32[2,128,256]{2,1,0:T(8,128)S(1)}, u32[]{:S(2)}, u32[]{:S(2)}) collective-permute-start(f32[2,128,256]{2,1,0:T(8,128)S(1)} %collective-permute-done.6.refs_1_), channel_id=1, source_target_pairs={{0,2},{1,3},{4,6},{5,7},{8,10},{9,11},{12,14},{13,15},{18,16},{19,... | collective-permute-start | bytes 786440 | tf_op jit(solution)/shard_map/ppermute | solution.py:494
  29.0 1.3 %collective-permute-start.9 = (f32[2,128,256]{2,1,0:T(8,128)S(1)}, f32[2,128,256]{2,1,0:T(8,128)S(1)}, u32[]{:S(2)}, u32[]{:S(2)}) collective-permute-start(f32[2,128,256]{2,1,0:T(8,128)S(1)} %collective-permute-done.8.refs_4_), channel_id=1, source_target_pairs={{0,2},{1,3},{4,6},{5,7},{8,10},{9,11},{12,14},{13,15},{18,16},{19,... | collective-permute-start | bytes 786440 | tf_op jit(solution)/shard_map/ppermute | solution.py:494
  30.3 2.9 %collective-permute-done.4.recv_ref = f32[776,128]{1,0:T(8,128)S(1)} collective-permute-done((f32[776,128]{1,0:T(8,128)S(1)}, f32[776,128]{1,0:T(8,128)S(1)}, u32[]{:S(2)}, u32[]{:S(2)}) %collective-permute-start.4) | collective-permute-done | bytes 397344 | tf_op jit(solution)/shard_map/ppermute | solution.py:494
  33.3 4.2 %collective-permute-start.5 = (f32[8,128]{1,0:T(8,128)S(1)}, f32[8,128]{1,0:T(8,128)S(1)}, u32[]{:S(2)}, u32[]{:S(2)}) collective-permute-start(f32[8,128]{1,0:T(8,128)S(1)} %get-tuple-element.64.refs_1_), channel_id=1, source_target_pairs={{0,2},{1,3},{2,0},{3,1},{4,6},{5,7},{6,4},{7,5},{8,10},{9,11},{10,... | collective-permute-start | bytes 12296 | tf_op jit(solution)/shard_map/ppermute | solution.py:494
  41.8 5.2 %collective-permute-done.11.recv_ref = f32[776,128]{1,0:T(8,128)S(1)} collective-permute-done((f32[776,128]{1,0:T(8,128)S(1)}, f32[776,128]{1,0:T(8,128)S(1)}, u32[]{:S(2)}, u32[]{:S(2)}) %collective-permute-start.11) | collective-permute-done | bytes 397344 | tf_op jit(solution)/shard_map/ppermute | solution.py:494
  47.2 1.3 %collective-permute-start.18 = (f32[2,128,256]{2,1,0:T(8,128)S(1)}, f32[2,128,256]{2,1,0:T(8,128)S(1)}, u32[]{:S(2)}, u32[]{:S(2)}) collective-permute-start(f32[2,128,256]{2,1,0:T(8,128)S(1)} %collective-permute-done.17.refs_4_), channel_id=1, source_target_pairs={{0,2},{1,3},{4,6},{5,7},{8,10},{9,11},{12,14},{13,15},{18,16},{19,... | collective-permute-start | bytes 786440 | tf_op jit(solution)/shard_map/ppermute | solution.py:494
  48.5 2.6 %collective-permute-done.15.refs_1_ = f32[2,128,256]{2,1,0:T(8,128)S(1)} collective-permute-done((f32[2,128,256]{2,1,0:T(8,128)S(1)}, f32[2,128,256]{2,1,0:T(8,128)S(1)}, u32[]{:S(2)}, u32[]{:S(2)}) %collective-permute-start.15) | collective-permute-done | bytes 262176 | tf_op jit(solution)/shard_map/ppermute | solution.py:494
  51.1 1.3 %collective-permute-start.16 = (f32[2,128,256]{2,1,0:T(8,128)S(1)}, f32[2,128,256]{2,1,0:T(8,128)S(1)}, u32[]{:S(2)}, u32[]{:S(2)}) collective-permute-start(f32[2,128,256]{2,1,0:T(8,128)S(1)} %collective-permute-done.15.refs_1_), channel_id=1, source_target_pairs={{0,2},{1,3},{4,6},{5,7},{8,10},{9,11},{12,14},{13,15},{18,16},{19,... | collective-permute-start | bytes 786440 | tf_op jit(solution)/shard_map/ppermute | solution.py:494
  52.4 6.8 %collective-permute-start.21 = (f32[2,128,256]{2,1,0:T(8,128)S(1)}, f32[2,128,256]{2,1,0:T(8,128)S(1)}, u32[]{:S(2)}, u32[]{:S(2)}) collective-permute-start(f32[2,128,256]{2,1,0:T(8,128)S(1)} %shard_map.105.refs_2_), channel_id=1, source_target_pairs={{2,16},{3,17},{6,20},{7,21},{10,24},{11,25},{14,28},{15,29},{16,2}... | collective-permute-start | bytes 786440 | tf_op jit(solution)/shard_map/ppermute | solution.py:494
  62.2 1.8 %collective-permute-start.19 = (f32[2,128,256]{2,1,0:T(8,128)S(1)}, f32[2,128,256]{2,1,0:T(8,128)S(1)}, u32[]{:S(2)}, u32[]{:S(2)}) collective-permute-start(f32[2,128,256]{2,1,0:T(8,128)S(1)} %get-tuple-element.101), channel_id=1, source_target_pairs={{0,2},{1,3},{2,0},{3,1},{4,6},{5,7},{6,4},{7,5},{8,10},{9,11},{10,... | collective-permute-start | bytes 786440 | tf_op jit(solution)/shard_map/ppermute | solution.py:494
  63.9 2.2 %collective-permute-done.21.refs_3_ = f32[2,128,256]{2,1,0:T(8,128)S(1)} collective-permute-done((f32[2,128,256]{2,1,0:T(8,128)S(1)}, f32[2,128,256]{2,1,0:T(8,128)S(1)}, u32[]{:S(2)}, u32[]{:S(2)}) %collective-permute-start.21) | collective-permute-done | bytes 262176 | tf_op jit(solution)/shard_map/ppermute | solution.py:494
  66.2 2.0 %collective-permute-done.22.recv_ref = f32[3,128,128]{2,1,0:T(8,128)S(1)} collective-permute-done((f32[3,128,128]{2,1,0:T(8,128)S(1)}, f32[3,128,128]{2,1,0:T(8,128)S(1)}, u32[]{:S(2)}, u32[]{:S(2)}) %collective-permute-start.22) | collective-permute-done | bytes 196640 | tf_op jit(solution)/shard_map/ppermute | solution.py:494
  68.8 3.1 %collective-permute-done.23.recv_ref = f32[3,64,128]{2,1,0:T(8,128)S(1)} collective-permute-done((f32[3,64,128]{2,1,0:T(8,128)S(1)}, f32[3,64,128]{2,1,0:T(8,128)S(1)}, u32[]{:S(2)}, u32[]{:S(2)}) %collective-permute-start.23) | collective-permute-done | bytes 98336 | tf_op jit(solution)/shard_map/ppermute | solution.py:494
  72.0 1.6 %collective-permute-start.24 = (f32[3,32,128]{2,1,0:T(8,128)S(1)}, f32[3,32,128]{2,1,0:T(8,128)S(1)}, u32[]{:S(2)}, u32[]{:S(2)}) collective-permute-start(f32[3,32,128]{2,1,0:T(8,128)S(1)} %get-tuple-element.110), channel_id=1, source_target_pairs={{0,8},{1,9},{2,3},{3,2},{4,12},{5,13},{6,7},{7,6},{8,0},{9,1},{10,... | collective-permute-start | bytes 147464 | tf_op jit(solution)/shard_map/ppermute | solution.py:494
  73.6 1.9 %collective-permute-start.20 = (f32[2,128,256]{2,1,0:T(8,128)S(1)}, f32[2,128,256]{2,1,0:T(8,128)S(1)}, u32[]{:S(2)}, u32[]{:S(2)}) collective-permute-start(f32[2,128,256]{2,1,0:T(8,128)S(1)} %shard_map.112.refs_0_), channel_id=1, source_target_pairs={{2,16},{3,17},{6,20},{7,21},{10,24},{11,25},{14,28},{15,29},{16,2}... | collective-permute-start | bytes 786440 | tf_op jit(solution)/shard_map/ppermute | solution.py:494
  75.5 1.1 %collective-permute-start.25 = (f32[3,32,128]{2,1,0:T(8,128)S(1)}, f32[3,32,128]{2,1,0:T(8,128)S(1)}, u32[]{:S(2)}, u32[]{:S(2)}) collective-permute-start(f32[3,32,128]{2,1,0:T(8,128)S(1)} %shard_map.116.mine_ref), channel_id=1, source_target_pairs={{0,2},{1,3},{2,0},{3,1},{4,6},{5,7},{6,4},{7,5},{8,10},{9,11},{10,... | collective-permute-start | bytes 147464 | tf_op jit(solution)/shard_map/ppermute | solution.py:494
  77.5 1.3 %collective-permute-start.26 = (f32[2,3,32,128]{3,2,1,0:T(8,128)S(1)}, f32[2,3,32,128]{3,2,1,0:T(8,128)S(1)}, u32[]{:S(2)}, u32[]{:S(2)}) collective-permute-start(f32[2,3,32,128]{3,2,1,0:T(8,128)S(1)} %shard_map.117.own_ref), channel_id=1, source_target_pairs={{0,16},{1,17},{4,20},{5,21},{8,24},{9,25},{12,28},{13,29},{18,2},{... | collective-permute-start | bytes 294920 | tf_op jit(solution)/shard_map/ppermute | solution.py:494
  78.8 6.7 %collective-permute-done.26.moved_ref = f32[2,3,32,128]{3,2,1,0:T(8,128)S(1)} collective-permute-done((f32[2,3,32,128]{3,2,1,0:T(8,128)S(1)}, f32[2,3,32,128]{3,2,1,0:T(8,128)S(1)}, u32[]{:S(2)}, u32[]{:S(2)}) %collective-permute-start.26) | collective-permute-done | bytes 98336 | tf_op jit(solution)/shard_map/ppermute | solution.py:494
  86.3 2.7 %collective-permute-done.27.other_ref = f32[1,2,3,32,128]{4,3,2,1,0:T(8,128)S(1)} collective-permute-done((f32[1,2,3,32,128]{4,3,2,1,0:T(8,128)S(1)}, f32[1,2,3,32,128]{4,3,2,1,0:T(8,128)S(1)}, u32[]{:S(2)}, u32[]{:S(2)}) %collective-permute-start.27) | collective-permute-done | bytes 98336 | tf_op jit(solution)/shard_map/ppermute | solution.py:494
  89.0 1.2 %collective-permute-start.28 = (f32[2,2,3,32,128]{4,3,2,1,0:T(8,128)S(1)}, f32[2,2,3,32,128]{4,3,2,1,0:T(8,128)S(1)}, u32[]{:S(2)}, u32[]{:S(2)}) collective-permute-start(f32[2,2,3,32,128]{4,3,2,1,0:T(8,128)S(1)} %bitcast.32), channel_id=1, source_target_pairs={{0,1},{1,0},{2,6},{3,7},{4,5},{5,4},{6,2},{7,3},{8,9},{9,8},{10,14... | collective-permute-start | bytes 589832 | tf_op jit(solution)/shard_map/ppermute | solution.py:494
  90.2 3.7 %collective-permute-done.28.other_ref = f32[2,2,3,32,128]{4,3,2,1,0:T(8,128)S(1)} collective-permute-done((f32[2,2,3,32,128]{4,3,2,1,0:T(8,128)S(1)}, f32[2,2,3,32,128]{4,3,2,1,0:T(8,128)S(1)}, u32[]{:S(2)}, u32[]{:S(2)}) %collective-permute-start.28) | collective-permute-done | bytes 196640 | tf_op jit(solution)/shard_map/ppermute | solution.py:494
  94.8 6.1 %collective-permute-done.29.recv_ref = f32[4,2,3,32,128]{4,3,2,1,0:T(8,128)S(1)} collective-permute-done((f32[4,2,3,32,128]{4,3,2,1,0:T(8,128)S(1)}, f32[4,2,3,32,128]{4,3,2,1,0:T(8,128)S(1)}, u32[]{:S(2)}, u32[]{:S(2)}) %collective-permute-start.29) | collective-permute-done | bytes 393248 | tf_op jit(solution)/shard_map/ppermute | solution.py:494
  (71 shorter events, 15.5 us)
Async XLA Ops:
  0.6 8.4 %copy-start = (bf16[1,3,128,1,256]{4,2,3,1,0:T(8,128)(2,1)S(1)}, bf16[1,3,128,1,256]{4,2,3,1,0:T(8,128)(2,1)}, u32[]{:S(2)}) copy-start(bf16[1,3,128,1,256]{4,2,3,1,0:T(8,128)(2,1)} %param.6) | copy-start | bytes 589828
  0.6 8.4 %copy-start.1 = (bf16[1,3,128,1,256]{4,2,3,1,0:T(8,128)(2,1)S(1)}, bf16[1,3,128,1,256]{4,2,3,1,0:T(8,128)(2,1)}, u32[]{:S(2)}) copy-start(bf16[1,3,128,1,256]{4,2,3,1,0:T(8,128)(2,1)} %param.9) | copy-start | bytes 589828
  2.3 8.7 %collective-permute-start = (f32[2,128,256]{2,1,0:T(8,128)}, f32[2,128,256]{2,1,0:T(8,128)S(1)}, u32[]{:S(2)}, u32[]{:S(2)}) collective-permute-start(f32[2,128,256]{2,1,0:T(8,128)} %shard_map.93.refs_0_), channel_id=1, source_target_pairs={{0,2},{1,3},{2,18},{3,19},{4,6},{5,7},{6,22},{7,23},{8,10},{9,11},... | collective-permute-start | bytes 786440 | tf_op jit(solution)/shard_map/ppermute | solution.py:494
  9.0 6.2 %collective-permute-start.2 = (f32[768,128]{1,0:T(8,128)S(1)}, f32[768,128]{1,0:T(8,128)S(1)}, u32[]{:S(2)}, u32[]{:S(2)}) collective-permute-start(f32[768,128]{1,0:T(8,128)S(1)} %get-tuple-element.62), channel_id=1, source_target_pairs={{0,2},{1,3},{2,0},{3,1},{4,6},{5,7},{6,4},{7,5},{8,10},{9,11},{10,... | collective-permute-start | bytes 1179656 | tf_op jit(solution)/shard_map/ppermute | solution.py:494
  11.0 5.1 %collective-permute-start.1 = (f32[2,128,256]{2,1,0:T(8,128)S(1)}, f32[2,128,256]{2,1,0:T(8,128)S(1)}, u32[]{:S(2)}, u32[]{:S(2)}) collective-permute-start(f32[2,128,256]{2,1,0:T(8,128)S(1)} %collective-permute-done.refs_1_), channel_id=1, source_target_pairs={{0,2},{1,3},{4,6},{5,7},{8,10},{9,11},{12,14},{13,15},{18,16},{19,... | collective-permute-start | bytes 786440 | tf_op jit(solution)/shard_map/ppermute | solution.py:494
  12.5 25.0 %collective-permute-start.10 = (f32[1560,128]{1,0:T(8,128)S(1)}, f32[1560,128]{1,0:T(8,128)S(1)}, u32[]{:S(2)}, u32[]{:S(2)}) collective-permute-start(f32[1560,128]{1,0:T(8,128)S(1)} %get-tuple-element.73), channel_id=1, source_target_pairs={{0,2},{1,3},{2,0},{3,1},{4,6},{5,7},{6,4},{7,5},{8,10},{9,11},{10,... | collective-permute-start | bytes 2396168 | tf_op jit(solution)/shard_map/ppermute | solution.py:494
  16.8 7.5 %collective-permute-start.3 = (f32[776,128]{1,0:T(8,128)S(1)}, f32[776,128]{1,0:T(8,128)S(1)}, u32[]{:S(2)}, u32[]{:S(2)}) collective-permute-start(f32[776,128]{1,0:T(8,128)S(1)} %shard_map.97.mine_ref), channel_id=1, source_target_pairs={{0,4},{1,5},{2,10},{3,11},{4,0},{5,1},{6,14},{7,15},{8,12},{9,13},... | collective-permute-start | bytes 1191944 | tf_op jit(solution)/shard_map/ppermute | solution.py:494
  17.7 10.0 %collective-permute-start.6 = (f32[2,128,256]{2,1,0:T(8,128)S(1)}, f32[2,128,256]{2,1,0:T(8,128)S(1)}, u32[]{:S(2)}, u32[]{:S(2)}) collective-permute-start(f32[2,128,256]{2,1,0:T(8,128)S(1)} %get-tuple-element.66.refs_0_), channel_id=1, source_target_pairs={{0,2},{1,3},{2,18},{3,19},{4,6},{5,7},{6,22},{7,23},{8,10},{9,11},... | collective-permute-start | bytes 786440 | tf_op jit(solution)/shard_map/ppermute | solution.py:494
  19.5 9.6 %collective-permute-start.8 = (f32[2,128,256]{2,1,0:T(8,128)S(1)}, f32[2,128,256]{2,1,0:T(8,128)S(1)}, u32[]{:S(2)}, u32[]{:S(2)}) collective-permute-start(f32[2,128,256]{2,1,0:T(8,128)S(1)} %get-tuple-element.69.refs_3_), channel_id=1, source_target_pairs={{0,2},{1,3},{2,18},{3,19},{4,6},{5,7},{6,22},{7,23},{8,10},{9,11},... | collective-permute-start | bytes 786440 | tf_op jit(solution)/shard_map/ppermute | solution.py:494
  24.3 8.9 %collective-permute-start.4 = (f32[776,128]{1,0:T(8,128)S(1)}, f32[776,128]{1,0:T(8,128)S(1)}, u32[]{:S(2)}, u32[]{:S(2)}) collective-permute-start(f32[776,128]{1,0:T(8,128)S(1)} %shard_map.98.mine_ref), channel_id=1, source_target_pairs={{0,8},{1,9},{2,6},{3,7},{4,12},{5,13},{6,2},{7,3},{8,0},{9,1},{10,... | collective-permute-start | bytes 1191944 | tf_op jit(solution)/shard_map/ppermute | solution.py:494
  27.7 9.8 %collective-permute-start.7 = (f32[2,128,256]{2,1,0:T(8,128)S(1)}, f32[2,128,256]{2,1,0:T(8,128)S(1)}, u32[]{:S(2)}, u32[]{:S(2)}) collective-permute-start(f32[2,128,256]{2,1,0:T(8,128)S(1)} %collective-permute-done.6.refs_1_), channel_id=1, source_target_pairs={{0,2},{1,3},{4,6},{5,7},{8,10},{9,11},{12,14},{13,15},{18,16},{19,... | collective-permute-start | bytes 786440 | tf_op jit(solution)/shard_map/ppermute | solution.py:494
  29.0 8.5 %collective-permute-start.9 = (f32[2,128,256]{2,1,0:T(8,128)S(1)}, f32[2,128,256]{2,1,0:T(8,128)S(1)}, u32[]{:S(2)}, u32[]{:S(2)}) collective-permute-start(f32[2,128,256]{2,1,0:T(8,128)S(1)} %collective-permute-done.8.refs_4_), channel_id=1, source_target_pairs={{0,2},{1,3},{4,6},{5,7},{8,10},{9,11},{12,14},{13,15},{18,16},{19,... | collective-permute-start | bytes 786440 | tf_op jit(solution)/shard_map/ppermute | solution.py:494
  33.3 5.1 %collective-permute-start.5 = (f32[8,128]{1,0:T(8,128)S(1)}, f32[8,128]{1,0:T(8,128)S(1)}, u32[]{:S(2)}, u32[]{:S(2)}) collective-permute-start(f32[8,128]{1,0:T(8,128)S(1)} %get-tuple-element.64.refs_1_), channel_id=1, source_target_pairs={{0,2},{1,3},{2,0},{3,1},{4,6},{5,7},{6,4},{7,5},{8,10},{9,11},{10,... | collective-permute-start | bytes 12296 | tf_op jit(solution)/shard_map/ppermute | solution.py:494
  39.1 7.9 %collective-permute-start.11 = (f32[776,128]{1,0:T(8,128)S(1)}, f32[776,128]{1,0:T(8,128)S(1)}, u32[]{:S(2)}, u32[]{:S(2)}) collective-permute-start(f32[776,128]{1,0:T(8,128)S(1)} %get-tuple-element.79.mine_ref), channel_id=1, source_target_pairs={{0,4},{1,5},{2,10},{3,11},{4,0},{5,1},{6,14},{7,15},{8,12},{9,13},... | collective-permute-start | bytes 1191944 | tf_op jit(solution)/shard_map/ppermute | solution.py:494
  39.7 2.0 %collective-permute-start.12 = (f32[2,128,256]{2,1,0:T(8,128)S(1)}, f32[2,128,256]{2,1,0:T(8,128)S(1)}, u32[]{:S(2)}, u32[]{:S(2)}) collective-permute-start(f32[2,128,256]{2,1,0:T(8,128)S(1)} %get-tuple-element.83), channel_id=1, source_target_pairs={{0,2},{1,3},{2,0},{3,1},{4,6},{5,7},{6,4},{7,5},{8,10},{9,11},{10,... | collective-permute-start | bytes 786440 | tf_op jit(solution)/shard_map/ppermute | solution.py:494
  41.0 6.2 %collective-permute-start.17 = (f32[2,128,256]{2,1,0:T(8,128)S(1)}, f32[2,128,256]{2,1,0:T(8,128)S(1)}, u32[]{:S(2)}, u32[]{:S(2)}) collective-permute-start(f32[2,128,256]{2,1,0:T(8,128)S(1)} %get-tuple-element.91.refs_3_), channel_id=1, source_target_pairs={{0,2},{1,3},{2,18},{3,19},{4,6},{5,7},{6,22},{7,23},{8,10},{9,11},... | collective-permute-start | bytes 786440 | tf_op jit(solution)/shard_map/ppermute | solution.py:494
  41.1 10.0 %collective-permute-start.15 = (f32[2,128,256]{2,1,0:T(8,128)S(1)}, f32[2,128,256]{2,1,0:T(8,128)S(1)}, u32[]{:S(2)}, u32[]{:S(2)}) collective-permute-start(f32[2,128,256]{2,1,0:T(8,128)S(1)} %get-tuple-element.88.refs_0_), channel_id=1, source_target_pairs={{0,2},{1,3},{2,18},{3,19},{4,6},{5,7},{6,22},{7,23},{8,10},{9,11},... | collective-permute-start | bytes 786440 | tf_op jit(solution)/shard_map/ppermute | solution.py:494
  47.1 12.1 %collective-permute-start.13 = (f32[776,128]{1,0:T(8,128)S(1)}, f32[776,128]{1,0:T(8,128)S(1)}, u32[]{:S(2)}, u32[]{:S(2)}) collective-permute-start(f32[776,128]{1,0:T(8,128)S(1)} %shard_map.106.mine_ref), channel_id=1, source_target_pairs={{0,8},{1,9},{2,6},{3,7},{4,12},{5,13},{6,2},{7,3},{8,0},{9,1},{10,... | collective-permute-start | bytes 1191944 | tf_op jit(solution)/shard_map/ppermute | solution.py:494
  47.2 12.8 %collective-permute-start.18 = (f32[2,128,256]{2,1,0:T(8,128)S(1)}, f32[2,128,256]{2,1,0:T(8,128)S(1)}, u32[]{:S(2)}, u32[]{:S(2)}) collective-permute-start(f32[2,128,256]{2,1,0:T(8,128)S(1)} %collective-permute-done.17.refs_4_), channel_id=1, source_target_pairs={{0,2},{1,3},{4,6},{5,7},{8,10},{9,11},{12,14},{13,15},{18,16},{19,... | collective-permute-start | bytes 786440 | tf_op jit(solution)/shard_map/ppermute | solution.py:494
  51.1 8.9 %collective-permute-start.16 = (f32[2,128,256]{2,1,0:T(8,128)S(1)}, f32[2,128,256]{2,1,0:T(8,128)S(1)}, u32[]{:S(2)}, u32[]{:S(2)}) collective-permute-start(f32[2,128,256]{2,1,0:T(8,128)S(1)} %collective-permute-done.15.refs_1_), channel_id=1, source_target_pairs={{0,2},{1,3},{4,6},{5,7},{8,10},{9,11},{12,14},{13,15},{18,16},{19,... | collective-permute-start | bytes 786440 | tf_op jit(solution)/shard_map/ppermute | solution.py:494
  52.4 13.8 %collective-permute-start.21 = (f32[2,128,256]{2,1,0:T(8,128)S(1)}, f32[2,128,256]{2,1,0:T(8,128)S(1)}, u32[]{:S(2)}, u32[]{:S(2)}) collective-permute-start(f32[2,128,256]{2,1,0:T(8,128)S(1)} %shard_map.105.refs_2_), channel_id=1, source_target_pairs={{2,16},{3,17},{6,20},{7,21},{10,24},{11,25},{14,28},{15,29},{16,2}... | collective-permute-start | bytes 786440 | tf_op jit(solution)/shard_map/ppermute | solution.py:494
  59.3 1.5 %collective-permute-start.14 = (f32[8,128]{1,0:T(8,128)S(1)}, f32[8,128]{1,0:T(8,128)S(1)}, u32[]{:S(2)}, u32[]{:S(2)}) collective-permute-start(f32[8,128]{1,0:T(8,128)S(1)} %get-tuple-element.86.refs_1_), channel_id=1, source_target_pairs={{0,2},{1,3},{2,0},{3,1},{4,6},{5,7},{6,4},{7,5},{8,10},{9,11},{10,... | collective-permute-start | bytes 12296 | tf_op jit(solution)/shard_map/ppermute | solution.py:494
  61.5 6.6 %collective-permute-start.22 = (f32[3,128,128]{2,1,0:T(8,128)S(1)}, f32[3,128,128]{2,1,0:T(8,128)S(1)}, u32[]{:S(2)}, u32[]{:S(2)}) collective-permute-start(f32[3,128,128]{2,1,0:T(8,128)S(1)} %get-tuple-element.105), channel_id=1, source_target_pairs={{0,4},{1,5},{2,10},{3,11},{4,0},{5,1},{6,14},{7,15},{8,12},{9,13},... | collective-permute-start | bytes 589832 | tf_op jit(solution)/shard_map/ppermute | solution.py:494
  62.2 11.4 %collective-permute-start.19 = (f32[2,128,256]{2,1,0:T(8,128)S(1)}, f32[2,128,256]{2,1,0:T(8,128)S(1)}, u32[]{:S(2)}, u32[]{:S(2)}) collective-permute-start(f32[2,128,256]{2,1,0:T(8,128)S(1)} %get-tuple-element.101), channel_id=1, source_target_pairs={{0,2},{1,3},{2,0},{3,1},{4,6},{5,7},{6,4},{7,5},{8,10},{9,11},{10,... | collective-permute-start | bytes 786440 | tf_op jit(solution)/shard_map/ppermute | solution.py:494
  68.2 3.7 %collective-permute-start.23 = (f32[3,64,128]{2,1,0:T(8,128)S(1)}, f32[3,64,128]{2,1,0:T(8,128)S(1)}, u32[]{:S(2)}, u32[]{:S(2)}) collective-permute-start(f32[3,64,128]{2,1,0:T(8,128)S(1)} %get-tuple-element.108), channel_id=1, source_target_pairs={{0,1},{1,0},{2,6},{3,7},{4,5},{5,4},{6,2},{7,3},{8,9},{9,8},{10,14... | collective-permute-start | bytes 294920 | tf_op jit(solution)/shard_map/ppermute | solution.py:494
  72.0 3.5 %collective-permute-start.24 = (f32[3,32,128]{2,1,0:T(8,128)S(1)}, f32[3,32,128]{2,1,0:T(8,128)S(1)}, u32[]{:S(2)}, u32[]{:S(2)}) collective-permute-start(f32[3,32,128]{2,1,0:T(8,128)S(1)} %get-tuple-element.110), channel_id=1, source_target_pairs={{0,8},{1,9},{2,3},{3,2},{4,12},{5,13},{6,7},{7,6},{8,0},{9,1},{10,... | collective-permute-start | bytes 147464 | tf_op jit(solution)/shard_map/ppermute | solution.py:494
  73.6 12.7 %collective-permute-start.20 = (f32[2,128,256]{2,1,0:T(8,128)S(1)}, f32[2,128,256]{2,1,0:T(8,128)S(1)}, u32[]{:S(2)}, u32[]{:S(2)}) collective-permute-start(f32[2,128,256]{2,1,0:T(8,128)S(1)} %shard_map.112.refs_0_), channel_id=1, source_target_pairs={{2,16},{3,17},{6,20},{7,21},{10,24},{11,25},{14,28},{15,29},{16,2}... | collective-permute-start | bytes 786440 | tf_op jit(solution)/shard_map/ppermute | solution.py:494
  75.5 1.9 %collective-permute-start.25 = (f32[3,32,128]{2,1,0:T(8,128)S(1)}, f32[3,32,128]{2,1,0:T(8,128)S(1)}, u32[]{:S(2)}, u32[]{:S(2)}) collective-permute-start(f32[3,32,128]{2,1,0:T(8,128)S(1)} %shard_map.116.mine_ref), channel_id=1, source_target_pairs={{0,2},{1,3},{2,0},{3,1},{4,6},{5,7},{6,4},{7,5},{8,10},{9,11},{10,... | collective-permute-start | bytes 147464 | tf_op jit(solution)/shard_map/ppermute | solution.py:494
  77.5 8.0 %collective-permute-start.26 = (f32[2,3,32,128]{3,2,1,0:T(8,128)S(1)}, f32[2,3,32,128]{3,2,1,0:T(8,128)S(1)}, u32[]{:S(2)}, u32[]{:S(2)}) collective-permute-start(f32[2,3,32,128]{3,2,1,0:T(8,128)S(1)} %shard_map.117.own_ref), channel_id=1, source_target_pairs={{0,16},{1,17},{4,20},{5,21},{8,24},{9,25},{12,28},{13,29},{18,2},{... | collective-permute-start | bytes 294920 | tf_op jit(solution)/shard_map/ppermute | solution.py:494
  85.4 3.5 %collective-permute-start.27 = (f32[1,2,3,32,128]{4,3,2,1,0:T(8,128)S(1)}, f32[1,2,3,32,128]{4,3,2,1,0:T(8,128)S(1)}, u32[]{:S(2)}, u32[]{:S(2)}) collective-permute-start(f32[1,2,3,32,128]{4,3,2,1,0:T(8,128)S(1)} %bitcast.38), channel_id=1, source_target_pairs={{0,8},{1,9},{2,3},{3,2},{4,12},{5,13},{6,7},{7,6},{8,0},{9,1},{10,... | collective-permute-start | bytes 294920 | tf_op jit(solution)/shard_map/ppermute | solution.py:494
  89.0 4.9 %collective-permute-start.28 = (f32[2,2,3,32,128]{4,3,2,1,0:T(8,128)S(1)}, f32[2,2,3,32,128]{4,3,2,1,0:T(8,128)S(1)}, u32[]{:S(2)}, u32[]{:S(2)}) collective-permute-start(f32[2,2,3,32,128]{4,3,2,1,0:T(8,128)S(1)} %bitcast.32), channel_id=1, source_target_pairs={{0,1},{1,0},{2,6},{3,7},{4,5},{5,4},{6,2},{7,3},{8,9},{9,8},{10,14... | collective-permute-start | bytes 589832 | tf_op jit(solution)/shard_map/ppermute | solution.py:494
  93.9 7.0 %collective-permute-start.29 = (f32[4,2,3,32,128]{4,3,2,1,0:T(8,128)S(1)}, f32[4,2,3,32,128]{4,3,2,1,0:T(8,128)S(1)}, u32[]{:S(2)}, u32[]{:S(2)}) collective-permute-start(f32[4,2,3,32,128]{4,3,2,1,0:T(8,128)S(1)} %bitcast.29), channel_id=1, source_target_pairs={{0,4},{1,5},{2,10},{3,11},{4,0},{5,1},{6,14},{7,15},{8,12},{9,13},... | collective-permute-start | bytes 1179656 | tf_op jit(solution)/shard_map/ppermute | solution.py:494
  (5 other events, 21.7 us)

commit v4 on v3

--- a/solution.py
+++ b/solution.py
@@ -176,7 +176,15 @@
     ins, outs, (scratch, sems) = refs[:count], refs[count:-2], refs[-2:]
     fetch([(ref.at[group], scratch.at[at]) for at, ref in enumerate(ins)], sems)
     for index in range(count):
-        outs[index // 2][index % 2] = scratch[index].astype(F32)
+        value = scratch[index].astype(F32)
+        outs[index // 2][index % 2] = value
+        if 2 * len(outs) > count:
+            outs[-1][index] = value
+
+
+def part_kernel(in_ref, *out_refs):
+    for at, ref in enumerate(out_refs):
+        ref[...] = in_ref[2 * at : 2 * at + 2]
 
 
 def weights_kernel(tok_count, *refs):
@@ -260,6 +268,12 @@
     out_ref[...] = total
     for ref in tail_refs:
         ref[...] = total[total.shape[0] - ref.shape[0] :]
+
+
+def carry_kernel(mine_ref, recv_ref, *refs):
+    refs[-1][:2] = mine_ref[...] + recv_ref[...]
+    if len(refs) == 2:
+        refs[1][2:] = refs[0][...]
 
 
 def key_kernel(scale, share, order, *refs):
@@ -419,19 +433,17 @@
     pl.when(jnp.logical_not(stays))(functools.partial(put, give_ref, keep_ref))
 
 
-def tokens_out_kernel(tok_count, *refs):
-    key_ref, value_ref = refs[-2:]
+def tokens_out_kernel(tok_count, own_ref, moved_ref, key_ref, value_ref):
     stays = working(tok_count)
-    ins = refs[:-2]
-    groups = len(ins) // 2
-    for index in range(groups):
-
-        def put(source):
-            key_ref[index] = source[0].astype(key_ref.dtype)
-            value_ref[index] = source[1].astype(value_ref.dtype)
-
-        pl.when(stays)(functools.partial(put, ins[2 * index]))
-        pl.when(jnp.logical_not(stays))(functools.partial(put, ins[2 * index + 1]))
+    groups = own_ref.shape[0] // 2
+
+    def put(source):
+        for index in range(groups):
+            key_ref[index] = source[2 * index].astype(key_ref.dtype)
+            value_ref[index] = source[2 * index + 1].astype(value_ref.dtype)
+
+    pl.when(stays)(functools.partial(put, own_ref))
+    pl.when(jnp.logical_not(stays))(functools.partial(put, moved_ref))
     key_ref[groups] = jnp.zeros_like(key_ref[groups])
     value_ref[groups] = jnp.zeros_like(value_ref[groups])
 
@@ -535,10 +547,11 @@
     init = fast_init.reshape(3, dim, dim)
     steps = updates.reshape(groups - 1, 3, dim, dim)
 
-    def send(arrays, index, limit=16):
+    def send(arrays, index, limit=16, whole=False):
+        outs = [shape(2, count, dim)] * (len(arrays) // 2)
         return call(
             functools.partial(send_kernel, index, len(arrays)),
-            [shape(2, count, dim)] * (len(arrays) // 2),
+            outs + [shape(len(arrays), count, dim)] * whole,
             *arrays,
             limit=limit,
             in_specs=[pl.BlockSpec(memory_space=pltpu.HBM)] * len(arrays),
@@ -575,6 +588,9 @@
 
     def tokens(index, after):
         arrays = []
+        if not isinstance(first[index], list):
+            pairs = [shape(2, count, dim)] * len(own[index])
+            first[index] = call(part_kernel, pairs, first[index])
         for mine, arrived in zip(own[index], first[index]):
             arrays += [mine, arrived, sibling(tie(arrived, after), True)]
         return arrays
@@ -595,15 +611,20 @@
     )
     factors = list(weights[top:])
     weights = [*weights[:top], top_weights]
-    token_grads = {}
+    token_grads = []
     for index in reversed(range(top)):
-        own[index] = send([q_all, c_all, k_all, v_all], index)
-        first[index] = [spread(tie(array, first[index + 1])) for array in own[index]]
+        one = index == 0
+        own[index] = send([q_all, c_all, k_all, v_all], index, whole=one)
+        if one:
+            *own[index], whole = own[index]
+            first[index] = spread(tie(whole, first[index + 1]))
+        else:
+            first[index] = [spread(tie(array, first[index + 1])) for array in own[index]]
         for at in range(len(tok_dims)):
             arrived = meet(payload, (tok_dims[at], tok_dims[at - 1]))
             if at + 1 < len(tok_dims):
-                if at == 0 and index + 1 in token_grads:
-                    arrived = tie(arrived, token_grads[index + 1])
+                if at == 0 and token_grads:
+                    arrived = tie(arrived, (token_grads[-1], first[index]))
                 (payload,) = call(add_kernel, [shape(rows + PAD, half)], payload, arrived)
         grad, coef, keyed = call(
             functools.partial(pre_kernel, tok_count),
@@ -616,7 +637,7 @@
         if index > 0:
             out_shapes, order = [shape(rows + PAD, half)], None
         else:
-            dims = tok_dims[:1] + vid_dims + tok_dims[1:]
+            dims = tok_dims + vid_dims
             rs_orders = [dims, dims[-1:] + dims[:-1]]
             order = [rs_orders[0][0], rs_orders[1][0]]
             out_shapes = [shape(3, half, half)] * 2
@@ -642,17 +663,17 @@
             weights[index],
             upper,
         )
-        (d_tokens,) = call(add_kernel, [shape(2, count, dim)], keep, sibling(give))
-        token_grads[index] = d_tokens
+        done = 2 * (top - index)
+        (d_tokens,) = call(
+            carry_kernel, [shape(done, count, dim)], keep, sibling(give), *token_grads[-1:]
+        )
+        token_grads.append(d_tokens)
 
     kept, sends = outs
-    returned = {index: swap(token_grads[index]) for index in range(top)}
+    returned = swap(token_grads[-1])
 
     def wait(array, point):
-        for index in range(top):
-            if point == (4,0)[min(index, 1)]:
-                array = tie(array, returned[index])
-        return array
+        return tie(array, returned) if point == 5 else array
 
     for at in range(len(dims)):
         arrived = meet(sends, [order[at] for order in rs_orders])
@@ -680,13 +701,11 @@
         block,
         arrived,
     )
-    arrays = []
-    for index in range(top):
-        arrays += [token_grads[index], returned[index]]
     key_grad, value_grad = call(
         functools.partial(tokens_out_kernel, tok_count),
         [shape(groups, count, dim, dtype=BF16)] * 2,
-        *arrays,
+        token_grads[-1],
+        returned,
     )
     back = lambda array: array.reshape(queries.shape)
     return back(query_grad), back(key_grad), back(value_grad), init_grad.reshape(fast_init.shape)

time: 104 us -> 101 us (0.971)
  starting transfers between devices: 41.6 us -> 37.3 us
  waiting for transfers between devices: 44.3 us -> 46.2 us
    ppermute x30 -> x28, starting transfers between devices: 41.6 us -> 37.3 us  [permute(): return lax.ppermute(array, ('tok', 'head', 'vid'), pairs)]
    ppermute x30 -> x28, waiting for transfers between devices: 44.3 us -> 46.2 us  [permute(): return lax.ppermute(array, ('tok', 'head', 'vid'), pairs)]
    pallas_call x29 -> x30, Pallas kernels: 12.8 us -> 12.9 us  [call(): pl.pallas_call(kernel, out_shape=outs, **kwargs, scratch_shapes=scratch,...]
  transfers between devices with their start and end apart: 30 -> 28, of which waited for: 14 -> 15; matrix products, arithmetic and copies ran while one was open for 0% -> 0% of each run, Pallas kernels for 9% -> 9%
where the time goes in v4:
time: 101 us; the launch traced here: 99.5 us
  waiting for transfers between devices  46.2 us (46%)
  starting transfers between devices  37.3 us (37%)
  Pallas kernels  12.9 us (13%)
  local copies, waits for them, and re-layouts  2.15 us (2%)
    ppermute x28, waiting for transfers between devices, permute(): return lax.ppermute(array, ('tok', 'head', 'vid'), pairs)  46.2 us
    ppermute x28, starting transfers between devices, permute(): return lax.ppermute(array, ('tok', 'head', 'vid'), pairs)  37.3 us
    pallas_call x30, Pallas kernels, call(): pl.pallas_call(kernel, out_shape=outs, **kwargs, scratch_shapes=scratch,...  12.9 us
    unnamed x14, local copies, waits for them, and re-layouts  2.15 us
  transfers between devices with their start and end apart: 28, of which 15 were waited for; matrix products, arithmetic and copies ran while one was open for 0% of the time, Pallas kernels for 9%

profile of v4, /device:TPU:1, one launch (start us, length us, event | category | flops | bytes accessed | tf_op | source)
XLA Modules:
  0.0 99.5 jit_solution(10872313891988006029)
XLA Ops:
  0.7 1.7 %shard_map.93.refs_0_ = f32[2,128,256]{2,1,0:T(8,128)} custom-call(bf16[3,128,256]{2,1,0:T(8,128)(2,1)} %bitcast.19, bf16[3,128,256]{2,1,0:T(8,128)(2,1)} %bitcast.23), custom_call_target="tpu_custom_call" | custom-call | flops 1 | bytes 1 | tf_op jit(solution)/shard_map/pallas_call | solution.py:452
  2.3 3.2 %collective-permute-start = (f32[2,128,256]{2,1,0:T(8,128)}, f32[2,128,256]{2,1,0:T(8,128)S(1)}, u32[]{:S(2)}, u32[]{:S(2)}) collective-permute-start(f32[2,128,256]{2,1,0:T(8,128)} %shard_map.93.refs_0_), channel_id=1, source_target_pairs={{0,2},{1,3},{2,18},{3,19},{4,6},{5,7},{6,22},{7,23},{8,10},{9,11},... | collective-permute-start | bytes 786440 | tf_op jit(solution)/shard_map/ppermute | solution.py:506
  6.5 1.1 %copy-done.4 = bf16[1,2,1,3,256,256]{5,4,3,2,1,0:T(8,128)(2,1)S(1)} copy-done((bf16[1,2,1,3,256,256]{5,4,3,2,1,0:T(8,128)(2,1)S(1)}, bf16[1,2,1,3,256,256]{5,4,3,2,1,0:T(8,128)(2,1)}, u32[]{:S(2)}) %copy-start.4) | copy-done | bytes 786456
  7.6 1.3 %shard_map.94 = (f32[2,3,256,256]{3,2,1,0:T(8,128)S(1)}, f32[768,128]{1,0:T(8,128)S(1)}, f32[1560,128]{1,0:T(8,128)S(1)}, f32[768,128]{1,0:T(8,128)S(1)}, f32[1560,128]{1,0:T(8,128)S(1)}) custom-call(bf16[3,256,256]{2,1,0:T(8,128)(2,1)S(1)} %bitcast.27, bf16[2,3,256,256]{3,2,1,0:T(8,128)(2,1)S(1)} %bitcast.31), custom_call_target="tpu_custom_call" | custom-call | flops 1 | bytes 1 | tf_op jit(solution)/shard_map/pallas_call | solution.py:452
  9.1 1.9 %shard_map.95 = bf16[3,128,256]{2,1,0:T(8,128)(2,1)} custom-call(bf16[3,128,256]{2,1,0:T(8,128)(2,1)S(1)} %bitcast.20, bf16[3,128,256]{2,1,0:T(8,128)(2,1)S(1)} %bitcast.24, bf16[3,256,256]{2,1,0:T(8,128)(2,1)S(1)} %bitcast.28, f32[2,3,256,256]{3,2,1,0:T(8,128)S(1)} %get-tuple-element.60.full_ref), custom_call_target="tpu_custom_call" | custom-call | flops 1 | bytes 1 | tf_op jit(solution)/shard_map/pallas_call | solution.py:452
  11.0 1.4 %collective-permute-start.1 = (f32[2,128,256]{2,1,0:T(8,128)S(1)}, f32[2,128,256]{2,1,0:T(8,128)S(1)}, u32[]{:S(2)}, u32[]{:S(2)}) collective-permute-start(f32[2,128,256]{2,1,0:T(8,128)S(1)} %collective-permute-done.refs_1_), channel_id=1, source_target_pairs={{0,2},{1,3},{4,6},{5,7},{8,10},{9,11},{12,14},{13,15},{18,16},{19,... | collective-permute-start | bytes 786440 | tf_op jit(solution)/shard_map/ppermute | solution.py:506
  12.5 2.8 %collective-permute-start.10 = (f32[1560,128]{1,0:T(8,128)S(1)}, f32[1560,128]{1,0:T(8,128)S(1)}, u32[]{:S(2)}, u32[]{:S(2)}) collective-permute-start(f32[1560,128]{1,0:T(8,128)S(1)} %get-tuple-element.74), channel_id=1, source_target_pairs={{0,2},{1,3},{2,0},{3,1},{4,6},{5,7},{6,4},{7,5},{8,10},{9,11},{10,... | collective-permute-start | bytes 2396168 | tf_op jit(solution)/shard_map/ppermute | solution.py:506
  17.7 1.8 %collective-permute-start.6 = (f32[2,128,256]{2,1,0:T(8,128)S(1)}, f32[2,128,256]{2,1,0:T(8,128)S(1)}, u32[]{:S(2)}, u32[]{:S(2)}) collective-permute-start(f32[2,128,256]{2,1,0:T(8,128)S(1)} %get-tuple-element.67.refs_0_), channel_id=1, source_target_pairs={{0,2},{1,3},{2,18},{3,19},{4,6},{5,7},{6,22},{7,23},{8,10},{9,11},... | collective-permute-start | bytes 786440 | tf_op jit(solution)/shard_map/ppermute | solution.py:506
  19.6 4.6 %collective-permute-done.3.recv_ref = f32[776,128]{1,0:T(8,128)S(1)} collective-permute-done((f32[776,128]{1,0:T(8,128)S(1)}, f32[776,128]{1,0:T(8,128)S(1)}, u32[]{:S(2)}, u32[]{:S(2)}) %collective-permute-start.3) | collective-permute-done | bytes 397344 | tf_op jit(solution)/shard_map/ppermute | solution.py:506
  24.3 3.4 %collective-permute-start.4 = (f32[776,128]{1,0:T(8,128)S(1)}, f32[776,128]{1,0:T(8,128)S(1)}, u32[]{:S(2)}, u32[]{:S(2)}) collective-permute-start(f32[776,128]{1,0:T(8,128)S(1)} %shard_map.98.mine_ref), channel_id=1, source_target_pairs={{0,8},{1,9},{2,6},{3,7},{4,12},{5,13},{6,2},{7,3},{8,0},{9,1},{10,... | collective-permute-start | bytes 1191944 | tf_op jit(solution)/shard_map/ppermute | solution.py:506
  27.7 1.3 %collective-permute-start.7 = (f32[2,128,256]{2,1,0:T(8,128)S(1)}, f32[2,128,256]{2,1,0:T(8,128)S(1)}, u32[]{:S(2)}, u32[]{:S(2)}) collective-permute-start(f32[2,128,256]{2,1,0:T(8,128)S(1)} %collective-permute-done.6.refs_1_), channel_id=1, source_target_pairs={{0,2},{1,3},{4,6},{5,7},{8,10},{9,11},{12,14},{13,15},{18,16},{19,... | collective-permute-start | bytes 786440 | tf_op jit(solution)/shard_map/ppermute | solution.py:506
  29.0 1.3 %collective-permute-start.9 = (f32[2,128,256]{2,1,0:T(8,128)S(1)}, f32[2,128,256]{2,1,0:T(8,128)S(1)}, u32[]{:S(2)}, u32[]{:S(2)}) collective-permute-start(f32[2,128,256]{2,1,0:T(8,128)S(1)} %collective-permute-done.8.refs_4_), channel_id=1, source_target_pairs={{0,2},{1,3},{4,6},{5,7},{8,10},{9,11},{12,14},{13,15},{18,16},{19,... | collective-permute-start | bytes 786440 | tf_op jit(solution)/shard_map/ppermute | solution.py:506
  30.8 5.9 %collective-permute-start.13 = (f32[4,128,256]{2,1,0:T(8,128)S(1)}, f32[4,128,256]{2,1,0:T(8,128)S(1)}, u32[]{:S(2)}, u32[]{:S(2)}) collective-permute-start(f32[4,128,256]{2,1,0:T(8,128)S(1)} %get-tuple-element.86), channel_id=1, source_target_pairs={{0,2},{1,3},{2,18},{3,19},{4,6},{5,7},{6,22},{7,23},{8,10},{9,11},... | collective-permute-start | bytes 1572872 | tf_op jit(solution)/shard_map/ppermute | solution.py:506
  40.6 1.2 %collective-permute-done.12.recv_ref = f32[2,128,256]{2,1,0:T(8,128)S(1)} collective-permute-done((f32[2,128,256]{2,1,0:T(8,128)S(1)}, f32[2,128,256]{2,1,0:T(8,128)S(1)}, u32[]{:S(2)}, u32[]{:S(2)}) %collective-permute-start.12) | collective-permute-done | bytes 262176 | tf_op jit(solution)/shard_map/ppermute | solution.py:506
  42.8 8.5 %collective-permute-done.11.recv_ref = f32[776,128]{1,0:T(8,128)S(1)} collective-permute-done((f32[776,128]{1,0:T(8,128)S(1)}, f32[776,128]{1,0:T(8,128)S(1)}, u32[]{:S(2)}, u32[]{:S(2)}) %collective-permute-start.11) | collective-permute-done | bytes 397344 | tf_op jit(solution)/shard_map/ppermute | solution.py:506
  51.8 1.3 %collective-permute-start.17 = (f32[2,128,256]{2,1,0:T(8,128)S(1)}, f32[2,128,256]{2,1,0:T(8,128)S(1)}, u32[]{:S(2)}, u32[]{:S(2)}) collective-permute-start(f32[2,128,256]{2,1,0:T(8,128)S(1)} %get-tuple-element.95.refs_4_), channel_id=1, source_target_pairs={{0,2},{1,3},{4,6},{5,7},{8,10},{9,11},{12,14},{13,15},{18,16},{19,... | collective-permute-start | bytes 786440 | tf_op jit(solution)/shard_map/ppermute | solution.py:506
  53.1 1.3 %collective-permute-start.16 = (f32[2,128,256]{2,1,0:T(8,128)S(1)}, f32[2,128,256]{2,1,0:T(8,128)S(1)}, u32[]{:S(2)}, u32[]{:S(2)}) collective-permute-start(f32[2,128,256]{2,1,0:T(8,128)S(1)} %get-tuple-element.92.refs_1_), channel_id=1, source_target_pairs={{0,2},{1,3},{4,6},{5,7},{8,10},{9,11},{12,14},{13,15},{18,16},{19,... | collective-permute-start | bytes 786440 | tf_op jit(solution)/shard_map/ppermute | solution.py:506
  54.4 3.7 %collective-permute-done.14.recv_ref = f32[776,128]{1,0:T(8,128)S(1)} collective-permute-done((f32[776,128]{1,0:T(8,128)S(1)}, f32[776,128]{1,0:T(8,128)S(1)}, u32[]{:S(2)}, u32[]{:S(2)}) %collective-permute-start.14) | collective-permute-done | bytes 397344 | tf_op jit(solution)/shard_map/ppermute | solution.py:506
  60.2 1.6 %collective-permute-start.20 = (f32[3,128,128]{2,1,0:T(8,128)S(1)}, f32[3,128,128]{2,1,0:T(8,128)S(1)}, u32[]{:S(2)}, u32[]{:S(2)}) collective-permute-start(f32[3,128,128]{2,1,0:T(8,128)S(1)} %get-tuple-element.108), channel_id=1, source_target_pairs={{0,4},{1,5},{2,3},{3,2},{4,0},{5,1},{6,7},{7,6},{8,12},{9,13},{10,... | collective-permute-start | bytes 589832 | tf_op jit(solution)/shard_map/ppermute | solution.py:506
  62.4 2.7 %collective-permute-done.20.recv_ref = f32[3,128,128]{2,1,0:T(8,128)S(1)} collective-permute-done((f32[3,128,128]{2,1,0:T(8,128)S(1)}, f32[3,128,128]{2,1,0:T(8,128)S(1)}, u32[]{:S(2)}, u32[]{:S(2)}) %collective-permute-start.20) | collective-permute-done | bytes 196640 | tf_op jit(solution)/shard_map/ppermute | solution.py:506
  65.6 3.0 %collective-permute-start.19 = (f32[4,128,256]{2,1,0:T(8,128)S(1)}, f32[4,128,256]{2,1,0:T(8,128)S(1)}, u32[]{:S(2)}, u32[]{:S(2)}) collective-permute-start(f32[4,128,256]{2,1,0:T(8,128)S(1)} %shard_map.113.own_ref), channel_id=1, source_target_pairs={{2,16},{3,17},{6,20},{7,21},{10,24},{11,25},{14,28},{15,29},{16,2}... | collective-permute-start | bytes 1572872 | tf_op jit(solution)/shard_map/ppermute | solution.py:506
  68.9 6.4 %collective-permute-done.22.recv_ref = f32[3,32,128]{2,1,0:T(8,128)S(1)} collective-permute-done((f32[3,32,128]{2,1,0:T(8,128)S(1)}, f32[3,32,128]{2,1,0:T(8,128)S(1)}, u32[]{:S(2)}, u32[]{:S(2)}) %collective-permute-start.22) | collective-permute-done | bytes 49184 | tf_op jit(solution)/shard_map/ppermute | solution.py:506
  75.4 1.2 %collective-permute-done.23.other_ref = f32[3,32,128]{2,1,0:T(8,128)S(1)} collective-permute-done((f32[3,32,128]{2,1,0:T(8,128)S(1)}, f32[3,32,128]{2,1,0:T(8,128)S(1)}, u32[]{:S(2)}, u32[]{:S(2)}) %collective-permute-start.23) | collective-permute-done | bytes 49184 | tf_op jit(solution)/shard_map/ppermute | solution.py:506
  76.6 1.3 %collective-permute-start.24 = (f32[2,3,32,128]{3,2,1,0:T(8,128)S(1)}, f32[2,3,32,128]{3,2,1,0:T(8,128)S(1)}, u32[]{:S(2)}, u32[]{:S(2)}) collective-permute-start(f32[2,3,32,128]{3,2,1,0:T(8,128)S(1)} %shard_map.118.own_ref), channel_id=1, source_target_pairs={{0,16},{1,17},{4,20},{5,21},{8,24},{9,25},{12,28},{13,29},{18,2},{... | collective-permute-start | bytes 294920 | tf_op jit(solution)/shard_map/ppermute | solution.py:506
  77.9 5.3 %collective-permute-done.24.moved_ref = f32[2,3,32,128]{3,2,1,0:T(8,128)S(1)} collective-permute-done((f32[2,3,32,128]{3,2,1,0:T(8,128)S(1)}, f32[2,3,32,128]{3,2,1,0:T(8,128)S(1)}, u32[]{:S(2)}, u32[]{:S(2)}) %collective-permute-start.24) | collective-permute-done | bytes 98336 | tf_op jit(solution)/shard_map/ppermute | solution.py:506
  83.2 1.7 %collective-permute-start.25 = (f32[1,2,3,32,128]{4,3,2,1,0:T(8,128)S(1)}, f32[1,2,3,32,128]{4,3,2,1,0:T(8,128)S(1)}, u32[]{:S(2)}, u32[]{:S(2)}) collective-permute-start(f32[1,2,3,32,128]{4,3,2,1,0:T(8,128)S(1)} %bitcast.38), channel_id=1, source_target_pairs={{0,1},{1,0},{2,10},{3,11},{4,5},{5,4},{6,14},{7,15},{8,9},{9,8},{1... | collective-permute-start | bytes 294920 | tf_op jit(solution)/shard_map/ppermute | solution.py:506
  84.9 2.0 %collective-permute-done.25.other_ref = f32[1,2,3,32,128]{4,3,2,1,0:T(8,128)S(1)} collective-permute-done((f32[1,2,3,32,128]{4,3,2,1,0:T(8,128)S(1)}, f32[1,2,3,32,128]{4,3,2,1,0:T(8,128)S(1)}, u32[]{:S(2)}, u32[]{:S(2)}) %collective-permute-start.25) | collective-permute-done | bytes 98336 | tf_op jit(solution)/shard_map/ppermute | solution.py:506
  86.9 1.3 %collective-permute-start.26 = (f32[2,2,3,32,128]{4,3,2,1,0:T(8,128)S(1)}, f32[2,2,3,32,128]{4,3,2,1,0:T(8,128)S(1)}, u32[]{:S(2)}, u32[]{:S(2)}) collective-permute-start(f32[2,2,3,32,128]{4,3,2,1,0:T(8,128)S(1)} %bitcast.32), channel_id=1, source_target_pairs={{0,8},{1,9},{2,6},{3,7},{4,12},{5,13},{6,2},{7,3},{8,0},{9,1},{10,... | collective-permute-start | bytes 589832 | tf_op jit(solution)/shard_map/ppermute | solution.py:506
  88.2 3.3 %collective-permute-done.26.other_ref = f32[2,2,3,32,128]{4,3,2,1,0:T(8,128)S(1)} collective-permute-done((f32[2,2,3,32,128]{4,3,2,1,0:T(8,128)S(1)}, f32[2,2,3,32,128]{4,3,2,1,0:T(8,128)S(1)}, u32[]{:S(2)}, u32[]{:S(2)}) %collective-permute-start.26) | collective-permute-done | bytes 196640 | tf_op jit(solution)/shard_map/ppermute | solution.py:506
  91.5 1.3 %collective-permute-start.27 = (f32[4,2,3,32,128]{4,3,2,1,0:T(8,128)S(1)}, f32[4,2,3,32,128]{4,3,2,1,0:T(8,128)S(1)}, u32[]{:S(2)}, u32[]{:S(2)}) collective-permute-start(f32[4,2,3,32,128]{4,3,2,1,0:T(8,128)S(1)} %bitcast.29), channel_id=1, source_target_pairs={{0,4},{1,5},{2,3},{3,2},{4,0},{5,1},{6,7},{7,6},{8,12},{9,13},{10,... | collective-permute-start | bytes 1179656 | tf_op jit(solution)/shard_map/ppermute | solution.py:506
  93.6 4.9 %collective-permute-done.27.recv_ref = f32[4,2,3,32,128]{4,3,2,1,0:T(8,128)S(1)} collective-permute-done((f32[4,2,3,32,128]{4,3,2,1,0:T(8,128)S(1)}, f32[4,2,3,32,128]{4,3,2,1,0:T(8,128)S(1)}, u32[]{:S(2)}, u32[]{:S(2)}) %collective-permute-start.27) | collective-permute-done | bytes 393248 | tf_op jit(solution)/shard_map/ppermute | solution.py:506
  98.5 1.0 %shard_map.122 = f32[3,256,256]{2,1,0:T(8,128)} custom-call(f32[4,2,3,32,128]{4,3,2,1,0:T(8,128)S(1)} %bitcast.30, f32[4,2,3,32,128]{4,3,2,1,0:T(8,128)S(1)} %collective-permute-done.27.recv_ref), custom_call_target="tpu_custom_call" | custom-call | flops 1 | bytes 1 | tf_op jit(solution)/shard_map/pallas_call | solution.py:452
  (68 shorter events, 13.8 us)
Async XLA Ops:
  0.6 8.4 %copy-start = (bf16[1,3,128,1,256]{4,2,3,1,0:T(8,128)(2,1)S(1)}, bf16[1,3,128,1,256]{4,2,3,1,0:T(8,128)(2,1)}, u32[]{:S(2)}) copy-start(bf16[1,3,128,1,256]{4,2,3,1,0:T(8,128)(2,1)} %param.6) | copy-start | bytes 589828
  0.6 8.4 %copy-start.1 = (bf16[1,3,128,1,256]{4,2,3,1,0:T(8,128)(2,1)S(1)}, bf16[1,3,128,1,256]{4,2,3,1,0:T(8,128)(2,1)}, u32[]{:S(2)}) copy-start(bf16[1,3,128,1,256]{4,2,3,1,0:T(8,128)(2,1)} %param.9) | copy-start | bytes 589828
  2.3 8.7 %collective-permute-start = (f32[2,128,256]{2,1,0:T(8,128)}, f32[2,128,256]{2,1,0:T(8,128)S(1)}, u32[]{:S(2)}, u32[]{:S(2)}) collective-permute-start(f32[2,128,256]{2,1,0:T(8,128)} %shard_map.93.refs_0_), channel_id=1, source_target_pairs={{0,2},{1,3},{2,18},{3,19},{4,6},{5,7},{6,22},{7,23},{8,10},{9,11},... | collective-permute-start | bytes 786440 | tf_op jit(solution)/shard_map/ppermute | solution.py:506
  9.0 6.2 %collective-permute-start.2 = (f32[768,128]{1,0:T(8,128)S(1)}, f32[768,128]{1,0:T(8,128)S(1)}, u32[]{:S(2)}, u32[]{:S(2)}) collective-permute-start(f32[768,128]{1,0:T(8,128)S(1)} %get-tuple-element.63), channel_id=1, source_target_pairs={{0,2},{1,3},{2,0},{3,1},{4,6},{5,7},{6,4},{7,5},{8,10},{9,11},{10,... | collective-permute-start | bytes 1179656 | tf_op jit(solution)/shard_map/ppermute | solution.py:506
  9.1 7.1 %copy-start.3 = (f32[2,128,256]{2,1,0:T(8,128)S(1)}, f32[2,128,256]{2,1,0:T(8,128)}, u32[]{:S(2)}) copy-start(f32[2,128,256]{2,1,0:T(8,128)} %shard_map.93.refs_0_) | copy-start | bytes 786436
  11.0 6.2 %copy-start.6 = (bf16[1,3,128,1,256]{4,2,3,1,0:T(8,128)(2,1)S(1)}, bf16[1,3,128,1,256]{4,2,3,1,0:T(8,128)(2,1)}, u32[]{:S(2)}) copy-start(bf16[1,3,128,1,256]{4,2,3,1,0:T(8,128)(2,1)} %param.8) | copy-start | bytes 589828
  11.0 5.1 %collective-permute-start.1 = (f32[2,128,256]{2,1,0:T(8,128)S(1)}, f32[2,128,256]{2,1,0:T(8,128)S(1)}, u32[]{:S(2)}, u32[]{:S(2)}) collective-permute-start(f32[2,128,256]{2,1,0:T(8,128)S(1)} %collective-permute-done.refs_1_), channel_id=1, source_target_pairs={{0,2},{1,3},{4,6},{5,7},{8,10},{9,11},{12,14},{13,15},{18,16},{19,... | collective-permute-start | bytes 786440 | tf_op jit(solution)/shard_map/ppermute | solution.py:506
  12.5 25.0 %collective-permute-start.10 = (f32[1560,128]{1,0:T(8,128)S(1)}, f32[1560,128]{1,0:T(8,128)S(1)}, u32[]{:S(2)}, u32[]{:S(2)}) collective-permute-start(f32[1560,128]{1,0:T(8,128)S(1)} %get-tuple-element.74), channel_id=1, source_target_pairs={{0,2},{1,3},{2,0},{3,1},{4,6},{5,7},{6,4},{7,5},{8,10},{9,11},{10,... | collective-permute-start | bytes 2396168 | tf_op jit(solution)/shard_map/ppermute | solution.py:506
  16.8 7.5 %collective-permute-start.3 = (f32[776,128]{1,0:T(8,128)S(1)}, f32[776,128]{1,0:T(8,128)S(1)}, u32[]{:S(2)}, u32[]{:S(2)}) collective-permute-start(f32[776,128]{1,0:T(8,128)S(1)} %shard_map.97.mine_ref), channel_id=1, source_target_pairs={{0,4},{1,5},{2,10},{3,11},{4,0},{5,1},{6,14},{7,15},{8,12},{9,13},... | collective-permute-start | bytes 1191944 | tf_op jit(solution)/shard_map/ppermute | solution.py:506
  17.7 10.0 %collective-permute-start.6 = (f32[2,128,256]{2,1,0:T(8,128)S(1)}, f32[2,128,256]{2,1,0:T(8,128)S(1)}, u32[]{:S(2)}, u32[]{:S(2)}) collective-permute-start(f32[2,128,256]{2,1,0:T(8,128)S(1)} %get-tuple-element.67.refs_0_), channel_id=1, source_target_pairs={{0,2},{1,3},{2,18},{3,19},{4,6},{5,7},{6,22},{7,23},{8,10},{9,11},... | collective-permute-start | bytes 786440 | tf_op jit(solution)/shard_map/ppermute | solution.py:506
  19.5 9.6 %collective-permute-start.8 = (f32[2,128,256]{2,1,0:T(8,128)S(1)}, f32[2,128,256]{2,1,0:T(8,128)S(1)}, u32[]{:S(2)}, u32[]{:S(2)}) collective-permute-start(f32[2,128,256]{2,1,0:T(8,128)S(1)} %get-tuple-element.70.refs_3_), channel_id=1, source_target_pairs={{0,2},{1,3},{2,18},{3,19},{4,6},{5,7},{6,22},{7,23},{8,10},{9,11},... | collective-permute-start | bytes 786440 | tf_op jit(solution)/shard_map/ppermute | solution.py:506
  24.3 12.3 %collective-permute-start.4 = (f32[776,128]{1,0:T(8,128)S(1)}, f32[776,128]{1,0:T(8,128)S(1)}, u32[]{:S(2)}, u32[]{:S(2)}) collective-permute-start(f32[776,128]{1,0:T(8,128)S(1)} %shard_map.98.mine_ref), channel_id=1, source_target_pairs={{0,8},{1,9},{2,6},{3,7},{4,12},{5,13},{6,2},{7,3},{8,0},{9,1},{10,... | collective-permute-start | bytes 1191944 | tf_op jit(solution)/shard_map/ppermute | solution.py:506
  27.7 9.8 %collective-permute-start.7 = (f32[2,128,256]{2,1,0:T(8,128)S(1)}, f32[2,128,256]{2,1,0:T(8,128)S(1)}, u32[]{:S(2)}, u32[]{:S(2)}) collective-permute-start(f32[2,128,256]{2,1,0:T(8,128)S(1)} %collective-permute-done.6.refs_1_), channel_id=1, source_target_pairs={{0,2},{1,3},{4,6},{5,7},{8,10},{9,11},{12,14},{13,15},{18,16},{19,... | collective-permute-start | bytes 786440 | tf_op jit(solution)/shard_map/ppermute | solution.py:506
  29.0 8.5 %collective-permute-start.9 = (f32[2,128,256]{2,1,0:T(8,128)S(1)}, f32[2,128,256]{2,1,0:T(8,128)S(1)}, u32[]{:S(2)}, u32[]{:S(2)}) collective-permute-start(f32[2,128,256]{2,1,0:T(8,128)S(1)} %collective-permute-done.8.refs_4_), channel_id=1, source_target_pairs={{0,2},{1,3},{4,6},{5,7},{8,10},{9,11},{12,14},{13,15},{18,16},{19,... | collective-permute-start | bytes 786440 | tf_op jit(solution)/shard_map/ppermute | solution.py:506
  30.8 12.1 %collective-permute-start.13 = (f32[4,128,256]{2,1,0:T(8,128)S(1)}, f32[4,128,256]{2,1,0:T(8,128)S(1)}, u32[]{:S(2)}, u32[]{:S(2)}) collective-permute-start(f32[4,128,256]{2,1,0:T(8,128)S(1)} %get-tuple-element.86), channel_id=1, source_target_pairs={{0,2},{1,3},{2,18},{3,19},{4,6},{5,7},{6,22},{7,23},{8,10},{9,11},... | collective-permute-start | bytes 1572872 | tf_op jit(solution)/shard_map/ppermute | solution.py:506
  36.7 1.7 %collective-permute-start.5 = (f32[8,128]{1,0:T(8,128)S(1)}, f32[8,128]{1,0:T(8,128)S(1)}, u32[]{:S(2)}, u32[]{:S(2)}) collective-permute-start(f32[8,128]{1,0:T(8,128)S(1)} %get-tuple-element.65.refs_1_), channel_id=1, source_target_pairs={{0,2},{1,3},{2,0},{3,1},{4,6},{5,7},{6,4},{7,5},{8,10},{9,11},{10,... | collective-permute-start | bytes 12296 | tf_op jit(solution)/shard_map/ppermute | solution.py:506
  39.1 12.3 %collective-permute-start.11 = (f32[776,128]{1,0:T(8,128)S(1)}, f32[776,128]{1,0:T(8,128)S(1)}, u32[]{:S(2)}, u32[]{:S(2)}) collective-permute-start(f32[776,128]{1,0:T(8,128)S(1)} %get-tuple-element.80.mine_ref), channel_id=1, source_target_pairs={{0,4},{1,5},{2,10},{3,11},{4,0},{5,1},{6,14},{7,15},{8,12},{9,13},... | collective-permute-start | bytes 1191944 | tf_op jit(solution)/shard_map/ppermute | solution.py:506
  39.7 2.0 %collective-permute-start.12 = (f32[2,128,256]{2,1,0:T(8,128)S(1)}, f32[2,128,256]{2,1,0:T(8,128)S(1)}, u32[]{:S(2)}, u32[]{:S(2)}) collective-permute-start(f32[2,128,256]{2,1,0:T(8,128)S(1)} %get-tuple-element.84), channel_id=1, source_target_pairs={{0,2},{1,3},{2,0},{3,1},{4,6},{5,7},{6,4},{7,5},{8,10},{9,11},{10,... | collective-permute-start | bytes 786440 | tf_op jit(solution)/shard_map/ppermute | solution.py:506
  51.4 6.7 %collective-permute-start.14 = (f32[776,128]{1,0:T(8,128)S(1)}, f32[776,128]{1,0:T(8,128)S(1)}, u32[]{:S(2)}, u32[]{:S(2)}) collective-permute-start(f32[776,128]{1,0:T(8,128)S(1)} %shard_map.107.mine_ref), channel_id=1, source_target_pairs={{0,8},{1,9},{2,6},{3,7},{4,12},{5,13},{6,2},{7,3},{8,0},{9,1},{10,... | collective-permute-start | bytes 1191944 | tf_op jit(solution)/shard_map/ppermute | solution.py:506
  51.8 6.5 %collective-permute-start.17 = (f32[2,128,256]{2,1,0:T(8,128)S(1)}, f32[2,128,256]{2,1,0:T(8,128)S(1)}, u32[]{:S(2)}, u32[]{:S(2)}) collective-permute-start(f32[2,128,256]{2,1,0:T(8,128)S(1)} %get-tuple-element.95.refs_4_), channel_id=1, source_target_pairs={{0,2},{1,3},{4,6},{5,7},{8,10},{9,11},{12,14},{13,15},{18,16},{19,... | collective-permute-start | bytes 786440 | tf_op jit(solution)/shard_map/ppermute | solution.py:506
  53.1 5.2 %collective-permute-start.16 = (f32[2,128,256]{2,1,0:T(8,128)S(1)}, f32[2,128,256]{2,1,0:T(8,128)S(1)}, u32[]{:S(2)}, u32[]{:S(2)}) collective-permute-start(f32[2,128,256]{2,1,0:T(8,128)S(1)} %get-tuple-element.92.refs_1_), channel_id=1, source_target_pairs={{0,2},{1,3},{4,6},{5,7},{8,10},{9,11},{12,14},{13,15},{18,16},{19,... | collective-permute-start | bytes 786440 | tf_op jit(solution)/shard_map/ppermute | solution.py:506
  58.2 1.2 %collective-permute-start.15 = (f32[8,128]{1,0:T(8,128)S(1)}, f32[8,128]{1,0:T(8,128)S(1)}, u32[]{:S(2)}, u32[]{:S(2)}) collective-permute-start(f32[8,128]{1,0:T(8,128)S(1)} %get-tuple-element.89.refs_1_), channel_id=1, source_target_pairs={{0,2},{1,3},{2,0},{3,1},{4,6},{5,7},{6,4},{7,5},{8,10},{9,11},{10,... | collective-permute-start | bytes 12296 | tf_op jit(solution)/shard_map/ppermute | solution.py:506
  60.2 5.0 %collective-permute-start.20 = (f32[3,128,128]{2,1,0:T(8,128)S(1)}, f32[3,128,128]{2,1,0:T(8,128)S(1)}, u32[]{:S(2)}, u32[]{:S(2)}) collective-permute-start(f32[3,128,128]{2,1,0:T(8,128)S(1)} %get-tuple-element.108), channel_id=1, source_target_pairs={{0,4},{1,5},{2,3},{3,2},{4,0},{5,1},{6,7},{7,6},{8,12},{9,13},{10,... | collective-permute-start | bytes 589832 | tf_op jit(solution)/shard_map/ppermute | solution.py:506
  62.4 3.2 %collective-permute-start.18 = (f32[2,128,256]{2,1,0:T(8,128)S(1)}, f32[2,128,256]{2,1,0:T(8,128)S(1)}, u32[]{:S(2)}, u32[]{:S(2)}) collective-permute-start(f32[2,128,256]{2,1,0:T(8,128)S(1)} %get-tuple-element.104), channel_id=1, source_target_pairs={{0,2},{1,3},{2,0},{3,1},{4,6},{5,7},{6,4},{7,5},{8,10},{9,11},{10,... | collective-permute-start | bytes 786440 | tf_op jit(solution)/shard_map/ppermute | solution.py:506
  65.2 3.5 %collective-permute-start.21 = (f32[3,64,128]{2,1,0:T(8,128)S(1)}, f32[3,64,128]{2,1,0:T(8,128)S(1)}, u32[]{:S(2)}, u32[]{:S(2)}) collective-permute-start(f32[3,64,128]{2,1,0:T(8,128)S(1)} %get-tuple-element.110), channel_id=1, source_target_pairs={{0,8},{1,9},{2,6},{3,7},{4,12},{5,13},{6,2},{7,3},{8,0},{9,1},{10,... | collective-permute-start | bytes 294920 | tf_op jit(solution)/shard_map/ppermute | solution.py:506
  65.6 22.5 %collective-permute-start.19 = (f32[4,128,256]{2,1,0:T(8,128)S(1)}, f32[4,128,256]{2,1,0:T(8,128)S(1)}, u32[]{:S(2)}, u32[]{:S(2)}) collective-permute-start(f32[4,128,256]{2,1,0:T(8,128)S(1)} %shard_map.113.own_ref), channel_id=1, source_target_pairs={{2,16},{3,17},{6,20},{7,21},{10,24},{11,25},{14,28},{15,29},{16,2}... | collective-permute-start | bytes 1572872 | tf_op jit(solution)/shard_map/ppermute | solution.py:506
  68.8 6.6 %collective-permute-start.22 = (f32[3,32,128]{2,1,0:T(8,128)S(1)}, f32[3,32,128]{2,1,0:T(8,128)S(1)}, u32[]{:S(2)}, u32[]{:S(2)}) collective-permute-start(f32[3,32,128]{2,1,0:T(8,128)S(1)} %get-tuple-element.112), channel_id=1, source_target_pairs={{0,1},{1,0},{2,10},{3,11},{4,5},{5,4},{6,14},{7,15},{8,9},{9,8},{1... | collective-permute-start | bytes 147464 | tf_op jit(solution)/shard_map/ppermute | solution.py:506
  75.3 1.2 %collective-permute-start.23 = (f32[3,32,128]{2,1,0:T(8,128)S(1)}, f32[3,32,128]{2,1,0:T(8,128)S(1)}, u32[]{:S(2)}, u32[]{:S(2)}) collective-permute-start(f32[3,32,128]{2,1,0:T(8,128)S(1)} %shard_map.117.mine_ref), channel_id=1, source_target_pairs={{0,2},{1,3},{2,0},{3,1},{4,6},{5,7},{6,4},{7,5},{8,10},{9,11},{10,... | collective-permute-start | bytes 147464 | tf_op jit(solution)/shard_map/ppermute | solution.py:506
  76.6 6.6 %collective-permute-start.24 = (f32[2,3,32,128]{3,2,1,0:T(8,128)S(1)}, f32[2,3,32,128]{3,2,1,0:T(8,128)S(1)}, u32[]{:S(2)}, u32[]{:S(2)}) collective-permute-start(f32[2,3,32,128]{3,2,1,0:T(8,128)S(1)} %shard_map.118.own_ref), channel_id=1, source_target_pairs={{0,16},{1,17},{4,20},{5,21},{8,24},{9,25},{12,28},{13,29},{18,2},{... | collective-permute-start | bytes 294920 | tf_op jit(solution)/shard_map/ppermute | solution.py:506
  83.2 3.7 %collective-permute-start.25 = (f32[1,2,3,32,128]{4,3,2,1,0:T(8,128)S(1)}, f32[1,2,3,32,128]{4,3,2,1,0:T(8,128)S(1)}, u32[]{:S(2)}, u32[]{:S(2)}) collective-permute-start(f32[1,2,3,32,128]{4,3,2,1,0:T(8,128)S(1)} %bitcast.38), channel_id=1, source_target_pairs={{0,1},{1,0},{2,10},{3,11},{4,5},{5,4},{6,14},{7,15},{8,9},{9,8},{1... | collective-permute-start | bytes 294920 | tf_op jit(solution)/shard_map/ppermute | solution.py:506
  86.9 4.6 %collective-permute-start.26 = (f32[2,2,3,32,128]{4,3,2,1,0:T(8,128)S(1)}, f32[2,2,3,32,128]{4,3,2,1,0:T(8,128)S(1)}, u32[]{:S(2)}, u32[]{:S(2)}) collective-permute-start(f32[2,2,3,32,128]{4,3,2,1,0:T(8,128)S(1)} %bitcast.32), channel_id=1, source_target_pairs={{0,8},{1,9},{2,6},{3,7},{4,12},{5,13},{6,2},{7,3},{8,0},{9,1},{10,... | collective-permute-start | bytes 589832 | tf_op jit(solution)/shard_map/ppermute | solution.py:506
  91.5 7.0 %collective-permute-start.27 = (f32[4,2,3,32,128]{4,3,2,1,0:T(8,128)S(1)}, f32[4,2,3,32,128]{4,3,2,1,0:T(8,128)S(1)}, u32[]{:S(2)}, u32[]{:S(2)}) collective-permute-start(f32[4,2,3,32,128]{4,3,2,1,0:T(8,128)S(1)} %bitcast.29), channel_id=1, source_target_pairs={{0,4},{1,5},{2,3},{3,2},{4,0},{5,1},{6,7},{7,6},{8,12},{9,13},{10,... | collective-permute-start | bytes 1179656 | tf_op jit(solution)/shard_map/ppermute | solution.py:506
  (3 other events, 8.4 us)

commit v5 on v4

--- a/solution.py
+++ b/solution.py
@@ -448,13 +448,13 @@
     value_ref[groups] = jnp.zeros_like(value_ref[groups])
 
 
-def call(kernel, outs, *args, scratch=(), limit=16, **kwargs):
+def call(kernel, outs, *args, scratch=(), limit=16, flops=1, **kwargs):
     return pl.pallas_call(
         kernel,
         out_shape=outs,
         **kwargs,
         scratch_shapes=scratch,
-        cost_estimate=pl.CostEstimate(flops=1, bytes_accessed=1, transcendentals=0),
+        cost_estimate=pl.CostEstimate(flops=flops, bytes_accessed=1, transcendentals=0),
         compiler_params=pltpu.CompilerParams(vmem_limit_bytes=limit * 1024 * 1024),
     )(*args)
 
@@ -590,7 +590,7 @@
         arrays = []
         if not isinstance(first[index], list):
             pairs = [shape(2, count, dim)] * len(own[index])
-            first[index] = call(part_kernel, pairs, first[index])
+            first[index] = call(part_kernel, pairs, first[index], flops=4000000000)
         for mine, arrived in zip(own[index], first[index]):
             arrays += [mine, arrived, sibling(tie(arrived, after), True)]
         return arrays
@@ -613,7 +613,7 @@
     weights = [*weights[:top], top_weights]
     token_grads = []
     for index in reversed(range(top)):
-        one = index == 0
+        one = True
         own[index] = send([q_all, c_all, k_all, v_all], index, whole=one)
         if one:
             *own[index], whole = own[index]
@@ -624,7 +624,7 @@
             arrived = meet(payload, (tok_dims[at], tok_dims[at - 1]))
             if at + 1 < len(tok_dims):
                 if at == 0 and token_grads:
-                    arrived = tie(arrived, (token_grads[-1], first[index]))
+                    arrived = tie(arrived, token_grads[-1])
                 (payload,) = call(add_kernel, [shape(rows + PAD, half)], payload, arrived)
         grad, coef, keyed = call(
             functools.partial(pre_kernel, tok_count),

time: 101 us -> 100 us (0.990)
  starting transfers between devices: 37.3 us -> 34.1 us
  waiting for transfers between devices: 46.2 us -> 48.8 us
    ppermute x28 -> x27, starting transfers between devices: 37.3 us -> 34.1 us  [permute(): return lax.ppermute(array, ('tok', 'head', 'vid'), pairs)]
    ppermute x28 -> x27, waiting for transfers between devices: 46.2 us -> 48.8 us  [permute(): return lax.ppermute(array, ('tok', 'head', 'vid'), pairs)]
    pallas_call x30 -> x31, Pallas kernels: 12.9 us -> 13.1 us  [call(): pl.pallas_call(kernel, out_shape=outs, **kwargs, scratch_shapes=scratch,...]
  transfers between devices with their start and end apart: 28 -> 27, of which waited for: 15 -> 15; matrix products, arithmetic and copies ran while one was open for 0% -> 0% of each run, Pallas kernels for 9% -> 10%
where the time goes in v5:
time: 100 us; the launch traced here: 99.1 us
  waiting for transfers between devices  48.8 us (49%)
  starting transfers between devices  34.1 us (34%)
  Pallas kernels  13.1 us (13%)
  local copies, waits for them, and re-layouts  2.15 us (2%)
  between operations  1 us (1%)
    ppermute x27, waiting for transfers between devices, permute(): return lax.ppermute(array, ('tok', 'head', 'vid'), pairs)  48.8 us
    ppermute x27, starting transfers between devices, permute(): return lax.ppermute(array, ('tok', 'head', 'vid'), pairs)  34.1 us
    pallas_call x31, Pallas kernels, call(): pl.pallas_call(kernel, out_shape=outs, **kwargs, scratch_shapes=scratch,...  13.1 us
    unnamed x14, local copies, waits for them, and re-layouts  2.15 us
  transfers between devices with their start and end apart: 27, of which 15 were waited for; matrix products, arithmetic and copies ran while one was open for 0% of the time, Pallas kernels for 10%

profile of v5, /device:TPU:1, one launch (start us, length us, event | category | flops | bytes accessed | tf_op | source)
XLA Modules:
  0.0 99.1 jit_solution(1142073253746526553)
XLA Ops:
  0.7 1.7 %shard_map.93.refs_0_ = f32[2,128,256]{2,1,0:T(8,128)} custom-call(bf16[3,128,256]{2,1,0:T(8,128)(2,1)} %bitcast.19, bf16[3,128,256]{2,1,0:T(8,128)(2,1)} %bitcast.23), custom_call_target="tpu_custom_call" | custom-call | flops 1 | bytes 1 | tf_op jit(solution)/shard_map/pallas_call | solution.py:452
  2.3 3.2 %collective-permute-start = (f32[2,128,256]{2,1,0:T(8,128)}, f32[2,128,256]{2,1,0:T(8,128)S(1)}, u32[]{:S(2)}, u32[]{:S(2)}) collective-permute-start(f32[2,128,256]{2,1,0:T(8,128)} %shard_map.93.refs_0_), channel_id=1, source_target_pairs={{0,2},{1,3},{2,18},{3,19},{4,6},{5,7},{6,22},{7,23},{8,10},{9,11},... | collective-permute-start | bytes 786440 | tf_op jit(solution)/shard_map/ppermute | solution.py:506
  7.6 1.3 %shard_map.94 = (f32[2,3,256,256]{3,2,1,0:T(8,128)S(1)}, f32[768,128]{1,0:T(8,128)S(1)}, f32[1560,128]{1,0:T(8,128)S(1)}, f32[768,128]{1,0:T(8,128)S(1)}, f32[1560,128]{1,0:T(8,128)S(1)}) custom-call(bf16[3,256,256]{2,1,0:T(8,128)(2,1)S(1)} %bitcast.27, bf16[2,3,256,256]{3,2,1,0:T(8,128)(2,1)S(1)} %bitcast.31), custom_call_target="tpu_custom_call" | custom-call | flops 1 | bytes 1 | tf_op jit(solution)/shard_map/pallas_call | solution.py:452
  9.1 1.9 %shard_map.95 = bf16[3,128,256]{2,1,0:T(8,128)(2,1)} custom-call(bf16[3,128,256]{2,1,0:T(8,128)(2,1)S(1)} %bitcast.20, bf16[3,128,256]{2,1,0:T(8,128)(2,1)S(1)} %bitcast.24, bf16[3,256,256]{2,1,0:T(8,128)(2,1)S(1)} %bitcast.28, f32[2,3,256,256]{3,2,1,0:T(8,128)S(1)} %get-tuple-element.62.full_ref), custom_call_target="tpu_custom_call" | custom-call | flops 1 | bytes 1 | tf_op jit(solution)/shard_map/pallas_call | solution.py:452
  11.0 1.4 %collective-permute-start.1 = (f32[2,128,256]{2,1,0:T(8,128)S(1)}, f32[2,128,256]{2,1,0:T(8,128)S(1)}, u32[]{:S(2)}, u32[]{:S(2)}) collective-permute-start(f32[2,128,256]{2,1,0:T(8,128)S(1)} %collective-permute-done.refs_1_), channel_id=1, source_target_pairs={{0,2},{1,3},{4,6},{5,7},{8,10},{9,11},{12,14},{13,15},{18,16},{19,... | collective-permute-start | bytes 786440 | tf_op jit(solution)/shard_map/ppermute | solution.py:506
  12.9 2.7 %collective-permute-start.6 = (f32[4,128,256]{2,1,0:T(8,128)S(1)}, f32[4,128,256]{2,1,0:T(8,128)S(1)}, u32[]{:S(2)}, u32[]{:S(2)}) collective-permute-start(f32[4,128,256]{2,1,0:T(8,128)S(1)} %get-tuple-element.70), channel_id=1, source_target_pairs={{0,2},{1,3},{2,18},{3,19},{4,6},{5,7},{6,22},{7,23},{8,10},{9,11},... | collective-permute-start | bytes 1572872 | tf_op jit(solution)/shard_map/ppermute | solution.py:506
  16.8 1.7 %collective-permute-start.3 = (f32[776,128]{1,0:T(8,128)S(1)}, f32[776,128]{1,0:T(8,128)S(1)}, u32[]{:S(2)}, u32[]{:S(2)}) collective-permute-start(f32[776,128]{1,0:T(8,128)S(1)} %shard_map.97.mine_ref), channel_id=1, source_target_pairs={{0,4},{1,5},{2,10},{3,11},{4,0},{5,1},{6,14},{7,15},{8,12},{9,13},... | collective-permute-start | bytes 1191944 | tf_op jit(solution)/shard_map/ppermute | solution.py:506
  18.8 9.5 %collective-permute-done.3.recv_ref = f32[776,128]{1,0:T(8,128)S(1)} collective-permute-done((f32[776,128]{1,0:T(8,128)S(1)}, f32[776,128]{1,0:T(8,128)S(1)}, u32[]{:S(2)}, u32[]{:S(2)}) %collective-permute-start.3) | collective-permute-done | bytes 397344 | tf_op jit(solution)/shard_map/ppermute | solution.py:506
  29.6 1.3 %collective-permute-start.7 = (f32[2,128,256]{2,1,0:T(8,128)S(1)}, f32[2,128,256]{2,1,0:T(8,128)S(1)}, u32[]{:S(2)}, u32[]{:S(2)}) collective-permute-start(f32[2,128,256]{2,1,0:T(8,128)S(1)} %get-tuple-element.72.refs_1_), channel_id=1, source_target_pairs={{0,2},{1,3},{4,6},{5,7},{8,10},{9,11},{12,14},{13,15},{18,16},{19,... | collective-permute-start | bytes 786440 | tf_op jit(solution)/shard_map/ppermute | solution.py:506
  30.9 1.3 %collective-permute-start.8 = (f32[2,128,256]{2,1,0:T(8,128)S(1)}, f32[2,128,256]{2,1,0:T(8,128)S(1)}, u32[]{:S(2)}, u32[]{:S(2)}) collective-permute-start(f32[2,128,256]{2,1,0:T(8,128)S(1)} %get-tuple-element.75.refs_4_), channel_id=1, source_target_pairs={{0,2},{1,3},{4,6},{5,7},{8,10},{9,11},{12,14},{13,15},{18,16},{19,... | collective-permute-start | bytes 786440 | tf_op jit(solution)/shard_map/ppermute | solution.py:506
  32.6 1.9 %collective-permute-start.14 = (f32[4,128,256]{2,1,0:T(8,128)S(1)}, f32[4,128,256]{2,1,0:T(8,128)S(1)}, u32[]{:S(2)}, u32[]{:S(2)}) collective-permute-start(f32[4,128,256]{2,1,0:T(8,128)S(1)} %get-tuple-element.94), channel_id=1, source_target_pairs={{0,2},{1,3},{2,18},{3,19},{4,6},{5,7},{6,22},{7,23},{8,10},{9,11},... | collective-permute-start | bytes 1572872 | tf_op jit(solution)/shard_map/ppermute | solution.py:506
  37.8 1.6 %collective-permute-start.11 = (f32[2,128,256]{2,1,0:T(8,128)S(1)}, f32[2,128,256]{2,1,0:T(8,128)S(1)}, u32[]{:S(2)}, u32[]{:S(2)}) collective-permute-start(f32[2,128,256]{2,1,0:T(8,128)S(1)} %get-tuple-element.88), channel_id=1, source_target_pairs={{0,2},{1,3},{2,0},{3,1},{4,6},{5,7},{6,4},{7,5},{8,10},{9,11},{10,... | collective-permute-start | bytes 786440 | tf_op jit(solution)/shard_map/ppermute | solution.py:506
  39.4 1.2 %collective-permute-done.11.recv_ref = f32[2,128,256]{2,1,0:T(8,128)S(1)} collective-permute-done((f32[2,128,256]{2,1,0:T(8,128)S(1)}, f32[2,128,256]{2,1,0:T(8,128)S(1)}, u32[]{:S(2)}, u32[]{:S(2)}) %collective-permute-start.11) | collective-permute-done | bytes 262176 | tf_op jit(solution)/shard_map/ppermute | solution.py:506
  40.6 9.2 %collective-permute-done.10.recv_ref = f32[776,128]{1,0:T(8,128)S(1)} collective-permute-done((f32[776,128]{1,0:T(8,128)S(1)}, f32[776,128]{1,0:T(8,128)S(1)}, u32[]{:S(2)}, u32[]{:S(2)}) %collective-permute-start.10) | collective-permute-done | bytes 397344 | tf_op jit(solution)/shard_map/ppermute | solution.py:506
  49.9 1.7 %collective-permute-start.12 = (f32[776,128]{1,0:T(8,128)S(1)}, f32[776,128]{1,0:T(8,128)S(1)}, u32[]{:S(2)}, u32[]{:S(2)}) collective-permute-start(f32[776,128]{1,0:T(8,128)S(1)} %shard_map.107.mine_ref), channel_id=1, source_target_pairs={{0,8},{1,9},{2,6},{3,7},{4,12},{5,13},{6,2},{7,3},{8,0},{9,1},{10,... | collective-permute-start | bytes 1191944 | tf_op jit(solution)/shard_map/ppermute | solution.py:506
  51.6 1.3 %collective-permute-start.16 = (f32[2,128,256]{2,1,0:T(8,128)S(1)}, f32[2,128,256]{2,1,0:T(8,128)S(1)}, u32[]{:S(2)}, u32[]{:S(2)}) collective-permute-start(f32[2,128,256]{2,1,0:T(8,128)S(1)} %get-tuple-element.99.refs_4_), channel_id=1, source_target_pairs={{0,2},{1,3},{4,6},{5,7},{8,10},{9,11},{12,14},{13,15},{18,16},{19,... | collective-permute-start | bytes 786440 | tf_op jit(solution)/shard_map/ppermute | solution.py:506
  52.9 1.3 %collective-permute-start.15 = (f32[2,128,256]{2,1,0:T(8,128)S(1)}, f32[2,128,256]{2,1,0:T(8,128)S(1)}, u32[]{:S(2)}, u32[]{:S(2)}) collective-permute-start(f32[2,128,256]{2,1,0:T(8,128)S(1)} %get-tuple-element.96.refs_1_), channel_id=1, source_target_pairs={{0,2},{1,3},{4,6},{5,7},{8,10},{9,11},{12,14},{13,15},{18,16},{19,... | collective-permute-start | bytes 786440 | tf_op jit(solution)/shard_map/ppermute | solution.py:506
  54.2 2.6 %collective-permute-done.12.recv_ref = f32[776,128]{1,0:T(8,128)S(1)} collective-permute-done((f32[776,128]{1,0:T(8,128)S(1)}, f32[776,128]{1,0:T(8,128)S(1)}, u32[]{:S(2)}, u32[]{:S(2)}) %collective-permute-start.12) | collective-permute-done | bytes 397344 | tf_op jit(solution)/shard_map/ppermute | solution.py:506
  58.8 1.3 %collective-permute-start.19 = (f32[3,128,128]{2,1,0:T(8,128)S(1)}, f32[3,128,128]{2,1,0:T(8,128)S(1)}, u32[]{:S(2)}, u32[]{:S(2)}) collective-permute-start(f32[3,128,128]{2,1,0:T(8,128)S(1)} %get-tuple-element.112), channel_id=1, source_target_pairs={{0,4},{1,5},{2,3},{3,2},{4,0},{5,1},{6,7},{7,6},{8,12},{9,13},{10,... | collective-permute-start | bytes 589832 | tf_op jit(solution)/shard_map/ppermute | solution.py:506
  61.4 2.3 %collective-permute-done.19.recv_ref = f32[3,128,128]{2,1,0:T(8,128)S(1)} collective-permute-done((f32[3,128,128]{2,1,0:T(8,128)S(1)}, f32[3,128,128]{2,1,0:T(8,128)S(1)}, u32[]{:S(2)}, u32[]{:S(2)}) %collective-permute-start.19) | collective-permute-done | bytes 196640 | tf_op jit(solution)/shard_map/ppermute | solution.py:506
  63.7 1.5 %collective-permute-start.20 = (f32[3,64,128]{2,1,0:T(8,128)S(1)}, f32[3,64,128]{2,1,0:T(8,128)S(1)}, u32[]{:S(2)}, u32[]{:S(2)}) collective-permute-start(f32[3,64,128]{2,1,0:T(8,128)S(1)} %get-tuple-element.114), channel_id=1, source_target_pairs={{0,8},{1,9},{2,6},{3,7},{4,12},{5,13},{6,2},{7,3},{8,0},{9,1},{10,... | collective-permute-start | bytes 294920 | tf_op jit(solution)/shard_map/ppermute | solution.py:506
  65.3 2.9 %collective-permute-start.18 = (f32[4,128,256]{2,1,0:T(8,128)S(1)}, f32[4,128,256]{2,1,0:T(8,128)S(1)}, u32[]{:S(2)}, u32[]{:S(2)}) collective-permute-start(f32[4,128,256]{2,1,0:T(8,128)S(1)} %shard_map.114.own_ref), channel_id=1, source_target_pairs={{2,16},{3,17},{6,20},{7,21},{10,24},{11,25},{14,28},{15,29},{16,2}... | collective-permute-start | bytes 1572872 | tf_op jit(solution)/shard_map/ppermute | solution.py:506
  68.3 6.5 %collective-permute-done.21.recv_ref = f32[3,32,128]{2,1,0:T(8,128)S(1)} collective-permute-done((f32[3,32,128]{2,1,0:T(8,128)S(1)}, f32[3,32,128]{2,1,0:T(8,128)S(1)}, u32[]{:S(2)}, u32[]{:S(2)}) %collective-permute-start.21) | collective-permute-done | bytes 49184 | tf_op jit(solution)/shard_map/ppermute | solution.py:506
  74.9 1.2 %collective-permute-done.22.other_ref = f32[3,32,128]{2,1,0:T(8,128)S(1)} collective-permute-done((f32[3,32,128]{2,1,0:T(8,128)S(1)}, f32[3,32,128]{2,1,0:T(8,128)S(1)}, u32[]{:S(2)}, u32[]{:S(2)}) %collective-permute-start.22) | collective-permute-done | bytes 49184 | tf_op jit(solution)/shard_map/ppermute | solution.py:506
  76.1 1.3 %collective-permute-start.23 = (f32[2,3,32,128]{3,2,1,0:T(8,128)S(1)}, f32[2,3,32,128]{3,2,1,0:T(8,128)S(1)}, u32[]{:S(2)}, u32[]{:S(2)}) collective-permute-start(f32[2,3,32,128]{3,2,1,0:T(8,128)S(1)} %shard_map.119.own_ref), channel_id=1, source_target_pairs={{0,16},{1,17},{4,20},{5,21},{8,24},{9,25},{12,28},{13,29},{18,2},{... | collective-permute-start | bytes 294920 | tf_op jit(solution)/shard_map/ppermute | solution.py:506
  77.4 5.0 %collective-permute-done.23.moved_ref = f32[2,3,32,128]{3,2,1,0:T(8,128)S(1)} collective-permute-done((f32[2,3,32,128]{3,2,1,0:T(8,128)S(1)}, f32[2,3,32,128]{3,2,1,0:T(8,128)S(1)}, u32[]{:S(2)}, u32[]{:S(2)}) %collective-permute-start.23) | collective-permute-done | bytes 98336 | tf_op jit(solution)/shard_map/ppermute | solution.py:506
  82.4 2.0 %collective-permute-start.24 = (f32[1,2,3,32,128]{4,3,2,1,0:T(8,128)S(1)}, f32[1,2,3,32,128]{4,3,2,1,0:T(8,128)S(1)}, u32[]{:S(2)}, u32[]{:S(2)}) collective-permute-start(f32[1,2,3,32,128]{4,3,2,1,0:T(8,128)S(1)} %bitcast.38), channel_id=1, source_target_pairs={{0,1},{1,0},{2,10},{3,11},{4,5},{5,4},{6,14},{7,15},{8,9},{9,8},{1... | collective-permute-start | bytes 294920 | tf_op jit(solution)/shard_map/ppermute | solution.py:506
  84.4 2.0 %collective-permute-done.24.other_ref = f32[1,2,3,32,128]{4,3,2,1,0:T(8,128)S(1)} collective-permute-done((f32[1,2,3,32,128]{4,3,2,1,0:T(8,128)S(1)}, f32[1,2,3,32,128]{4,3,2,1,0:T(8,128)S(1)}, u32[]{:S(2)}, u32[]{:S(2)}) %collective-permute-start.24) | collective-permute-done | bytes 98336 | tf_op jit(solution)/shard_map/ppermute | solution.py:506
  86.5 1.5 %collective-permute-start.25 = (f32[2,2,3,32,128]{4,3,2,1,0:T(8,128)S(1)}, f32[2,2,3,32,128]{4,3,2,1,0:T(8,128)S(1)}, u32[]{:S(2)}, u32[]{:S(2)}) collective-permute-start(f32[2,2,3,32,128]{4,3,2,1,0:T(8,128)S(1)} %bitcast.32), channel_id=1, source_target_pairs={{0,8},{1,9},{2,6},{3,7},{4,12},{5,13},{6,2},{7,3},{8,0},{9,1},{10,... | collective-permute-start | bytes 589832 | tf_op jit(solution)/shard_map/ppermute | solution.py:506
  88.0 3.1 %collective-permute-done.25.other_ref = f32[2,2,3,32,128]{4,3,2,1,0:T(8,128)S(1)} collective-permute-done((f32[2,2,3,32,128]{4,3,2,1,0:T(8,128)S(1)}, f32[2,2,3,32,128]{4,3,2,1,0:T(8,128)S(1)}, u32[]{:S(2)}, u32[]{:S(2)}) %collective-permute-start.25) | collective-permute-done | bytes 196640 | tf_op jit(solution)/shard_map/ppermute | solution.py:506
  91.1 1.6 %collective-permute-start.26 = (f32[4,2,3,32,128]{4,3,2,1,0:T(8,128)S(1)}, f32[4,2,3,32,128]{4,3,2,1,0:T(8,128)S(1)}, u32[]{:S(2)}, u32[]{:S(2)}) collective-permute-start(f32[4,2,3,32,128]{4,3,2,1,0:T(8,128)S(1)} %bitcast.29), channel_id=1, source_target_pairs={{0,4},{1,5},{2,3},{3,2},{4,0},{5,1},{6,7},{7,6},{8,12},{9,13},{10,... | collective-permute-start | bytes 1179656 | tf_op jit(solution)/shard_map/ppermute | solution.py:506
  93.4 4.7 %collective-permute-done.26.recv_ref = f32[4,2,3,32,128]{4,3,2,1,0:T(8,128)S(1)} collective-permute-done((f32[4,2,3,32,128]{4,3,2,1,0:T(8,128)S(1)}, f32[4,2,3,32,128]{4,3,2,1,0:T(8,128)S(1)}, u32[]{:S(2)}, u32[]{:S(2)}) %collective-permute-start.26) | collective-permute-done | bytes 393248 | tf_op jit(solution)/shard_map/ppermute | solution.py:506
  (67 shorter events, 14.5 us)
Async XLA Ops:
  0.6 8.5 %copy-start = (bf16[1,3,128,1,256]{4,2,3,1,0:T(8,128)(2,1)S(1)}, bf16[1,3,128,1,256]{4,2,3,1,0:T(8,128)(2,1)}, u32[]{:S(2)}) copy-start(bf16[1,3,128,1,256]{4,2,3,1,0:T(8,128)(2,1)} %param.6) | copy-start | bytes 589828
  0.6 8.5 %copy-start.1 = (bf16[1,3,128,1,256]{4,2,3,1,0:T(8,128)(2,1)S(1)}, bf16[1,3,128,1,256]{4,2,3,1,0:T(8,128)(2,1)}, u32[]{:S(2)}) copy-start(bf16[1,3,128,1,256]{4,2,3,1,0:T(8,128)(2,1)} %param.9) | copy-start | bytes 589828
  2.3 8.7 %collective-permute-start = (f32[2,128,256]{2,1,0:T(8,128)}, f32[2,128,256]{2,1,0:T(8,128)S(1)}, u32[]{:S(2)}, u32[]{:S(2)}) collective-permute-start(f32[2,128,256]{2,1,0:T(8,128)} %shard_map.93.refs_0_), channel_id=1, source_target_pairs={{0,2},{1,3},{2,18},{3,19},{4,6},{5,7},{6,22},{7,23},{8,10},{9,11},... | collective-permute-start | bytes 786440 | tf_op jit(solution)/shard_map/ppermute | solution.py:506
  9.0 3.5 %copy-start.5 = (bf16[1,3,128,1,256]{4,2,3,1,0:T(8,128)(2,1)S(1)}, bf16[1,3,128,1,256]{4,2,3,1,0:T(8,128)(2,1)}, u32[]{:S(2)}) copy-start(bf16[1,3,128,1,256]{4,2,3,1,0:T(8,128)(2,1)} %param.7) | copy-start | bytes 589828
  9.0 3.5 %copy-start.6 = (bf16[1,3,128,1,256]{4,2,3,1,0:T(8,128)(2,1)S(1)}, bf16[1,3,128,1,256]{4,2,3,1,0:T(8,128)(2,1)}, u32[]{:S(2)}) copy-start(bf16[1,3,128,1,256]{4,2,3,1,0:T(8,128)(2,1)} %param.8) | copy-start | bytes 589828
  9.0 6.7 %collective-permute-start.2 = (f32[768,128]{1,0:T(8,128)S(1)}, f32[768,128]{1,0:T(8,128)S(1)}, u32[]{:S(2)}, u32[]{:S(2)}) collective-permute-start(f32[768,128]{1,0:T(8,128)S(1)} %get-tuple-element.65), channel_id=1, source_target_pairs={{0,2},{1,3},{2,0},{3,1},{4,6},{5,7},{6,4},{7,5},{8,10},{9,11},{10,... | collective-permute-start | bytes 1179656 | tf_op jit(solution)/shard_map/ppermute | solution.py:506
  11.0 5.1 %copy-start.3 = (f32[2,128,256]{2,1,0:T(8,128)S(1)}, f32[2,128,256]{2,1,0:T(8,128)}, u32[]{:S(2)}) copy-start(f32[2,128,256]{2,1,0:T(8,128)} %shard_map.93.refs_0_) | copy-start | bytes 786436
  11.0 5.1 %collective-permute-start.1 = (f32[2,128,256]{2,1,0:T(8,128)S(1)}, f32[2,128,256]{2,1,0:T(8,128)S(1)}, u32[]{:S(2)}, u32[]{:S(2)}) collective-permute-start(f32[2,128,256]{2,1,0:T(8,128)S(1)} %collective-permute-done.refs_1_), channel_id=1, source_target_pairs={{0,2},{1,3},{4,6},{5,7},{8,10},{9,11},{12,14},{13,15},{18,16},{19,... | collective-permute-start | bytes 786440 | tf_op jit(solution)/shard_map/ppermute | solution.py:506
  12.9 16.6 %collective-permute-start.6 = (f32[4,128,256]{2,1,0:T(8,128)S(1)}, f32[4,128,256]{2,1,0:T(8,128)S(1)}, u32[]{:S(2)}, u32[]{:S(2)}) collective-permute-start(f32[4,128,256]{2,1,0:T(8,128)S(1)} %get-tuple-element.70), channel_id=1, source_target_pairs={{0,2},{1,3},{2,18},{3,19},{4,6},{5,7},{6,22},{7,23},{8,10},{9,11},... | collective-permute-start | bytes 1572872 | tf_op jit(solution)/shard_map/ppermute | solution.py:506
  16.8 11.6 %collective-permute-start.3 = (f32[776,128]{1,0:T(8,128)S(1)}, f32[776,128]{1,0:T(8,128)S(1)}, u32[]{:S(2)}, u32[]{:S(2)}) collective-permute-start(f32[776,128]{1,0:T(8,128)S(1)} %shard_map.97.mine_ref), channel_id=1, source_target_pairs={{0,4},{1,5},{2,10},{3,11},{4,0},{5,1},{6,14},{7,15},{8,12},{9,13},... | collective-permute-start | bytes 1191944 | tf_op jit(solution)/shard_map/ppermute | solution.py:506
  18.5 16.8 %collective-permute-start.9 = (f32[1560,128]{1,0:T(8,128)S(1)}, f32[1560,128]{1,0:T(8,128)S(1)}, u32[]{:S(2)}, u32[]{:S(2)}) collective-permute-start(f32[1560,128]{1,0:T(8,128)S(1)} %get-tuple-element.78), channel_id=1, source_target_pairs={{0,2},{1,3},{2,0},{3,1},{4,6},{5,7},{6,4},{7,5},{8,10},{9,11},{10,... | collective-permute-start | bytes 2396168 | tf_op jit(solution)/shard_map/ppermute | solution.py:506
  28.4 6.7 %collective-permute-start.4 = (f32[776,128]{1,0:T(8,128)S(1)}, f32[776,128]{1,0:T(8,128)S(1)}, u32[]{:S(2)}, u32[]{:S(2)}) collective-permute-start(f32[776,128]{1,0:T(8,128)S(1)} %shard_map.98.mine_ref), channel_id=1, source_target_pairs={{0,8},{1,9},{2,6},{3,7},{4,12},{5,13},{6,2},{7,3},{8,0},{9,1},{10,... | collective-permute-start | bytes 1191944 | tf_op jit(solution)/shard_map/ppermute | solution.py:506
  29.6 5.8 %collective-permute-start.7 = (f32[2,128,256]{2,1,0:T(8,128)S(1)}, f32[2,128,256]{2,1,0:T(8,128)S(1)}, u32[]{:S(2)}, u32[]{:S(2)}) collective-permute-start(f32[2,128,256]{2,1,0:T(8,128)S(1)} %get-tuple-element.72.refs_1_), channel_id=1, source_target_pairs={{0,2},{1,3},{4,6},{5,7},{8,10},{9,11},{12,14},{13,15},{18,16},{19,... | collective-permute-start | bytes 786440 | tf_op jit(solution)/shard_map/ppermute | solution.py:506
  30.9 4.5 %collective-permute-start.8 = (f32[2,128,256]{2,1,0:T(8,128)S(1)}, f32[2,128,256]{2,1,0:T(8,128)S(1)}, u32[]{:S(2)}, u32[]{:S(2)}) collective-permute-start(f32[2,128,256]{2,1,0:T(8,128)S(1)} %get-tuple-element.75.refs_4_), channel_id=1, source_target_pairs={{0,2},{1,3},{4,6},{5,7},{8,10},{9,11},{12,14},{13,15},{18,16},{19,... | collective-permute-start | bytes 786440 | tf_op jit(solution)/shard_map/ppermute | solution.py:506
  32.6 19.0 %collective-permute-start.14 = (f32[4,128,256]{2,1,0:T(8,128)S(1)}, f32[4,128,256]{2,1,0:T(8,128)S(1)}, u32[]{:S(2)}, u32[]{:S(2)}) collective-permute-start(f32[4,128,256]{2,1,0:T(8,128)S(1)} %get-tuple-element.94), channel_id=1, source_target_pairs={{0,2},{1,3},{2,18},{3,19},{4,6},{5,7},{6,22},{7,23},{8,10},{9,11},... | collective-permute-start | bytes 1572872 | tf_op jit(solution)/shard_map/ppermute | solution.py:506
  35.2 1.2 %collective-permute-start.5 = (f32[8,128]{1,0:T(8,128)S(1)}, f32[8,128]{1,0:T(8,128)S(1)}, u32[]{:S(2)}, u32[]{:S(2)}) collective-permute-start(f32[8,128]{1,0:T(8,128)S(1)} %get-tuple-element.67.refs_1_), channel_id=1, source_target_pairs={{0,2},{1,3},{2,0},{3,1},{4,6},{5,7},{6,4},{7,5},{8,10},{9,11},{10,... | collective-permute-start | bytes 12296 | tf_op jit(solution)/shard_map/ppermute | solution.py:506
  37.1 12.7 %collective-permute-start.10 = (f32[776,128]{1,0:T(8,128)S(1)}, f32[776,128]{1,0:T(8,128)S(1)}, u32[]{:S(2)}, u32[]{:S(2)}) collective-permute-start(f32[776,128]{1,0:T(8,128)S(1)} %get-tuple-element.84.mine_ref), channel_id=1, source_target_pairs={{0,4},{1,5},{2,10},{3,11},{4,0},{5,1},{6,14},{7,15},{8,12},{9,13},... | collective-permute-start | bytes 1191944 | tf_op jit(solution)/shard_map/ppermute | solution.py:506
  37.8 2.8 %collective-permute-start.11 = (f32[2,128,256]{2,1,0:T(8,128)S(1)}, f32[2,128,256]{2,1,0:T(8,128)S(1)}, u32[]{:S(2)}, u32[]{:S(2)}) collective-permute-start(f32[2,128,256]{2,1,0:T(8,128)S(1)} %get-tuple-element.88), channel_id=1, source_target_pairs={{0,2},{1,3},{2,0},{3,1},{4,6},{5,7},{6,4},{7,5},{8,10},{9,11},{10,... | collective-permute-start | bytes 786440 | tf_op jit(solution)/shard_map/ppermute | solution.py:506
  49.9 6.9 %collective-permute-start.12 = (f32[776,128]{1,0:T(8,128)S(1)}, f32[776,128]{1,0:T(8,128)S(1)}, u32[]{:S(2)}, u32[]{:S(2)}) collective-permute-start(f32[776,128]{1,0:T(8,128)S(1)} %shard_map.107.mine_ref), channel_id=1, source_target_pairs={{0,8},{1,9},{2,6},{3,7},{4,12},{5,13},{6,2},{7,3},{8,0},{9,1},{10,... | collective-permute-start | bytes 1191944 | tf_op jit(solution)/shard_map/ppermute | solution.py:506
  51.6 5.3 %collective-permute-start.16 = (f32[2,128,256]{2,1,0:T(8,128)S(1)}, f32[2,128,256]{2,1,0:T(8,128)S(1)}, u32[]{:S(2)}, u32[]{:S(2)}) collective-permute-start(f32[2,128,256]{2,1,0:T(8,128)S(1)} %get-tuple-element.99.refs_4_), channel_id=1, source_target_pairs={{0,2},{1,3},{4,6},{5,7},{8,10},{9,11},{12,14},{13,15},{18,16},{19,... | collective-permute-start | bytes 786440 | tf_op jit(solution)/shard_map/ppermute | solution.py:506
  52.9 4.0 %collective-permute-start.15 = (f32[2,128,256]{2,1,0:T(8,128)S(1)}, f32[2,128,256]{2,1,0:T(8,128)S(1)}, u32[]{:S(2)}, u32[]{:S(2)}) collective-permute-start(f32[2,128,256]{2,1,0:T(8,128)S(1)} %get-tuple-element.96.refs_1_), channel_id=1, source_target_pairs={{0,2},{1,3},{4,6},{5,7},{8,10},{9,11},{12,14},{13,15},{18,16},{19,... | collective-permute-start | bytes 786440 | tf_op jit(solution)/shard_map/ppermute | solution.py:506
  56.8 1.2 %collective-permute-start.13 = (f32[8,128]{1,0:T(8,128)S(1)}, f32[8,128]{1,0:T(8,128)S(1)}, u32[]{:S(2)}, u32[]{:S(2)}) collective-permute-start(f32[8,128]{1,0:T(8,128)S(1)} %get-tuple-element.91.refs_1_), channel_id=1, source_target_pairs={{0,2},{1,3},{2,0},{3,1},{4,6},{5,7},{6,4},{7,5},{8,10},{9,11},{10,... | collective-permute-start | bytes 12296 | tf_op jit(solution)/shard_map/ppermute | solution.py:506
  58.8 4.9 %collective-permute-start.19 = (f32[3,128,128]{2,1,0:T(8,128)S(1)}, f32[3,128,128]{2,1,0:T(8,128)S(1)}, u32[]{:S(2)}, u32[]{:S(2)}) collective-permute-start(f32[3,128,128]{2,1,0:T(8,128)S(1)} %get-tuple-element.112), channel_id=1, source_target_pairs={{0,4},{1,5},{2,3},{3,2},{4,0},{5,1},{6,7},{7,6},{8,12},{9,13},{10,... | collective-permute-start | bytes 589832 | tf_op jit(solution)/shard_map/ppermute | solution.py:506
  60.7 4.6 %collective-permute-start.17 = (f32[2,128,256]{2,1,0:T(8,128)S(1)}, f32[2,128,256]{2,1,0:T(8,128)S(1)}, u32[]{:S(2)}, u32[]{:S(2)}) collective-permute-start(f32[2,128,256]{2,1,0:T(8,128)S(1)} %get-tuple-element.108), channel_id=1, source_target_pairs={{0,2},{1,3},{2,0},{3,1},{4,6},{5,7},{6,4},{7,5},{8,10},{9,11},{10,... | collective-permute-start | bytes 786440 | tf_op jit(solution)/shard_map/ppermute | solution.py:506
  63.7 4.5 %collective-permute-start.20 = (f32[3,64,128]{2,1,0:T(8,128)S(1)}, f32[3,64,128]{2,1,0:T(8,128)S(1)}, u32[]{:S(2)}, u32[]{:S(2)}) collective-permute-start(f32[3,64,128]{2,1,0:T(8,128)S(1)} %get-tuple-element.114), channel_id=1, source_target_pairs={{0,8},{1,9},{2,6},{3,7},{4,12},{5,13},{6,2},{7,3},{8,0},{9,1},{10,... | collective-permute-start | bytes 294920 | tf_op jit(solution)/shard_map/ppermute | solution.py:506
  65.3 22.7 %collective-permute-start.18 = (f32[4,128,256]{2,1,0:T(8,128)S(1)}, f32[4,128,256]{2,1,0:T(8,128)S(1)}, u32[]{:S(2)}, u32[]{:S(2)}) collective-permute-start(f32[4,128,256]{2,1,0:T(8,128)S(1)} %shard_map.114.own_ref), channel_id=1, source_target_pairs={{2,16},{3,17},{6,20},{7,21},{10,24},{11,25},{14,28},{15,29},{16,2}... | collective-permute-start | bytes 1572872 | tf_op jit(solution)/shard_map/ppermute | solution.py:506
  68.3 6.6 %collective-permute-start.21 = (f32[3,32,128]{2,1,0:T(8,128)S(1)}, f32[3,32,128]{2,1,0:T(8,128)S(1)}, u32[]{:S(2)}, u32[]{:S(2)}) collective-permute-start(f32[3,32,128]{2,1,0:T(8,128)S(1)} %get-tuple-element.116), channel_id=1, source_target_pairs={{0,1},{1,0},{2,10},{3,11},{4,5},{5,4},{6,14},{7,15},{8,9},{9,8},{1... | collective-permute-start | bytes 147464 | tf_op jit(solution)/shard_map/ppermute | solution.py:506
  74.9 1.2 %collective-permute-start.22 = (f32[3,32,128]{2,1,0:T(8,128)S(1)}, f32[3,32,128]{2,1,0:T(8,128)S(1)}, u32[]{:S(2)}, u32[]{:S(2)}) collective-permute-start(f32[3,32,128]{2,1,0:T(8,128)S(1)} %shard_map.118.mine_ref), channel_id=1, source_target_pairs={{0,2},{1,3},{2,0},{3,1},{4,6},{5,7},{6,4},{7,5},{8,10},{9,11},{10,... | collective-permute-start | bytes 147464 | tf_op jit(solution)/shard_map/ppermute | solution.py:506
  76.1 6.3 %collective-permute-start.23 = (f32[2,3,32,128]{3,2,1,0:T(8,128)S(1)}, f32[2,3,32,128]{3,2,1,0:T(8,128)S(1)}, u32[]{:S(2)}, u32[]{:S(2)}) collective-permute-start(f32[2,3,32,128]{3,2,1,0:T(8,128)S(1)} %shard_map.119.own_ref), channel_id=1, source_target_pairs={{0,16},{1,17},{4,20},{5,21},{8,24},{9,25},{12,28},{13,29},{18,2},{... | collective-permute-start | bytes 294920 | tf_op jit(solution)/shard_map/ppermute | solution.py:506
  82.4 4.0 %collective-permute-start.24 = (f32[1,2,3,32,128]{4,3,2,1,0:T(8,128)S(1)}, f32[1,2,3,32,128]{4,3,2,1,0:T(8,128)S(1)}, u32[]{:S(2)}, u32[]{:S(2)}) collective-permute-start(f32[1,2,3,32,128]{4,3,2,1,0:T(8,128)S(1)} %bitcast.38), channel_id=1, source_target_pairs={{0,1},{1,0},{2,10},{3,11},{4,5},{5,4},{6,14},{7,15},{8,9},{9,8},{1... | collective-permute-start | bytes 294920 | tf_op jit(solution)/shard_map/ppermute | solution.py:506
  86.5 4.6 %collective-permute-start.25 = (f32[2,2,3,32,128]{4,3,2,1,0:T(8,128)S(1)}, f32[2,2,3,32,128]{4,3,2,1,0:T(8,128)S(1)}, u32[]{:S(2)}, u32[]{:S(2)}) collective-permute-start(f32[2,2,3,32,128]{4,3,2,1,0:T(8,128)S(1)} %bitcast.32), channel_id=1, source_target_pairs={{0,8},{1,9},{2,6},{3,7},{4,12},{5,13},{6,2},{7,3},{8,0},{9,1},{10,... | collective-permute-start | bytes 589832 | tf_op jit(solution)/shard_map/ppermute | solution.py:506
  91.1 7.0 %collective-permute-start.26 = (f32[4,2,3,32,128]{4,3,2,1,0:T(8,128)S(1)}, f32[4,2,3,32,128]{4,3,2,1,0:T(8,128)S(1)}, u32[]{:S(2)}, u32[]{:S(2)}) collective-permute-start(f32[4,2,3,32,128]{4,3,2,1,0:T(8,128)S(1)} %bitcast.29), channel_id=1, source_target_pairs={{0,4},{1,5},{2,3},{3,2},{4,0},{5,1},{6,7},{7,6},{8,12},{9,13},{10,... | collective-permute-start | bytes 1179656 | tf_op jit(solution)/shard_map/ppermute | solution.py:506
  (2 other events, 2.1 us)

commit v6 on v5

--- a/solution.py
+++ b/solution.py
@@ -538,6 +538,7 @@
         def goes(tok, head, vid):
             if stays_at(tok, head):
                 return (tok ^ (tok_count // 2), head, vid)
+            return (tok, head ^ 1, vid)
 
         return permute(array, goes)
 

time: 100 us -> 99.8 us (level)
  starting transfers between devices: 34.1 us -> 30.7 us
  waiting for transfers between devices: 48.8 us -> 52 us
    ppermute x27, starting transfers between devices: 34.1 us -> 30.7 us  [permute(): return lax.ppermute(array, ('tok', 'head', 'vid'), pairs)]
    ppermute x27, waiting for transfers between devices: 48.8 us -> 52 us  [permute(): return lax.ppermute(array, ('tok', 'head', 'vid'), pairs)]
where the time goes in v6:
time: 99.8 us; the launch traced here: 99 us
  waiting for transfers between devices  52 us (52%)
  starting transfers between devices  30.7 us (31%)
  Pallas kernels  13.1 us (13%)
  local copies, waits for them, and re-layouts  2.15 us (2%)
  between operations  1 us (1%)
    ppermute x27, waiting for transfers between devices, permute(): return lax.ppermute(array, ('tok', 'head', 'vid'), pairs)  52 us
    ppermute x27, starting transfers between devices, permute(): return lax.ppermute(array, ('tok', 'head', 'vid'), pairs)  30.7 us
    pallas_call x31, Pallas kernels, call(): pl.pallas_call(kernel, out_shape=outs, **kwargs, scratch_shapes=scratch,...  13.1 us
    unnamed x14, local copies, waits for them, and re-layouts  2.15 us
  transfers between devices with their start and end apart: 27, of which 15 were waited for; matrix products, arithmetic and copies ran while one was open for 0% of the time, Pallas kernels for 10%

profile of v6, /device:TPU:1, one launch (start us, length us, event | category | flops | bytes accessed | tf_op | source)
XLA Modules:
  0.0 99.0 jit_solution(2539105636398474828)
XLA Ops:
  0.7 1.7 %shard_map.93.refs_0_ = f32[2,128,256]{2,1,0:T(8,128)} custom-call(bf16[3,128,256]{2,1,0:T(8,128)(2,1)} %bitcast.19, bf16[3,128,256]{2,1,0:T(8,128)(2,1)} %bitcast.23), custom_call_target="tpu_custom_call" | custom-call | flops 1 | bytes 1 | tf_op jit(solution)/shard_map/pallas_call | solution.py:452
  2.3 3.2 %collective-permute-start = (f32[2,128,256]{2,1,0:T(8,128)}, f32[2,128,256]{2,1,0:T(8,128)S(1)}, u32[]{:S(2)}, u32[]{:S(2)}) collective-permute-start(f32[2,128,256]{2,1,0:T(8,128)} %shard_map.93.refs_0_), channel_id=1, source_target_pairs={{0,2},{1,3},{2,18},{3,19},{4,6},{5,7},{6,22},{7,23},{8,10},{9,11},... | collective-permute-start | bytes 786440 | tf_op jit(solution)/shard_map/ppermute | solution.py:506
  6.5 1.1 %copy-done.4 = bf16[1,2,1,3,256,256]{5,4,3,2,1,0:T(8,128)(2,1)S(1)} copy-done((bf16[1,2,1,3,256,256]{5,4,3,2,1,0:T(8,128)(2,1)S(1)}, bf16[1,2,1,3,256,256]{5,4,3,2,1,0:T(8,128)(2,1)}, u32[]{:S(2)}) %copy-start.4) | copy-done | bytes 786456
  7.6 1.3 %shard_map.94 = (f32[2,3,256,256]{3,2,1,0:T(8,128)S(1)}, f32[768,128]{1,0:T(8,128)S(1)}, f32[1560,128]{1,0:T(8,128)S(1)}, f32[768,128]{1,0:T(8,128)S(1)}, f32[1560,128]{1,0:T(8,128)S(1)}) custom-call(bf16[3,256,256]{2,1,0:T(8,128)(2,1)S(1)} %bitcast.27, bf16[2,3,256,256]{3,2,1,0:T(8,128)(2,1)S(1)} %bitcast.31), custom_call_target="tpu_custom_call" | custom-call | flops 1 | bytes 1 | tf_op jit(solution)/shard_map/pallas_call | solution.py:452
  9.1 1.9 %shard_map.95 = bf16[3,128,256]{2,1,0:T(8,128)(2,1)} custom-call(bf16[3,128,256]{2,1,0:T(8,128)(2,1)S(1)} %bitcast.20, bf16[3,128,256]{2,1,0:T(8,128)(2,1)S(1)} %bitcast.24, bf16[3,256,256]{2,1,0:T(8,128)(2,1)S(1)} %bitcast.28, f32[2,3,256,256]{3,2,1,0:T(8,128)S(1)} %get-tuple-element.62.full_ref), custom_call_target="tpu_custom_call" | custom-call | flops 1 | bytes 1 | tf_op jit(solution)/shard_map/pallas_call | solution.py:452
  11.0 1.4 %collective-permute-start.1 = (f32[2,128,256]{2,1,0:T(8,128)S(1)}, f32[2,128,256]{2,1,0:T(8,128)S(1)}, u32[]{:S(2)}, u32[]{:S(2)}) collective-permute-start(f32[2,128,256]{2,1,0:T(8,128)S(1)} %collective-permute-done.refs_1_), channel_id=1, source_target_pairs={{0,2},{1,3},{4,6},{5,7},{8,10},{9,11},{12,14},{13,15},{18,16},{19,... | collective-permute-start | bytes 786440 | tf_op jit(solution)/shard_map/ppermute | solution.py:506
  12.9 2.7 %collective-permute-start.6 = (f32[4,128,256]{2,1,0:T(8,128)S(1)}, f32[4,128,256]{2,1,0:T(8,128)S(1)}, u32[]{:S(2)}, u32[]{:S(2)}) collective-permute-start(f32[4,128,256]{2,1,0:T(8,128)S(1)} %get-tuple-element.70), channel_id=1, source_target_pairs={{0,2},{1,3},{2,18},{3,19},{4,6},{5,7},{6,22},{7,23},{8,10},{9,11},... | collective-permute-start | bytes 1572872 | tf_op jit(solution)/shard_map/ppermute | solution.py:506
  16.8 1.7 %collective-permute-start.3 = (f32[776,128]{1,0:T(8,128)S(1)}, f32[776,128]{1,0:T(8,128)S(1)}, u32[]{:S(2)}, u32[]{:S(2)}) collective-permute-start(f32[776,128]{1,0:T(8,128)S(1)} %shard_map.97.mine_ref), channel_id=1, source_target_pairs={{0,4},{1,5},{2,10},{3,11},{4,0},{5,1},{6,14},{7,15},{8,12},{9,13},... | collective-permute-start | bytes 1191944 | tf_op jit(solution)/shard_map/ppermute | solution.py:506
  18.8 9.5 %collective-permute-done.3.recv_ref = f32[776,128]{1,0:T(8,128)S(1)} collective-permute-done((f32[776,128]{1,0:T(8,128)S(1)}, f32[776,128]{1,0:T(8,128)S(1)}, u32[]{:S(2)}, u32[]{:S(2)}) %collective-permute-start.3) | collective-permute-done | bytes 397344 | tf_op jit(solution)/shard_map/ppermute | solution.py:506
  28.4 1.1 %collective-permute-start.4 = (f32[776,128]{1,0:T(8,128)S(1)}, f32[776,128]{1,0:T(8,128)S(1)}, u32[]{:S(2)}, u32[]{:S(2)}) collective-permute-start(f32[776,128]{1,0:T(8,128)S(1)} %shard_map.98.mine_ref), channel_id=1, source_target_pairs={{0,8},{1,9},{2,6},{3,7},{4,12},{5,13},{6,2},{7,3},{8,0},{9,1},{10,... | collective-permute-start | bytes 1191944 | tf_op jit(solution)/shard_map/ppermute | solution.py:506
  29.6 1.3 %collective-permute-start.7 = (f32[2,128,256]{2,1,0:T(8,128)S(1)}, f32[2,128,256]{2,1,0:T(8,128)S(1)}, u32[]{:S(2)}, u32[]{:S(2)}) collective-permute-start(f32[2,128,256]{2,1,0:T(8,128)S(1)} %get-tuple-element.72.refs_1_), channel_id=1, source_target_pairs={{0,2},{1,3},{4,6},{5,7},{8,10},{9,11},{12,14},{13,15},{18,16},{19,... | collective-permute-start | bytes 786440 | tf_op jit(solution)/shard_map/ppermute | solution.py:506
  30.9 1.3 %collective-permute-start.8 = (f32[2,128,256]{2,1,0:T(8,128)S(1)}, f32[2,128,256]{2,1,0:T(8,128)S(1)}, u32[]{:S(2)}, u32[]{:S(2)}) collective-permute-start(f32[2,128,256]{2,1,0:T(8,128)S(1)} %get-tuple-element.75.refs_4_), channel_id=1, source_target_pairs={{0,2},{1,3},{4,6},{5,7},{8,10},{9,11},{12,14},{13,15},{18,16},{19,... | collective-permute-start | bytes 786440 | tf_op jit(solution)/shard_map/ppermute | solution.py:506
  32.6 1.9 %collective-permute-start.14 = (f32[4,128,256]{2,1,0:T(8,128)S(1)}, f32[4,128,256]{2,1,0:T(8,128)S(1)}, u32[]{:S(2)}, u32[]{:S(2)}) collective-permute-start(f32[4,128,256]{2,1,0:T(8,128)S(1)} %get-tuple-element.94), channel_id=1, source_target_pairs={{0,2},{1,3},{2,18},{3,19},{4,6},{5,7},{6,22},{7,23},{8,10},{9,11},... | collective-permute-start | bytes 1572872 | tf_op jit(solution)/shard_map/ppermute | solution.py:506
  37.8 1.6 %collective-permute-start.11 = (f32[2,128,256]{2,1,0:T(8,128)S(1)}, f32[2,128,256]{2,1,0:T(8,128)S(1)}, u32[]{:S(2)}, u32[]{:S(2)}) collective-permute-start(f32[2,128,256]{2,1,0:T(8,128)S(1)} %get-tuple-element.88), channel_id=1, source_target_pairs={{0,2},{1,3},{2,0},{3,1},{4,6},{5,7},{6,4},{7,5},{8,10},{9,11},{10,... | collective-permute-start | bytes 786440 | tf_op jit(solution)/shard_map/ppermute | solution.py:506
  39.4 1.2 %collective-permute-done.11.recv_ref = f32[2,128,256]{2,1,0:T(8,128)S(1)} collective-permute-done((f32[2,128,256]{2,1,0:T(8,128)S(1)}, f32[2,128,256]{2,1,0:T(8,128)S(1)}, u32[]{:S(2)}, u32[]{:S(2)}) %collective-permute-start.11) | collective-permute-done | bytes 262176 | tf_op jit(solution)/shard_map/ppermute | solution.py:506
  40.6 9.2 %collective-permute-done.10.recv_ref = f32[776,128]{1,0:T(8,128)S(1)} collective-permute-done((f32[776,128]{1,0:T(8,128)S(1)}, f32[776,128]{1,0:T(8,128)S(1)}, u32[]{:S(2)}, u32[]{:S(2)}) %collective-permute-start.10) | collective-permute-done | bytes 397344 | tf_op jit(solution)/shard_map/ppermute | solution.py:506
  49.9 1.7 %collective-permute-start.12 = (f32[776,128]{1,0:T(8,128)S(1)}, f32[776,128]{1,0:T(8,128)S(1)}, u32[]{:S(2)}, u32[]{:S(2)}) collective-permute-start(f32[776,128]{1,0:T(8,128)S(1)} %shard_map.107.mine_ref), channel_id=1, source_target_pairs={{0,8},{1,9},{2,6},{3,7},{4,12},{5,13},{6,2},{7,3},{8,0},{9,1},{10,... | collective-permute-start | bytes 1191944 | tf_op jit(solution)/shard_map/ppermute | solution.py:506
  51.6 1.3 %collective-permute-start.16 = (f32[2,128,256]{2,1,0:T(8,128)S(1)}, f32[2,128,256]{2,1,0:T(8,128)S(1)}, u32[]{:S(2)}, u32[]{:S(2)}) collective-permute-start(f32[2,128,256]{2,1,0:T(8,128)S(1)} %get-tuple-element.99.refs_4_), channel_id=1, source_target_pairs={{0,2},{1,3},{4,6},{5,7},{8,10},{9,11},{12,14},{13,15},{18,16},{19,... | collective-permute-start | bytes 786440 | tf_op jit(solution)/shard_map/ppermute | solution.py:506
  52.9 1.3 %collective-permute-start.15 = (f32[2,128,256]{2,1,0:T(8,128)S(1)}, f32[2,128,256]{2,1,0:T(8,128)S(1)}, u32[]{:S(2)}, u32[]{:S(2)}) collective-permute-start(f32[2,128,256]{2,1,0:T(8,128)S(1)} %get-tuple-element.96.refs_1_), channel_id=1, source_target_pairs={{0,2},{1,3},{4,6},{5,7},{8,10},{9,11},{12,14},{13,15},{18,16},{19,... | collective-permute-start | bytes 786440 | tf_op jit(solution)/shard_map/ppermute | solution.py:506
  54.2 2.6 %collective-permute-done.12.recv_ref = f32[776,128]{1,0:T(8,128)S(1)} collective-permute-done((f32[776,128]{1,0:T(8,128)S(1)}, f32[776,128]{1,0:T(8,128)S(1)}, u32[]{:S(2)}, u32[]{:S(2)}) %collective-permute-start.12) | collective-permute-done | bytes 397344 | tf_op jit(solution)/shard_map/ppermute | solution.py:506
  58.8 1.3 %collective-permute-start.19 = (f32[3,128,128]{2,1,0:T(8,128)S(1)}, f32[3,128,128]{2,1,0:T(8,128)S(1)}, u32[]{:S(2)}, u32[]{:S(2)}) collective-permute-start(f32[3,128,128]{2,1,0:T(8,128)S(1)} %get-tuple-element.112), channel_id=1, source_target_pairs={{0,4},{1,5},{2,3},{3,2},{4,0},{5,1},{6,7},{7,6},{8,12},{9,13},{10,... | collective-permute-start | bytes 589832 | tf_op jit(solution)/shard_map/ppermute | solution.py:506
  61.4 2.3 %collective-permute-done.19.recv_ref = f32[3,128,128]{2,1,0:T(8,128)S(1)} collective-permute-done((f32[3,128,128]{2,1,0:T(8,128)S(1)}, f32[3,128,128]{2,1,0:T(8,128)S(1)}, u32[]{:S(2)}, u32[]{:S(2)}) %collective-permute-start.19) | collective-permute-done | bytes 196640 | tf_op jit(solution)/shard_map/ppermute | solution.py:506
  63.7 1.5 %collective-permute-start.20 = (f32[3,64,128]{2,1,0:T(8,128)S(1)}, f32[3,64,128]{2,1,0:T(8,128)S(1)}, u32[]{:S(2)}, u32[]{:S(2)}) collective-permute-start(f32[3,64,128]{2,1,0:T(8,128)S(1)} %get-tuple-element.114), channel_id=1, source_target_pairs={{0,8},{1,9},{2,6},{3,7},{4,12},{5,13},{6,2},{7,3},{8,0},{9,1},{10,... | collective-permute-start | bytes 294920 | tf_op jit(solution)/shard_map/ppermute | solution.py:506
  65.3 2.9 %collective-permute-start.18 = (f32[4,128,256]{2,1,0:T(8,128)S(1)}, f32[4,128,256]{2,1,0:T(8,128)S(1)}, u32[]{:S(2)}, u32[]{:S(2)}) collective-permute-start(f32[4,128,256]{2,1,0:T(8,128)S(1)} %shard_map.114.own_ref), channel_id=1, source_target_pairs={{2,16},{3,17},{6,20},{7,21},{10,24},{11,25},{14,28},{15,29},{16,2}... | collective-permute-start | bytes 1572872 | tf_op jit(solution)/shard_map/ppermute | solution.py:506
  68.3 6.5 %collective-permute-done.21.recv_ref = f32[3,32,128]{2,1,0:T(8,128)S(1)} collective-permute-done((f32[3,32,128]{2,1,0:T(8,128)S(1)}, f32[3,32,128]{2,1,0:T(8,128)S(1)}, u32[]{:S(2)}, u32[]{:S(2)}) %collective-permute-start.21) | collective-permute-done | bytes 49184 | tf_op jit(solution)/shard_map/ppermute | solution.py:506
  74.9 1.2 %collective-permute-done.22.other_ref = f32[3,32,128]{2,1,0:T(8,128)S(1)} collective-permute-done((f32[3,32,128]{2,1,0:T(8,128)S(1)}, f32[3,32,128]{2,1,0:T(8,128)S(1)}, u32[]{:S(2)}, u32[]{:S(2)}) %collective-permute-start.22) | collective-permute-done | bytes 49184 | tf_op jit(solution)/shard_map/ppermute | solution.py:506
  76.3 6.4 %collective-permute-done.23.moved_ref = f32[2,3,32,128]{3,2,1,0:T(8,128)S(1)} collective-permute-done((f32[2,3,32,128]{3,2,1,0:T(8,128)S(1)}, f32[2,3,32,128]{3,2,1,0:T(8,128)S(1)}, u32[]{:S(2)}, u32[]{:S(2)}) %collective-permute-start.23) | collective-permute-done | bytes 98336 | tf_op jit(solution)/shard_map/ppermute | solution.py:506
  82.8 3.5 %collective-permute-done.24.other_ref = f32[1,2,3,32,128]{4,3,2,1,0:T(8,128)S(1)} collective-permute-done((f32[1,2,3,32,128]{4,3,2,1,0:T(8,128)S(1)}, f32[1,2,3,32,128]{4,3,2,1,0:T(8,128)S(1)}, u32[]{:S(2)}, u32[]{:S(2)}) %collective-permute-start.24) | collective-permute-done | bytes 98336 | tf_op jit(solution)/shard_map/ppermute | solution.py:506
  86.3 1.3 %collective-permute-start.25 = (f32[2,2,3,32,128]{4,3,2,1,0:T(8,128)S(1)}, f32[2,2,3,32,128]{4,3,2,1,0:T(8,128)S(1)}, u32[]{:S(2)}, u32[]{:S(2)}) collective-permute-start(f32[2,2,3,32,128]{4,3,2,1,0:T(8,128)S(1)} %bitcast.32), channel_id=1, source_target_pairs={{0,8},{1,9},{2,6},{3,7},{4,12},{5,13},{6,2},{7,3},{8,0},{9,1},{10,... | collective-permute-start | bytes 589832 | tf_op jit(solution)/shard_map/ppermute | solution.py:506
  87.5 3.3 %collective-permute-done.25.other_ref = f32[2,2,3,32,128]{4,3,2,1,0:T(8,128)S(1)} collective-permute-done((f32[2,2,3,32,128]{4,3,2,1,0:T(8,128)S(1)}, f32[2,2,3,32,128]{4,3,2,1,0:T(8,128)S(1)}, u32[]{:S(2)}, u32[]{:S(2)}) %collective-permute-start.25) | collective-permute-done | bytes 196640 | tf_op jit(solution)/shard_map/ppermute | solution.py:506
  90.9 1.6 %collective-permute-start.26 = (f32[4,2,3,32,128]{4,3,2,1,0:T(8,128)S(1)}, f32[4,2,3,32,128]{4,3,2,1,0:T(8,128)S(1)}, u32[]{:S(2)}, u32[]{:S(2)}) collective-permute-start(f32[4,2,3,32,128]{4,3,2,1,0:T(8,128)S(1)} %bitcast.29), channel_id=1, source_target_pairs={{0,4},{1,5},{2,3},{3,2},{4,0},{5,1},{6,7},{7,6},{8,12},{9,13},{10,... | collective-permute-start | bytes 1179656 | tf_op jit(solution)/shard_map/ppermute | solution.py:506
  93.2 4.7 %collective-permute-done.26.recv_ref = f32[4,2,3,32,128]{4,3,2,1,0:T(8,128)S(1)} collective-permute-done((f32[4,2,3,32,128]{4,3,2,1,0:T(8,128)S(1)}, f32[4,2,3,32,128]{4,3,2,1,0:T(8,128)S(1)}, u32[]{:S(2)}, u32[]{:S(2)}) %collective-permute-start.26) | collective-permute-done | bytes 393248 | tf_op jit(solution)/shard_map/ppermute | solution.py:506
  (67 shorter events, 12.5 us)
Async XLA Ops:
  0.6 8.5 %copy-start = (bf16[1,3,128,1,256]{4,2,3,1,0:T(8,128)(2,1)S(1)}, bf16[1,3,128,1,256]{4,2,3,1,0:T(8,128)(2,1)}, u32[]{:S(2)}) copy-start(bf16[1,3,128,1,256]{4,2,3,1,0:T(8,128)(2,1)} %param.6) | copy-start | bytes 589828
  0.6 8.5 %copy-start.1 = (bf16[1,3,128,1,256]{4,2,3,1,0:T(8,128)(2,1)S(1)}, bf16[1,3,128,1,256]{4,2,3,1,0:T(8,128)(2,1)}, u32[]{:S(2)}) copy-start(bf16[1,3,128,1,256]{4,2,3,1,0:T(8,128)(2,1)} %param.9) | copy-start | bytes 589828
  2.3 8.7 %collective-permute-start = (f32[2,128,256]{2,1,0:T(8,128)}, f32[2,128,256]{2,1,0:T(8,128)S(1)}, u32[]{:S(2)}, u32[]{:S(2)}) collective-permute-start(f32[2,128,256]{2,1,0:T(8,128)} %shard_map.93.refs_0_), channel_id=1, source_target_pairs={{0,2},{1,3},{2,18},{3,19},{4,6},{5,7},{6,22},{7,23},{8,10},{9,11},... | collective-permute-start | bytes 786440 | tf_op jit(solution)/shard_map/ppermute | solution.py:506
  9.0 3.5 %copy-start.5 = (bf16[1,3,128,1,256]{4,2,3,1,0:T(8,128)(2,1)S(1)}, bf16[1,3,128,1,256]{4,2,3,1,0:T(8,128)(2,1)}, u32[]{:S(2)}) copy-start(bf16[1,3,128,1,256]{4,2,3,1,0:T(8,128)(2,1)} %param.7) | copy-start | bytes 589828
  9.0 3.5 %copy-start.6 = (bf16[1,3,128,1,256]{4,2,3,1,0:T(8,128)(2,1)S(1)}, bf16[1,3,128,1,256]{4,2,3,1,0:T(8,128)(2,1)}, u32[]{:S(2)}) copy-start(bf16[1,3,128,1,256]{4,2,3,1,0:T(8,128)(2,1)} %param.8) | copy-start | bytes 589828
  9.0 6.7 %collective-permute-start.2 = (f32[768,128]{1,0:T(8,128)S(1)}, f32[768,128]{1,0:T(8,128)S(1)}, u32[]{:S(2)}, u32[]{:S(2)}) collective-permute-start(f32[768,128]{1,0:T(8,128)S(1)} %get-tuple-element.65), channel_id=1, source_target_pairs={{0,2},{1,3},{2,0},{3,1},{4,6},{5,7},{6,4},{7,5},{8,10},{9,11},{10,... | collective-permute-start | bytes 1179656 | tf_op jit(solution)/shard_map/ppermute | solution.py:506
  11.0 5.1 %copy-start.3 = (f32[2,128,256]{2,1,0:T(8,128)S(1)}, f32[2,128,256]{2,1,0:T(8,128)}, u32[]{:S(2)}) copy-start(f32[2,128,256]{2,1,0:T(8,128)} %shard_map.93.refs_0_) | copy-start | bytes 786436
  11.0 5.1 %collective-permute-start.1 = (f32[2,128,256]{2,1,0:T(8,128)S(1)}, f32[2,128,256]{2,1,0:T(8,128)S(1)}, u32[]{:S(2)}, u32[]{:S(2)}) collective-permute-start(f32[2,128,256]{2,1,0:T(8,128)S(1)} %collective-permute-done.refs_1_), channel_id=1, source_target_pairs={{0,2},{1,3},{4,6},{5,7},{8,10},{9,11},{12,14},{13,15},{18,16},{19,... | collective-permute-start | bytes 786440 | tf_op jit(solution)/shard_map/ppermute | solution.py:506
  12.9 16.6 %collective-permute-start.6 = (f32[4,128,256]{2,1,0:T(8,128)S(1)}, f32[4,128,256]{2,1,0:T(8,128)S(1)}, u32[]{:S(2)}, u32[]{:S(2)}) collective-permute-start(f32[4,128,256]{2,1,0:T(8,128)S(1)} %get-tuple-element.70), channel_id=1, source_target_pairs={{0,2},{1,3},{2,18},{3,19},{4,6},{5,7},{6,22},{7,23},{8,10},{9,11},... | collective-permute-start | bytes 1572872 | tf_op jit(solution)/shard_map/ppermute | solution.py:506
  16.8 11.6 %collective-permute-start.3 = (f32[776,128]{1,0:T(8,128)S(1)}, f32[776,128]{1,0:T(8,128)S(1)}, u32[]{:S(2)}, u32[]{:S(2)}) collective-permute-start(f32[776,128]{1,0:T(8,128)S(1)} %shard_map.97.mine_ref), channel_id=1, source_target_pairs={{0,4},{1,5},{2,10},{3,11},{4,0},{5,1},{6,14},{7,15},{8,12},{9,13},... | collective-permute-start | bytes 1191944 | tf_op jit(solution)/shard_map/ppermute | solution.py:506
  18.5 16.8 %collective-permute-start.9 = (f32[1560,128]{1,0:T(8,128)S(1)}, f32[1560,128]{1,0:T(8,128)S(1)}, u32[]{:S(2)}, u32[]{:S(2)}) collective-permute-start(f32[1560,128]{1,0:T(8,128)S(1)} %get-tuple-element.78), channel_id=1, source_target_pairs={{0,2},{1,3},{2,0},{3,1},{4,6},{5,7},{6,4},{7,5},{8,10},{9,11},{10,... | collective-permute-start | bytes 2396168 | tf_op jit(solution)/shard_map/ppermute | solution.py:506
  28.4 6.7 %collective-permute-start.4 = (f32[776,128]{1,0:T(8,128)S(1)}, f32[776,128]{1,0:T(8,128)S(1)}, u32[]{:S(2)}, u32[]{:S(2)}) collective-permute-start(f32[776,128]{1,0:T(8,128)S(1)} %shard_map.98.mine_ref), channel_id=1, source_target_pairs={{0,8},{1,9},{2,6},{3,7},{4,12},{5,13},{6,2},{7,3},{8,0},{9,1},{10,... | collective-permute-start | bytes 1191944 | tf_op jit(solution)/shard_map/ppermute | solution.py:506
  29.6 5.8 %collective-permute-start.7 = (f32[2,128,256]{2,1,0:T(8,128)S(1)}, f32[2,128,256]{2,1,0:T(8,128)S(1)}, u32[]{:S(2)}, u32[]{:S(2)}) collective-permute-start(f32[2,128,256]{2,1,0:T(8,128)S(1)} %get-tuple-element.72.refs_1_), channel_id=1, source_target_pairs={{0,2},{1,3},{4,6},{5,7},{8,10},{9,11},{12,14},{13,15},{18,16},{19,... | collective-permute-start | bytes 786440 | tf_op jit(solution)/shard_map/ppermute | solution.py:506
  30.9 4.5 %collective-permute-start.8 = (f32[2,128,256]{2,1,0:T(8,128)S(1)}, f32[2,128,256]{2,1,0:T(8,128)S(1)}, u32[]{:S(2)}, u32[]{:S(2)}) collective-permute-start(f32[2,128,256]{2,1,0:T(8,128)S(1)} %get-tuple-element.75.refs_4_), channel_id=1, source_target_pairs={{0,2},{1,3},{4,6},{5,7},{8,10},{9,11},{12,14},{13,15},{18,16},{19,... | collective-permute-start | bytes 786440 | tf_op jit(solution)/shard_map/ppermute | solution.py:506
  32.6 19.0 %collective-permute-start.14 = (f32[4,128,256]{2,1,0:T(8,128)S(1)}, f32[4,128,256]{2,1,0:T(8,128)S(1)}, u32[]{:S(2)}, u32[]{:S(2)}) collective-permute-start(f32[4,128,256]{2,1,0:T(8,128)S(1)} %get-tuple-element.94), channel_id=1, source_target_pairs={{0,2},{1,3},{2,18},{3,19},{4,6},{5,7},{6,22},{7,23},{8,10},{9,11},... | collective-permute-start | bytes 1572872 | tf_op jit(solution)/shard_map/ppermute | solution.py:506
  35.2 1.2 %collective-permute-start.5 = (f32[8,128]{1,0:T(8,128)S(1)}, f32[8,128]{1,0:T(8,128)S(1)}, u32[]{:S(2)}, u32[]{:S(2)}) collective-permute-start(f32[8,128]{1,0:T(8,128)S(1)} %get-tuple-element.67.refs_1_), channel_id=1, source_target_pairs={{0,2},{1,3},{2,0},{3,1},{4,6},{5,7},{6,4},{7,5},{8,10},{9,11},{10,... | collective-permute-start | bytes 12296 | tf_op jit(solution)/shard_map/ppermute | solution.py:506
  37.1 12.7 %collective-permute-start.10 = (f32[776,128]{1,0:T(8,128)S(1)}, f32[776,128]{1,0:T(8,128)S(1)}, u32[]{:S(2)}, u32[]{:S(2)}) collective-permute-start(f32[776,128]{1,0:T(8,128)S(1)} %get-tuple-element.84.mine_ref), channel_id=1, source_target_pairs={{0,4},{1,5},{2,10},{3,11},{4,0},{5,1},{6,14},{7,15},{8,12},{9,13},... | collective-permute-start | bytes 1191944 | tf_op jit(solution)/shard_map/ppermute | solution.py:506
  37.8 2.8 %collective-permute-start.11 = (f32[2,128,256]{2,1,0:T(8,128)S(1)}, f32[2,128,256]{2,1,0:T(8,128)S(1)}, u32[]{:S(2)}, u32[]{:S(2)}) collective-permute-start(f32[2,128,256]{2,1,0:T(8,128)S(1)} %get-tuple-element.88), channel_id=1, source_target_pairs={{0,2},{1,3},{2,0},{3,1},{4,6},{5,7},{6,4},{7,5},{8,10},{9,11},{10,... | collective-permute-start | bytes 786440 | tf_op jit(solution)/shard_map/ppermute | solution.py:506
  49.9 6.9 %collective-permute-start.12 = (f32[776,128]{1,0:T(8,128)S(1)}, f32[776,128]{1,0:T(8,128)S(1)}, u32[]{:S(2)}, u32[]{:S(2)}) collective-permute-start(f32[776,128]{1,0:T(8,128)S(1)} %shard_map.107.mine_ref), channel_id=1, source_target_pairs={{0,8},{1,9},{2,6},{3,7},{4,12},{5,13},{6,2},{7,3},{8,0},{9,1},{10,... | collective-permute-start | bytes 1191944 | tf_op jit(solution)/shard_map/ppermute | solution.py:506
  51.6 5.3 %collective-permute-start.16 = (f32[2,128,256]{2,1,0:T(8,128)S(1)}, f32[2,128,256]{2,1,0:T(8,128)S(1)}, u32[]{:S(2)}, u32[]{:S(2)}) collective-permute-start(f32[2,128,256]{2,1,0:T(8,128)S(1)} %get-tuple-element.99.refs_4_), channel_id=1, source_target_pairs={{0,2},{1,3},{4,6},{5,7},{8,10},{9,11},{12,14},{13,15},{18,16},{19,... | collective-permute-start | bytes 786440 | tf_op jit(solution)/shard_map/ppermute | solution.py:506
  52.9 4.0 %collective-permute-start.15 = (f32[2,128,256]{2,1,0:T(8,128)S(1)}, f32[2,128,256]{2,1,0:T(8,128)S(1)}, u32[]{:S(2)}, u32[]{:S(2)}) collective-permute-start(f32[2,128,256]{2,1,0:T(8,128)S(1)} %get-tuple-element.96.refs_1_), channel_id=1, source_target_pairs={{0,2},{1,3},{4,6},{5,7},{8,10},{9,11},{12,14},{13,15},{18,16},{19,... | collective-permute-start | bytes 786440 | tf_op jit(solution)/shard_map/ppermute | solution.py:506
  56.8 1.2 %collective-permute-start.13 = (f32[8,128]{1,0:T(8,128)S(1)}, f32[8,128]{1,0:T(8,128)S(1)}, u32[]{:S(2)}, u32[]{:S(2)}) collective-permute-start(f32[8,128]{1,0:T(8,128)S(1)} %get-tuple-element.91.refs_1_), channel_id=1, source_target_pairs={{0,2},{1,3},{2,0},{3,1},{4,6},{5,7},{6,4},{7,5},{8,10},{9,11},{10,... | collective-permute-start | bytes 12296 | tf_op jit(solution)/shard_map/ppermute | solution.py:506
  58.8 4.9 %collective-permute-start.19 = (f32[3,128,128]{2,1,0:T(8,128)S(1)}, f32[3,128,128]{2,1,0:T(8,128)S(1)}, u32[]{:S(2)}, u32[]{:S(2)}) collective-permute-start(f32[3,128,128]{2,1,0:T(8,128)S(1)} %get-tuple-element.112), channel_id=1, source_target_pairs={{0,4},{1,5},{2,3},{3,2},{4,0},{5,1},{6,7},{7,6},{8,12},{9,13},{10,... | collective-permute-start | bytes 589832 | tf_op jit(solution)/shard_map/ppermute | solution.py:506
  60.7 4.6 %collective-permute-start.17 = (f32[2,128,256]{2,1,0:T(8,128)S(1)}, f32[2,128,256]{2,1,0:T(8,128)S(1)}, u32[]{:S(2)}, u32[]{:S(2)}) collective-permute-start(f32[2,128,256]{2,1,0:T(8,128)S(1)} %get-tuple-element.108), channel_id=1, source_target_pairs={{0,2},{1,3},{2,0},{3,1},{4,6},{5,7},{6,4},{7,5},{8,10},{9,11},{10,... | collective-permute-start | bytes 786440 | tf_op jit(solution)/shard_map/ppermute | solution.py:506
  63.7 4.5 %collective-permute-start.20 = (f32[3,64,128]{2,1,0:T(8,128)S(1)}, f32[3,64,128]{2,1,0:T(8,128)S(1)}, u32[]{:S(2)}, u32[]{:S(2)}) collective-permute-start(f32[3,64,128]{2,1,0:T(8,128)S(1)} %get-tuple-element.114), channel_id=1, source_target_pairs={{0,8},{1,9},{2,6},{3,7},{4,12},{5,13},{6,2},{7,3},{8,0},{9,1},{10,... | collective-permute-start | bytes 294920 | tf_op jit(solution)/shard_map/ppermute | solution.py:506
  65.3 22.2 %collective-permute-start.18 = (f32[4,128,256]{2,1,0:T(8,128)S(1)}, f32[4,128,256]{2,1,0:T(8,128)S(1)}, u32[]{:S(2)}, u32[]{:S(2)}) collective-permute-start(f32[4,128,256]{2,1,0:T(8,128)S(1)} %shard_map.114.own_ref), channel_id=1, source_target_pairs={{2,16},{3,17},{6,20},{7,21},{10,24},{11,25},{14,28},{15,29},{16,2}... | collective-permute-start | bytes 1572872 | tf_op jit(solution)/shard_map/ppermute | solution.py:506
  68.3 6.6 %collective-permute-start.21 = (f32[3,32,128]{2,1,0:T(8,128)S(1)}, f32[3,32,128]{2,1,0:T(8,128)S(1)}, u32[]{:S(2)}, u32[]{:S(2)}) collective-permute-start(f32[3,32,128]{2,1,0:T(8,128)S(1)} %get-tuple-element.116), channel_id=1, source_target_pairs={{0,1},{1,0},{2,10},{3,11},{4,5},{5,4},{6,14},{7,15},{8,9},{9,8},{1... | collective-permute-start | bytes 147464 | tf_op jit(solution)/shard_map/ppermute | solution.py:506
  74.9 1.2 %collective-permute-start.22 = (f32[3,32,128]{2,1,0:T(8,128)S(1)}, f32[3,32,128]{2,1,0:T(8,128)S(1)}, u32[]{:S(2)}, u32[]{:S(2)}) collective-permute-start(f32[3,32,128]{2,1,0:T(8,128)S(1)} %shard_map.118.mine_ref), channel_id=1, source_target_pairs={{0,2},{1,3},{2,0},{3,1},{4,6},{5,7},{6,4},{7,5},{8,10},{9,11},{10,... | collective-permute-start | bytes 147464 | tf_op jit(solution)/shard_map/ppermute | solution.py:506
  76.1 6.6 %collective-permute-start.23 = (f32[2,3,32,128]{3,2,1,0:T(8,128)S(1)}, f32[2,3,32,128]{3,2,1,0:T(8,128)S(1)}, u32[]{:S(2)}, u32[]{:S(2)}) collective-permute-start(f32[2,3,32,128]{3,2,1,0:T(8,128)S(1)} %shard_map.119.own_ref), channel_id=1, source_target_pairs={{0,16},{1,17},{2,0},{3,1},{4,20},{5,21},{6,4},{7,5},{8,24},{9,25},... | collective-permute-start | bytes 294920 | tf_op jit(solution)/shard_map/ppermute | solution.py:506
  82.7 3.5 %collective-permute-start.24 = (f32[1,2,3,32,128]{4,3,2,1,0:T(8,128)S(1)}, f32[1,2,3,32,128]{4,3,2,1,0:T(8,128)S(1)}, u32[]{:S(2)}, u32[]{:S(2)}) collective-permute-start(f32[1,2,3,32,128]{4,3,2,1,0:T(8,128)S(1)} %bitcast.38), channel_id=1, source_target_pairs={{0,1},{1,0},{2,10},{3,11},{4,5},{5,4},{6,14},{7,15},{8,9},{9,8},{1... | collective-permute-start | bytes 294920 | tf_op jit(solution)/shard_map/ppermute | solution.py:506
  86.3 4.6 %collective-permute-start.25 = (f32[2,2,3,32,128]{4,3,2,1,0:T(8,128)S(1)}, f32[2,2,3,32,128]{4,3,2,1,0:T(8,128)S(1)}, u32[]{:S(2)}, u32[]{:S(2)}) collective-permute-start(f32[2,2,3,32,128]{4,3,2,1,0:T(8,128)S(1)} %bitcast.32), channel_id=1, source_target_pairs={{0,8},{1,9},{2,6},{3,7},{4,12},{5,13},{6,2},{7,3},{8,0},{9,1},{10,... | collective-permute-start | bytes 589832 | tf_op jit(solution)/shard_map/ppermute | solution.py:506
  90.9 7.0 %collective-permute-start.26 = (f32[4,2,3,32,128]{4,3,2,1,0:T(8,128)S(1)}, f32[4,2,3,32,128]{4,3,2,1,0:T(8,128)S(1)}, u32[]{:S(2)}, u32[]{:S(2)}) collective-permute-start(f32[4,2,3,32,128]{4,3,2,1,0:T(8,128)S(1)} %bitcast.29), channel_id=1, source_target_pairs={{0,4},{1,5},{2,3},{3,2},{4,0},{5,1},{6,7},{7,6},{8,12},{9,13},{10,... | collective-permute-start | bytes 1179656 | tf_op jit(solution)/shard_map/ppermute | solution.py:506
  (2 other events, 2.1 us)

commit v7 on v6

--- a/solution.py
+++ b/solution.py
@@ -690,7 +690,7 @@
         functools.partial(choose_kernel, tok_count), [shape(*pair.shape)], pair, lend(pair)
     )
     block = wait(block[None], 3)
-    ag_orders = [order[::-1] for order in rs_orders]
+    ag_orders = [vid_dims + tok_dims, tok_dims + vid_dims]
     for at in range(len(dims)):
         arrived = wait(meet(block, [order[at] for order in ag_orders]), 4 + at)
         if at + 1 < len(dims):

time: 99.8 us -> 99.8 us (level)
  no operation moved by 1% of the time
where the time goes in v7:
time: 99.8 us; the launch traced here: 99.1 us
  waiting for transfers between devices  52.2 us (52%)
  starting transfers between devices  30.7 us (31%)
  Pallas kernels  13.1 us (13%)
  local copies, waits for them, and re-layouts  2.15 us (2%)
  between operations  1.01 us (1%)
    ppermute x27, waiting for transfers between devices, permute(): return lax.ppermute(array, ('tok', 'head', 'vid'), pairs)  52.2 us
    ppermute x27, starting transfers between devices, permute(): return lax.ppermute(array, ('tok', 'head', 'vid'), pairs)  30.7 us
    pallas_call x31, Pallas kernels, call(): pl.pallas_call(kernel, out_shape=outs, **kwargs, scratch_shapes=scratch,...  13.1 us
    unnamed x14, local copies, waits for them, and re-layouts  2.15 us
  transfers between devices with their start and end apart: 27, of which 15 were waited for; matrix products, arithmetic and copies ran while one was open for 0% of the time, Pallas kernels for 10%

profile of v7, /device:TPU:1, one launch (start us, length us, event | category | flops | bytes accessed | tf_op | source)
XLA Modules:
  0.0 99.1 jit_solution(14432882195258970829)
XLA Ops:
  0.7 1.7 %shard_map.93.refs_0_ = f32[2,128,256]{2,1,0:T(8,128)} custom-call(bf16[3,128,256]{2,1,0:T(8,128)(2,1)} %bitcast.19, bf16[3,128,256]{2,1,0:T(8,128)(2,1)} %bitcast.23), custom_call_target="tpu_custom_call" | custom-call | flops 1 | bytes 1 | tf_op jit(solution)/shard_map/pallas_call | solution.py:452
  2.3 3.2 %collective-permute-start = (f32[2,128,256]{2,1,0:T(8,128)}, f32[2,128,256]{2,1,0:T(8,128)S(1)}, u32[]{:S(2)}, u32[]{:S(2)}) collective-permute-start(f32[2,128,256]{2,1,0:T(8,128)} %shard_map.93.refs_0_), channel_id=1, source_target_pairs={{0,2},{1,3},{2,18},{3,19},{4,6},{5,7},{6,22},{7,23},{8,10},{9,11},... | collective-permute-start | bytes 786440 | tf_op jit(solution)/shard_map/ppermute | solution.py:506
  6.5 1.1 %copy-done.4 = bf16[1,2,1,3,256,256]{5,4,3,2,1,0:T(8,128)(2,1)S(1)} copy-done((bf16[1,2,1,3,256,256]{5,4,3,2,1,0:T(8,128)(2,1)S(1)}, bf16[1,2,1,3,256,256]{5,4,3,2,1,0:T(8,128)(2,1)}, u32[]{:S(2)}) %copy-start.4) | copy-done | bytes 786456
  7.6 1.3 %shard_map.94 = (f32[2,3,256,256]{3,2,1,0:T(8,128)S(1)}, f32[768,128]{1,0:T(8,128)S(1)}, f32[1560,128]{1,0:T(8,128)S(1)}, f32[768,128]{1,0:T(8,128)S(1)}, f32[1560,128]{1,0:T(8,128)S(1)}) custom-call(bf16[3,256,256]{2,1,0:T(8,128)(2,1)S(1)} %bitcast.27, bf16[2,3,256,256]{3,2,1,0:T(8,128)(2,1)S(1)} %bitcast.31), custom_call_target="tpu_custom_call" | custom-call | flops 1 | bytes 1 | tf_op jit(solution)/shard_map/pallas_call | solution.py:452
  9.1 1.9 %shard_map.95 = bf16[3,128,256]{2,1,0:T(8,128)(2,1)} custom-call(bf16[3,128,256]{2,1,0:T(8,128)(2,1)S(1)} %bitcast.20, bf16[3,128,256]{2,1,0:T(8,128)(2,1)S(1)} %bitcast.24, bf16[3,256,256]{2,1,0:T(8,128)(2,1)S(1)} %bitcast.28, f32[2,3,256,256]{3,2,1,0:T(8,128)S(1)} %get-tuple-element.62.full_ref), custom_call_target="tpu_custom_call" | custom-call | flops 1 | bytes 1 | tf_op jit(solution)/shard_map/pallas_call | solution.py:452
  11.0 1.4 %collective-permute-start.1 = (f32[2,128,256]{2,1,0:T(8,128)S(1)}, f32[2,128,256]{2,1,0:T(8,128)S(1)}, u32[]{:S(2)}, u32[]{:S(2)}) collective-permute-start(f32[2,128,256]{2,1,0:T(8,128)S(1)} %collective-permute-done.refs_1_), channel_id=1, source_target_pairs={{0,2},{1,3},{4,6},{5,7},{8,10},{9,11},{12,14},{13,15},{18,16},{19,... | collective-permute-start | bytes 786440 | tf_op jit(solution)/shard_map/ppermute | solution.py:506
  12.9 2.7 %collective-permute-start.6 = (f32[4,128,256]{2,1,0:T(8,128)S(1)}, f32[4,128,256]{2,1,0:T(8,128)S(1)}, u32[]{:S(2)}, u32[]{:S(2)}) collective-permute-start(f32[4,128,256]{2,1,0:T(8,128)S(1)} %get-tuple-element.70), channel_id=1, source_target_pairs={{0,2},{1,3},{2,18},{3,19},{4,6},{5,7},{6,22},{7,23},{8,10},{9,11},... | collective-permute-start | bytes 1572872 | tf_op jit(solution)/shard_map/ppermute | solution.py:506
  16.8 1.7 %collective-permute-start.3 = (f32[776,128]{1,0:T(8,128)S(1)}, f32[776,128]{1,0:T(8,128)S(1)}, u32[]{:S(2)}, u32[]{:S(2)}) collective-permute-start(f32[776,128]{1,0:T(8,128)S(1)} %shard_map.97.mine_ref), channel_id=1, source_target_pairs={{0,4},{1,5},{2,10},{3,11},{4,0},{5,1},{6,14},{7,15},{8,12},{9,13},... | collective-permute-start | bytes 1191944 | tf_op jit(solution)/shard_map/ppermute | solution.py:506
  18.8 9.5 %collective-permute-done.3.recv_ref = f32[776,128]{1,0:T(8,128)S(1)} collective-permute-done((f32[776,128]{1,0:T(8,128)S(1)}, f32[776,128]{1,0:T(8,128)S(1)}, u32[]{:S(2)}, u32[]{:S(2)}) %collective-permute-start.3) | collective-permute-done | bytes 397344 | tf_op jit(solution)/shard_map/ppermute | solution.py:506
  28.4 1.1 %collective-permute-start.4 = (f32[776,128]{1,0:T(8,128)S(1)}, f32[776,128]{1,0:T(8,128)S(1)}, u32[]{:S(2)}, u32[]{:S(2)}) collective-permute-start(f32[776,128]{1,0:T(8,128)S(1)} %shard_map.98.mine_ref), channel_id=1, source_target_pairs={{0,8},{1,9},{2,6},{3,7},{4,12},{5,13},{6,2},{7,3},{8,0},{9,1},{10,... | collective-permute-start | bytes 1191944 | tf_op jit(solution)/shard_map/ppermute | solution.py:506
  29.6 1.3 %collective-permute-start.7 = (f32[2,128,256]{2,1,0:T(8,128)S(1)}, f32[2,128,256]{2,1,0:T(8,128)S(1)}, u32[]{:S(2)}, u32[]{:S(2)}) collective-permute-start(f32[2,128,256]{2,1,0:T(8,128)S(1)} %get-tuple-element.72.refs_1_), channel_id=1, source_target_pairs={{0,2},{1,3},{4,6},{5,7},{8,10},{9,11},{12,14},{13,15},{18,16},{19,... | collective-permute-start | bytes 786440 | tf_op jit(solution)/shard_map/ppermute | solution.py:506
  30.9 1.3 %collective-permute-start.8 = (f32[2,128,256]{2,1,0:T(8,128)S(1)}, f32[2,128,256]{2,1,0:T(8,128)S(1)}, u32[]{:S(2)}, u32[]{:S(2)}) collective-permute-start(f32[2,128,256]{2,1,0:T(8,128)S(1)} %get-tuple-element.75.refs_4_), channel_id=1, source_target_pairs={{0,2},{1,3},{4,6},{5,7},{8,10},{9,11},{12,14},{13,15},{18,16},{19,... | collective-permute-start | bytes 786440 | tf_op jit(solution)/shard_map/ppermute | solution.py:506
  32.6 1.9 %collective-permute-start.14 = (f32[4,128,256]{2,1,0:T(8,128)S(1)}, f32[4,128,256]{2,1,0:T(8,128)S(1)}, u32[]{:S(2)}, u32[]{:S(2)}) collective-permute-start(f32[4,128,256]{2,1,0:T(8,128)S(1)} %get-tuple-element.94), channel_id=1, source_target_pairs={{0,2},{1,3},{2,18},{3,19},{4,6},{5,7},{6,22},{7,23},{8,10},{9,11},... | collective-permute-start | bytes 1572872 | tf_op jit(solution)/shard_map/ppermute | solution.py:506
  37.8 1.6 %collective-permute-start.11 = (f32[2,128,256]{2,1,0:T(8,128)S(1)}, f32[2,128,256]{2,1,0:T(8,128)S(1)}, u32[]{:S(2)}, u32[]{:S(2)}) collective-permute-start(f32[2,128,256]{2,1,0:T(8,128)S(1)} %get-tuple-element.88), channel_id=1, source_target_pairs={{0,2},{1,3},{2,0},{3,1},{4,6},{5,7},{6,4},{7,5},{8,10},{9,11},{10,... | collective-permute-start | bytes 786440 | tf_op jit(solution)/shard_map/ppermute | solution.py:506
  39.4 1.2 %collective-permute-done.11.recv_ref = f32[2,128,256]{2,1,0:T(8,128)S(1)} collective-permute-done((f32[2,128,256]{2,1,0:T(8,128)S(1)}, f32[2,128,256]{2,1,0:T(8,128)S(1)}, u32[]{:S(2)}, u32[]{:S(2)}) %collective-permute-start.11) | collective-permute-done | bytes 262176 | tf_op jit(solution)/shard_map/ppermute | solution.py:506
  40.6 9.2 %collective-permute-done.10.recv_ref = f32[776,128]{1,0:T(8,128)S(1)} collective-permute-done((f32[776,128]{1,0:T(8,128)S(1)}, f32[776,128]{1,0:T(8,128)S(1)}, u32[]{:S(2)}, u32[]{:S(2)}) %collective-permute-start.10) | collective-permute-done | bytes 397344 | tf_op jit(solution)/shard_map/ppermute | solution.py:506
  49.9 1.7 %collective-permute-start.12 = (f32[776,128]{1,0:T(8,128)S(1)}, f32[776,128]{1,0:T(8,128)S(1)}, u32[]{:S(2)}, u32[]{:S(2)}) collective-permute-start(f32[776,128]{1,0:T(8,128)S(1)} %shard_map.107.mine_ref), channel_id=1, source_target_pairs={{0,8},{1,9},{2,6},{3,7},{4,12},{5,13},{6,2},{7,3},{8,0},{9,1},{10,... | collective-permute-start | bytes 1191944 | tf_op jit(solution)/shard_map/ppermute | solution.py:506
  51.6 1.3 %collective-permute-start.16 = (f32[2,128,256]{2,1,0:T(8,128)S(1)}, f32[2,128,256]{2,1,0:T(8,128)S(1)}, u32[]{:S(2)}, u32[]{:S(2)}) collective-permute-start(f32[2,128,256]{2,1,0:T(8,128)S(1)} %get-tuple-element.99.refs_4_), channel_id=1, source_target_pairs={{0,2},{1,3},{4,6},{5,7},{8,10},{9,11},{12,14},{13,15},{18,16},{19,... | collective-permute-start | bytes 786440 | tf_op jit(solution)/shard_map/ppermute | solution.py:506
  52.9 1.3 %collective-permute-start.15 = (f32[2,128,256]{2,1,0:T(8,128)S(1)}, f32[2,128,256]{2,1,0:T(8,128)S(1)}, u32[]{:S(2)}, u32[]{:S(2)}) collective-permute-start(f32[2,128,256]{2,1,0:T(8,128)S(1)} %get-tuple-element.96.refs_1_), channel_id=1, source_target_pairs={{0,2},{1,3},{4,6},{5,7},{8,10},{9,11},{12,14},{13,15},{18,16},{19,... | collective-permute-start | bytes 786440 | tf_op jit(solution)/shard_map/ppermute | solution.py:506
  54.2 2.6 %collective-permute-done.12.recv_ref = f32[776,128]{1,0:T(8,128)S(1)} collective-permute-done((f32[776,128]{1,0:T(8,128)S(1)}, f32[776,128]{1,0:T(8,128)S(1)}, u32[]{:S(2)}, u32[]{:S(2)}) %collective-permute-start.12) | collective-permute-done | bytes 397344 | tf_op jit(solution)/shard_map/ppermute | solution.py:506
  58.8 1.3 %collective-permute-start.19 = (f32[3,128,128]{2,1,0:T(8,128)S(1)}, f32[3,128,128]{2,1,0:T(8,128)S(1)}, u32[]{:S(2)}, u32[]{:S(2)}) collective-permute-start(f32[3,128,128]{2,1,0:T(8,128)S(1)} %get-tuple-element.112), channel_id=1, source_target_pairs={{0,4},{1,5},{2,3},{3,2},{4,0},{5,1},{6,7},{7,6},{8,12},{9,13},{10,... | collective-permute-start | bytes 589832 | tf_op jit(solution)/shard_map/ppermute | solution.py:506
  61.4 2.3 %collective-permute-done.19.recv_ref = f32[3,128,128]{2,1,0:T(8,128)S(1)} collective-permute-done((f32[3,128,128]{2,1,0:T(8,128)S(1)}, f32[3,128,128]{2,1,0:T(8,128)S(1)}, u32[]{:S(2)}, u32[]{:S(2)}) %collective-permute-start.19) | collective-permute-done | bytes 196640 | tf_op jit(solution)/shard_map/ppermute | solution.py:506
  63.7 1.5 %collective-permute-start.20 = (f32[3,64,128]{2,1,0:T(8,128)S(1)}, f32[3,64,128]{2,1,0:T(8,128)S(1)}, u32[]{:S(2)}, u32[]{:S(2)}) collective-permute-start(f32[3,64,128]{2,1,0:T(8,128)S(1)} %get-tuple-element.114), channel_id=1, source_target_pairs={{0,8},{1,9},{2,6},{3,7},{4,12},{5,13},{6,2},{7,3},{8,0},{9,1},{10,... | collective-permute-start | bytes 294920 | tf_op jit(solution)/shard_map/ppermute | solution.py:506
  65.3 2.9 %collective-permute-start.18 = (f32[4,128,256]{2,1,0:T(8,128)S(1)}, f32[4,128,256]{2,1,0:T(8,128)S(1)}, u32[]{:S(2)}, u32[]{:S(2)}) collective-permute-start(f32[4,128,256]{2,1,0:T(8,128)S(1)} %shard_map.114.own_ref), channel_id=1, source_target_pairs={{2,16},{3,17},{6,20},{7,21},{10,24},{11,25},{14,28},{15,29},{16,2}... | collective-permute-start | bytes 1572872 | tf_op jit(solution)/shard_map/ppermute | solution.py:506
  68.3 6.5 %collective-permute-done.21.recv_ref = f32[3,32,128]{2,1,0:T(8,128)S(1)} collective-permute-done((f32[3,32,128]{2,1,0:T(8,128)S(1)}, f32[3,32,128]{2,1,0:T(8,128)S(1)}, u32[]{:S(2)}, u32[]{:S(2)}) %collective-permute-start.21) | collective-permute-done | bytes 49184 | tf_op jit(solution)/shard_map/ppermute | solution.py:506
  74.9 1.2 %collective-permute-done.22.other_ref = f32[3,32,128]{2,1,0:T(8,128)S(1)} collective-permute-done((f32[3,32,128]{2,1,0:T(8,128)S(1)}, f32[3,32,128]{2,1,0:T(8,128)S(1)}, u32[]{:S(2)}, u32[]{:S(2)}) %collective-permute-start.22) | collective-permute-done | bytes 49184 | tf_op jit(solution)/shard_map/ppermute | solution.py:506
  76.3 6.4 %collective-permute-done.23.moved_ref = f32[2,3,32,128]{3,2,1,0:T(8,128)S(1)} collective-permute-done((f32[2,3,32,128]{3,2,1,0:T(8,128)S(1)}, f32[2,3,32,128]{3,2,1,0:T(8,128)S(1)}, u32[]{:S(2)}, u32[]{:S(2)}) %collective-permute-start.23) | collective-permute-done | bytes 98336 | tf_op jit(solution)/shard_map/ppermute | solution.py:506
  82.7 1.3 %collective-permute-start.24 = (f32[1,2,3,32,128]{4,3,2,1,0:T(8,128)S(1)}, f32[1,2,3,32,128]{4,3,2,1,0:T(8,128)S(1)}, u32[]{:S(2)}, u32[]{:S(2)}) collective-permute-start(f32[1,2,3,32,128]{4,3,2,1,0:T(8,128)S(1)} %bitcast.38), channel_id=1, source_target_pairs={{0,1},{1,0},{2,6},{3,7},{4,5},{5,4},{6,2},{7,3},{8,9},{9,8},{10,14... | collective-permute-start | bytes 294920 | tf_op jit(solution)/shard_map/ppermute | solution.py:506
  84.0 2.7 %collective-permute-done.24.other_ref = f32[1,2,3,32,128]{4,3,2,1,0:T(8,128)S(1)} collective-permute-done((f32[1,2,3,32,128]{4,3,2,1,0:T(8,128)S(1)}, f32[1,2,3,32,128]{4,3,2,1,0:T(8,128)S(1)}, u32[]{:S(2)}, u32[]{:S(2)}) %collective-permute-start.24) | collective-permute-done | bytes 98336 | tf_op jit(solution)/shard_map/ppermute | solution.py:506
  86.8 4.5 %collective-permute-done.25.other_ref = f32[2,2,3,32,128]{4,3,2,1,0:T(8,128)S(1)} collective-permute-done((f32[2,2,3,32,128]{4,3,2,1,0:T(8,128)S(1)}, f32[2,2,3,32,128]{4,3,2,1,0:T(8,128)S(1)}, u32[]{:S(2)}, u32[]{:S(2)}) %collective-permute-start.25) | collective-permute-done | bytes 196640 | tf_op jit(solution)/shard_map/ppermute | solution.py:506
  91.4 1.6 %collective-permute-start.26 = (f32[4,2,3,32,128]{4,3,2,1,0:T(8,128)S(1)}, f32[4,2,3,32,128]{4,3,2,1,0:T(8,128)S(1)}, u32[]{:S(2)}, u32[]{:S(2)}) collective-permute-start(f32[4,2,3,32,128]{4,3,2,1,0:T(8,128)S(1)} %bitcast.29), channel_id=1, source_target_pairs={{0,8},{1,9},{2,3},{3,2},{4,12},{5,13},{6,7},{7,6},{8,0},{9,1},{10,... | collective-permute-start | bytes 1179656 | tf_op jit(solution)/shard_map/ppermute | solution.py:506
  93.7 4.4 %collective-permute-done.26.recv_ref = f32[4,2,3,32,128]{4,3,2,1,0:T(8,128)S(1)} collective-permute-done((f32[4,2,3,32,128]{4,3,2,1,0:T(8,128)S(1)}, f32[4,2,3,32,128]{4,3,2,1,0:T(8,128)S(1)}, u32[]{:S(2)}, u32[]{:S(2)}) %collective-permute-start.26) | collective-permute-done | bytes 393248 | tf_op jit(solution)/shard_map/ppermute | solution.py:506
  (67 shorter events, 12.5 us)
Async XLA Ops:
  0.6 8.5 %copy-start = (bf16[1,3,128,1,256]{4,2,3,1,0:T(8,128)(2,1)S(1)}, bf16[1,3,128,1,256]{4,2,3,1,0:T(8,128)(2,1)}, u32[]{:S(2)}) copy-start(bf16[1,3,128,1,256]{4,2,3,1,0:T(8,128)(2,1)} %param.6) | copy-start | bytes 589828
  0.6 8.5 %copy-start.1 = (bf16[1,3,128,1,256]{4,2,3,1,0:T(8,128)(2,1)S(1)}, bf16[1,3,128,1,256]{4,2,3,1,0:T(8,128)(2,1)}, u32[]{:S(2)}) copy-start(bf16[1,3,128,1,256]{4,2,3,1,0:T(8,128)(2,1)} %param.9) | copy-start | bytes 589828
  2.3 8.7 %collective-permute-start = (f32[2,128,256]{2,1,0:T(8,128)}, f32[2,128,256]{2,1,0:T(8,128)S(1)}, u32[]{:S(2)}, u32[]{:S(2)}) collective-permute-start(f32[2,128,256]{2,1,0:T(8,128)} %shard_map.93.refs_0_), channel_id=1, source_target_pairs={{0,2},{1,3},{2,18},{3,19},{4,6},{5,7},{6,22},{7,23},{8,10},{9,11},... | collective-permute-start | bytes 786440 | tf_op jit(solution)/shard_map/ppermute | solution.py:506
  9.0 3.5 %copy-start.5 = (bf16[1,3,128,1,256]{4,2,3,1,0:T(8,128)(2,1)S(1)}, bf16[1,3,128,1,256]{4,2,3,1,0:T(8,128)(2,1)}, u32[]{:S(2)}) copy-start(bf16[1,3,128,1,256]{4,2,3,1,0:T(8,128)(2,1)} %param.7) | copy-start | bytes 589828
  9.0 3.5 %copy-start.6 = (bf16[1,3,128,1,256]{4,2,3,1,0:T(8,128)(2,1)S(1)}, bf16[1,3,128,1,256]{4,2,3,1,0:T(8,128)(2,1)}, u32[]{:S(2)}) copy-start(bf16[1,3,128,1,256]{4,2,3,1,0:T(8,128)(2,1)} %param.8) | copy-start | bytes 589828
  9.0 6.7 %collective-permute-start.2 = (f32[768,128]{1,0:T(8,128)S(1)}, f32[768,128]{1,0:T(8,128)S(1)}, u32[]{:S(2)}, u32[]{:S(2)}) collective-permute-start(f32[768,128]{1,0:T(8,128)S(1)} %get-tuple-element.65), channel_id=1, source_target_pairs={{0,2},{1,3},{2,0},{3,1},{4,6},{5,7},{6,4},{7,5},{8,10},{9,11},{10,... | collective-permute-start | bytes 1179656 | tf_op jit(solution)/shard_map/ppermute | solution.py:506
  11.0 5.1 %copy-start.3 = (f32[2,128,256]{2,1,0:T(8,128)S(1)}, f32[2,128,256]{2,1,0:T(8,128)}, u32[]{:S(2)}) copy-start(f32[2,128,256]{2,1,0:T(8,128)} %shard_map.93.refs_0_) | copy-start | bytes 786436
  11.0 5.1 %collective-permute-start.1 = (f32[2,128,256]{2,1,0:T(8,128)S(1)}, f32[2,128,256]{2,1,0:T(8,128)S(1)}, u32[]{:S(2)}, u32[]{:S(2)}) collective-permute-start(f32[2,128,256]{2,1,0:T(8,128)S(1)} %collective-permute-done.refs_1_), channel_id=1, source_target_pairs={{0,2},{1,3},{4,6},{5,7},{8,10},{9,11},{12,14},{13,15},{18,16},{19,... | collective-permute-start | bytes 786440 | tf_op jit(solution)/shard_map/ppermute | solution.py:506
  12.9 16.6 %collective-permute-start.6 = (f32[4,128,256]{2,1,0:T(8,128)S(1)}, f32[4,128,256]{2,1,0:T(8,128)S(1)}, u32[]{:S(2)}, u32[]{:S(2)}) collective-permute-start(f32[4,128,256]{2,1,0:T(8,128)S(1)} %get-tuple-element.70), channel_id=1, source_target_pairs={{0,2},{1,3},{2,18},{3,19},{4,6},{5,7},{6,22},{7,23},{8,10},{9,11},... | collective-permute-start | bytes 1572872 | tf_op jit(solution)/shard_map/ppermute | solution.py:506
  16.8 11.6 %collective-permute-start.3 = (f32[776,128]{1,0:T(8,128)S(1)}, f32[776,128]{1,0:T(8,128)S(1)}, u32[]{:S(2)}, u32[]{:S(2)}) collective-permute-start(f32[776,128]{1,0:T(8,128)S(1)} %shard_map.97.mine_ref), channel_id=1, source_target_pairs={{0,4},{1,5},{2,10},{3,11},{4,0},{5,1},{6,14},{7,15},{8,12},{9,13},... | collective-permute-start | bytes 1191944 | tf_op jit(solution)/shard_map/ppermute | solution.py:506
  18.5 16.8 %collective-permute-start.9 = (f32[1560,128]{1,0:T(8,128)S(1)}, f32[1560,128]{1,0:T(8,128)S(1)}, u32[]{:S(2)}, u32[]{:S(2)}) collective-permute-start(f32[1560,128]{1,0:T(8,128)S(1)} %get-tuple-element.78), channel_id=1, source_target_pairs={{0,2},{1,3},{2,0},{3,1},{4,6},{5,7},{6,4},{7,5},{8,10},{9,11},{10,... | collective-permute-start | bytes 2396168 | tf_op jit(solution)/shard_map/ppermute | solution.py:506
  28.4 6.7 %collective-permute-start.4 = (f32[776,128]{1,0:T(8,128)S(1)}, f32[776,128]{1,0:T(8,128)S(1)}, u32[]{:S(2)}, u32[]{:S(2)}) collective-permute-start(f32[776,128]{1,0:T(8,128)S(1)} %shard_map.98.mine_ref), channel_id=1, source_target_pairs={{0,8},{1,9},{2,6},{3,7},{4,12},{5,13},{6,2},{7,3},{8,0},{9,1},{10,... | collective-permute-start | bytes 1191944 | tf_op jit(solution)/shard_map/ppermute | solution.py:506
  29.6 5.8 %collective-permute-start.7 = (f32[2,128,256]{2,1,0:T(8,128)S(1)}, f32[2,128,256]{2,1,0:T(8,128)S(1)}, u32[]{:S(2)}, u32[]{:S(2)}) collective-permute-start(f32[2,128,256]{2,1,0:T(8,128)S(1)} %get-tuple-element.72.refs_1_), channel_id=1, source_target_pairs={{0,2},{1,3},{4,6},{5,7},{8,10},{9,11},{12,14},{13,15},{18,16},{19,... | collective-permute-start | bytes 786440 | tf_op jit(solution)/shard_map/ppermute | solution.py:506
  30.9 4.5 %collective-permute-start.8 = (f32[2,128,256]{2,1,0:T(8,128)S(1)}, f32[2,128,256]{2,1,0:T(8,128)S(1)}, u32[]{:S(2)}, u32[]{:S(2)}) collective-permute-start(f32[2,128,256]{2,1,0:T(8,128)S(1)} %get-tuple-element.75.refs_4_), channel_id=1, source_target_pairs={{0,2},{1,3},{4,6},{5,7},{8,10},{9,11},{12,14},{13,15},{18,16},{19,... | collective-permute-start | bytes 786440 | tf_op jit(solution)/shard_map/ppermute | solution.py:506
  32.6 19.0 %collective-permute-start.14 = (f32[4,128,256]{2,1,0:T(8,128)S(1)}, f32[4,128,256]{2,1,0:T(8,128)S(1)}, u32[]{:S(2)}, u32[]{:S(2)}) collective-permute-start(f32[4,128,256]{2,1,0:T(8,128)S(1)} %get-tuple-element.94), channel_id=1, source_target_pairs={{0,2},{1,3},{2,18},{3,19},{4,6},{5,7},{6,22},{7,23},{8,10},{9,11},... | collective-permute-start | bytes 1572872 | tf_op jit(solution)/shard_map/ppermute | solution.py:506
  35.2 1.2 %collective-permute-start.5 = (f32[8,128]{1,0:T(8,128)S(1)}, f32[8,128]{1,0:T(8,128)S(1)}, u32[]{:S(2)}, u32[]{:S(2)}) collective-permute-start(f32[8,128]{1,0:T(8,128)S(1)} %get-tuple-element.67.refs_1_), channel_id=1, source_target_pairs={{0,2},{1,3},{2,0},{3,1},{4,6},{5,7},{6,4},{7,5},{8,10},{9,11},{10,... | collective-permute-start | bytes 12296 | tf_op jit(solution)/shard_map/ppermute | solution.py:506
  37.1 12.7 %collective-permute-start.10 = (f32[776,128]{1,0:T(8,128)S(1)}, f32[776,128]{1,0:T(8,128)S(1)}, u32[]{:S(2)}, u32[]{:S(2)}) collective-permute-start(f32[776,128]{1,0:T(8,128)S(1)} %get-tuple-element.84.mine_ref), channel_id=1, source_target_pairs={{0,4},{1,5},{2,10},{3,11},{4,0},{5,1},{6,14},{7,15},{8,12},{9,13},... | collective-permute-start | bytes 1191944 | tf_op jit(solution)/shard_map/ppermute | solution.py:506
  37.8 2.8 %collective-permute-start.11 = (f32[2,128,256]{2,1,0:T(8,128)S(1)}, f32[2,128,256]{2,1,0:T(8,128)S(1)}, u32[]{:S(2)}, u32[]{:S(2)}) collective-permute-start(f32[2,128,256]{2,1,0:T(8,128)S(1)} %get-tuple-element.88), channel_id=1, source_target_pairs={{0,2},{1,3},{2,0},{3,1},{4,6},{5,7},{6,4},{7,5},{8,10},{9,11},{10,... | collective-permute-start | bytes 786440 | tf_op jit(solution)/shard_map/ppermute | solution.py:506
  49.9 6.9 %collective-permute-start.12 = (f32[776,128]{1,0:T(8,128)S(1)}, f32[776,128]{1,0:T(8,128)S(1)}, u32[]{:S(2)}, u32[]{:S(2)}) collective-permute-start(f32[776,128]{1,0:T(8,128)S(1)} %shard_map.107.mine_ref), channel_id=1, source_target_pairs={{0,8},{1,9},{2,6},{3,7},{4,12},{5,13},{6,2},{7,3},{8,0},{9,1},{10,... | collective-permute-start | bytes 1191944 | tf_op jit(solution)/shard_map/ppermute | solution.py:506
  51.6 5.3 %collective-permute-start.16 = (f32[2,128,256]{2,1,0:T(8,128)S(1)}, f32[2,128,256]{2,1,0:T(8,128)S(1)}, u32[]{:S(2)}, u32[]{:S(2)}) collective-permute-start(f32[2,128,256]{2,1,0:T(8,128)S(1)} %get-tuple-element.99.refs_4_), channel_id=1, source_target_pairs={{0,2},{1,3},{4,6},{5,7},{8,10},{9,11},{12,14},{13,15},{18,16},{19,... | collective-permute-start | bytes 786440 | tf_op jit(solution)/shard_map/ppermute | solution.py:506
  52.9 4.0 %collective-permute-start.15 = (f32[2,128,256]{2,1,0:T(8,128)S(1)}, f32[2,128,256]{2,1,0:T(8,128)S(1)}, u32[]{:S(2)}, u32[]{:S(2)}) collective-permute-start(f32[2,128,256]{2,1,0:T(8,128)S(1)} %get-tuple-element.96.refs_1_), channel_id=1, source_target_pairs={{0,2},{1,3},{4,6},{5,7},{8,10},{9,11},{12,14},{13,15},{18,16},{19,... | collective-permute-start | bytes 786440 | tf_op jit(solution)/shard_map/ppermute | solution.py:506
  56.8 1.2 %collective-permute-start.13 = (f32[8,128]{1,0:T(8,128)S(1)}, f32[8,128]{1,0:T(8,128)S(1)}, u32[]{:S(2)}, u32[]{:S(2)}) collective-permute-start(f32[8,128]{1,0:T(8,128)S(1)} %get-tuple-element.91.refs_1_), channel_id=1, source_target_pairs={{0,2},{1,3},{2,0},{3,1},{4,6},{5,7},{6,4},{7,5},{8,10},{9,11},{10,... | collective-permute-start | bytes 12296 | tf_op jit(solution)/shard_map/ppermute | solution.py:506
  58.8 4.9 %collective-permute-start.19 = (f32[3,128,128]{2,1,0:T(8,128)S(1)}, f32[3,128,128]{2,1,0:T(8,128)S(1)}, u32[]{:S(2)}, u32[]{:S(2)}) collective-permute-start(f32[3,128,128]{2,1,0:T(8,128)S(1)} %get-tuple-element.112), channel_id=1, source_target_pairs={{0,4},{1,5},{2,3},{3,2},{4,0},{5,1},{6,7},{7,6},{8,12},{9,13},{10,... | collective-permute-start | bytes 589832 | tf_op jit(solution)/shard_map/ppermute | solution.py:506
  60.7 4.6 %collective-permute-start.17 = (f32[2,128,256]{2,1,0:T(8,128)S(1)}, f32[2,128,256]{2,1,0:T(8,128)S(1)}, u32[]{:S(2)}, u32[]{:S(2)}) collective-permute-start(f32[2,128,256]{2,1,0:T(8,128)S(1)} %get-tuple-element.108), channel_id=1, source_target_pairs={{0,2},{1,3},{2,0},{3,1},{4,6},{5,7},{6,4},{7,5},{8,10},{9,11},{10,... | collective-permute-start | bytes 786440 | tf_op jit(solution)/shard_map/ppermute | solution.py:506
  63.7 4.5 %collective-permute-start.20 = (f32[3,64,128]{2,1,0:T(8,128)S(1)}, f32[3,64,128]{2,1,0:T(8,128)S(1)}, u32[]{:S(2)}, u32[]{:S(2)}) collective-permute-start(f32[3,64,128]{2,1,0:T(8,128)S(1)} %get-tuple-element.114), channel_id=1, source_target_pairs={{0,8},{1,9},{2,6},{3,7},{4,12},{5,13},{6,2},{7,3},{8,0},{9,1},{10,... | collective-permute-start | bytes 294920 | tf_op jit(solution)/shard_map/ppermute | solution.py:506
  65.3 21.5 %collective-permute-start.18 = (f32[4,128,256]{2,1,0:T(8,128)S(1)}, f32[4,128,256]{2,1,0:T(8,128)S(1)}, u32[]{:S(2)}, u32[]{:S(2)}) collective-permute-start(f32[4,128,256]{2,1,0:T(8,128)S(1)} %shard_map.114.own_ref), channel_id=1, source_target_pairs={{2,16},{3,17},{6,20},{7,21},{10,24},{11,25},{14,28},{15,29},{16,2}... | collective-permute-start | bytes 1572872 | tf_op jit(solution)/shard_map/ppermute | solution.py:506
  68.3 6.6 %collective-permute-start.21 = (f32[3,32,128]{2,1,0:T(8,128)S(1)}, f32[3,32,128]{2,1,0:T(8,128)S(1)}, u32[]{:S(2)}, u32[]{:S(2)}) collective-permute-start(f32[3,32,128]{2,1,0:T(8,128)S(1)} %get-tuple-element.116), channel_id=1, source_target_pairs={{0,1},{1,0},{2,10},{3,11},{4,5},{5,4},{6,14},{7,15},{8,9},{9,8},{1... | collective-permute-start | bytes 147464 | tf_op jit(solution)/shard_map/ppermute | solution.py:506
  74.9 1.2 %collective-permute-start.22 = (f32[3,32,128]{2,1,0:T(8,128)S(1)}, f32[3,32,128]{2,1,0:T(8,128)S(1)}, u32[]{:S(2)}, u32[]{:S(2)}) collective-permute-start(f32[3,32,128]{2,1,0:T(8,128)S(1)} %shard_map.118.mine_ref), channel_id=1, source_target_pairs={{0,2},{1,3},{2,0},{3,1},{4,6},{5,7},{6,4},{7,5},{8,10},{9,11},{10,... | collective-permute-start | bytes 147464 | tf_op jit(solution)/shard_map/ppermute | solution.py:506
  76.1 6.6 %collective-permute-start.23 = (f32[2,3,32,128]{3,2,1,0:T(8,128)S(1)}, f32[2,3,32,128]{3,2,1,0:T(8,128)S(1)}, u32[]{:S(2)}, u32[]{:S(2)}) collective-permute-start(f32[2,3,32,128]{3,2,1,0:T(8,128)S(1)} %shard_map.119.own_ref), channel_id=1, source_target_pairs={{0,16},{1,17},{2,0},{3,1},{4,20},{5,21},{6,4},{7,5},{8,24},{9,25},... | collective-permute-start | bytes 294920 | tf_op jit(solution)/shard_map/ppermute | solution.py:506
  82.7 4.0 %collective-permute-start.24 = (f32[1,2,3,32,128]{4,3,2,1,0:T(8,128)S(1)}, f32[1,2,3,32,128]{4,3,2,1,0:T(8,128)S(1)}, u32[]{:S(2)}, u32[]{:S(2)}) collective-permute-start(f32[1,2,3,32,128]{4,3,2,1,0:T(8,128)S(1)} %bitcast.38), channel_id=1, source_target_pairs={{0,1},{1,0},{2,6},{3,7},{4,5},{5,4},{6,2},{7,3},{8,9},{9,8},{10,14... | collective-permute-start | bytes 294920 | tf_op jit(solution)/shard_map/ppermute | solution.py:506
  86.8 4.6 %collective-permute-start.25 = (f32[2,2,3,32,128]{4,3,2,1,0:T(8,128)S(1)}, f32[2,2,3,32,128]{4,3,2,1,0:T(8,128)S(1)}, u32[]{:S(2)}, u32[]{:S(2)}) collective-permute-start(f32[2,2,3,32,128]{4,3,2,1,0:T(8,128)S(1)} %bitcast.32), channel_id=1, source_target_pairs={{0,4},{1,5},{2,10},{3,11},{4,0},{5,1},{6,14},{7,15},{8,12},{9,13},... | collective-permute-start | bytes 589832 | tf_op jit(solution)/shard_map/ppermute | solution.py:506
  91.4 6.7 %collective-permute-start.26 = (f32[4,2,3,32,128]{4,3,2,1,0:T(8,128)S(1)}, f32[4,2,3,32,128]{4,3,2,1,0:T(8,128)S(1)}, u32[]{:S(2)}, u32[]{:S(2)}) collective-permute-start(f32[4,2,3,32,128]{4,3,2,1,0:T(8,128)S(1)} %bitcast.29), channel_id=1, source_target_pairs={{0,8},{1,9},{2,3},{3,2},{4,12},{5,13},{6,7},{7,6},{8,0},{9,1},{10,... | collective-permute-start | bytes 1179656 | tf_op jit(solution)/shard_map/ppermute | solution.py:506
  (2 other events, 2.1 us)
